TPU v7x, 32 devices: a whole 2x2x4 slice. The times are simulated.
32 devices in a mesh: grp: 2 (over x), orb: 16 (over z, y, core).
Axes of the slice: x: 2, y: 2, z: 4, core: 2. Of those that a mesh axis runs over, the one named last changes fastest.
Arguments:
- tensor: bfloat16 [128, 2048, 384], P('grp', 'orb'), parts along dimension 0, may hold values from -0.25 to 0.25
- tensor_mask: int32 [16, 6], P('orb', 'grp'), parts along dimension 1, may hold values from 0 to 1, as said below
- occupied: bfloat16 [4, 2048, 384], P('grp', 'orb'), parts along dimension 0, may hold values from -0.3125 to 0.3125
- occupied_mask: int32 [4, 16, 3], P('grp', 'orb'), parts along dimension 0, may hold values from 0 to 1, as said below
- virtual: bfloat16 [4, 2048, 384], P('grp', 'orb'), parts along dimension 0, may hold values from -0.3125 to 0.3125
- virtual_mask: int32 [4, 16, 3], P('grp', 'orb'), parts along dimension 0, may hold values from 0 to 1, as said below
Outputs:
- polarizability: float32 [128, 128], P('orb', 'grp'), parts along dimension 1
There are 2 independent parts, one for each index of `grp`. A program takes and returns all parts, laid end to end along the dimension named above; each array names one. Nothing has to cross between parts.
Inputs may be any that keep to these rules, and one draw needn't show every extreme that they name: `tensor_mask`: 0 or 1; the block on the diagonal (k = 1) is always kept, blocks outside the 16 x 16 grid are always 0; kept blocks are denser in a region of the system drawn from the seed, shared by all three patterns. `occupied_mask`: as tensor_mask. `virtual_mask`: as tensor_mask.
All inputs are finite; a program needn't handle non-finite values.
Results may differ from a plain program's by a relative error of at most 0.0041.
Values may be sent and summed in bfloat16 or wider, within the bound.
No kernel may reach another device: no remote copies, remote signals or barrier semaphores. Data moves between devices by JAX's collectives and lax.ppermute only.
A program may use at most 192 MiB of HBM per device.

v0:
```python
import functools

import jax
import jax.numpy as jnp
from jax import lax
from jax.experimental import pallas as pl
from jax.experimental.pallas import tpu as pltpu
from jax.sharding import PartitionSpec as P

CUTS = (64, 128)
AUX_STEP = 16
GROUP = 4
ROW_STEP = 16
VMEM_LIMIT = 56 * 1024 * 1024


def dot(lhs, rhs):
    return jnp.dot(lhs, rhs, preferred_element_type=jnp.float32)


def dot_nt(lhs, rhs):
    return lax.dot_general(
        lhs, rhs, (((1,), (1,)), ((), ())), preferred_element_type=jnp.float32
    )


def flat(block):
    return pltpu.einshape("plc->p(lc)", block)


def own_kernel(
    times, width, b_ref, mask_ref, occ_ref, vir_ref, low_ref, high_ref,
    flat_ref, own_ref, wide_ref, thin_ref,
    left_w, right_w, low_w, occ_w, masked, own_n, wide_n, thin_n,
):
    w = width

    @pl.when(pl.program_id(0) == 0)
    def build():
        for t in range(times):
            v_low, v_own, v_high = (vir_ref[t, :, k * w : (k + 1) * w] for k in range(3))
            below_own, below_up = low_ref[t, :, :w], low_ref[t, :, w : 2 * w]
            above_down, above_own = high_ref[t, :, :w], high_ref[t, :, w : 2 * w]

            def cols(slot):
                return slice((slot * times + t) * w, (slot * times + t + 1) * w)

            left_w[:, cols(0)] = v_low.T
            left_w[:, cols(1)] = below_up
            right_w[:w, cols(0)] = v_own.T
            right_w[w:, cols(0)] = v_high.T
            right_w[:w, cols(1)] = v_own
            right_w[w:, cols(1)] = above_down
            right_w[:w, cols(2)] = above_down.T
            right_w[w:, cols(2)] = above_own.T
            low_w[:w, cols(0)] = below_own.T
            low_w[w:, cols(0)] = below_up.T
            low_w[:w, cols(1)] = below_own
            low_w[w:, cols(1)] = v_low

            occ_w[t, 0] = occ_ref[t, :, w : 2 * w]
            occ_w[t, 1] = low_ref[t, :, 2 * w :]
            occ_w[t, 2] = occ_ref[t, :, :w].T
            occ_w[t, 3] = high_ref[t, :, 2 * w :]
            occ_w[t, 4] = occ_ref[t, :, 2 * w :].T

    masked[...] = b_ref[...] * mask_ref[...]
    flat_ref[...] = flat(masked[...])

    def group(g, carry):
        first = g * GROUP
        rows = masked[pl.ds(first, GROUP)].reshape(GROUP * w, 3 * w)
        from_left = dot(rows[:, :w], left_w[...])
        from_right = dot(rows[:, w:], right_w[...])
        from_low = dot(rows[:, : 2 * w], low_w[...])

        def part(product, slot, t):
            return product[:, (slot * times + t) * w : (slot * times + t + 1) * w]

        for t in range(times):
            left_c, left_b = part(from_left, 0, t), part(from_left, 1, t)
            u_low = part(from_low, 0, t).astype(jnp.bfloat16)
            u_mid = (part(from_right, 0, t) + left_c).astype(jnp.bfloat16)
            u_top = part(from_right, 2, t).astype(jnp.bfloat16)
            x_low = part(from_low, 1, t).astype(jnp.bfloat16)
            x_mid = (part(from_right, 1, t) + left_b).astype(jnp.bfloat16)
            left_c, left_b = left_c.astype(jnp.bfloat16), left_b.astype(jnp.bfloat16)
            o_both = occ_w[t, 0:2].reshape(2 * w, w)
            for j in range(GROUP):
                p = first + j
                r = slice(j * w, (j + 1) * w)
                both = dot(o_both, jnp.concatenate([u_low[r], u_mid[r]], axis=1))
                both = both.astype(jnp.bfloat16)
                own_n[t, p, :, : 2 * w] = both[:w]
                wide_n[t, p] = both[w:]
                own_n[t, p, :, 2 * w :] = dot(occ_w[t, 0], u_top[r]).astype(jnp.bfloat16)
                wide_n[times + t, p] = dot(
                    occ_w[t, 2], jnp.concatenate([x_low[r], x_mid[r]], axis=1)
                ).astype(jnp.bfloat16)
                thin_n[t, p] = dot(occ_w[t, 3], left_c[r]).astype(jnp.bfloat16)
                thin_n[times + t, p] = dot(occ_w[t, 4], left_b[r]).astype(jnp.bfloat16)
        return carry

    lax.fori_loop(0, AUX_STEP // GROUP, group, 0)
    for t in range(times):
        own_ref[t] = flat(own_n[t])
    for s in range(2 * times):
        wide_ref[s] = flat(wide_n[s])
        thin_ref[s] = flat(thin_n[s])


def own_terms(tensor, mask_row, occ, vir, low, high):
    aux, w, band = tensor.shape
    times = occ.shape[0]
    bf = jnp.bfloat16
    whole = pl.BlockSpec((times, w, band), lambda i: (0, 0, 0))
    flops = 2 * aux * w * w * w * (14 * times + 9 * times)
    return pl.pallas_call(
        functools.partial(own_kernel, times, w),
        grid=(aux // AUX_STEP,),
        in_specs=[
            pl.BlockSpec((AUX_STEP, w, band), lambda i: (i, 0, 0)),
            pl.BlockSpec((1, 1, band), lambda i: (0, 0, 0)),
            whole, whole, whole, whole,
        ],
        out_specs=[
            pl.BlockSpec((AUX_STEP, w * band), lambda i: (i, 0)),
            pl.BlockSpec((times, AUX_STEP, w * band), lambda i: (0, i, 0)),
            pl.BlockSpec((2 * times, AUX_STEP, 2 * w * w), lambda i: (0, i, 0)),
            pl.BlockSpec((2 * times, AUX_STEP, w * w), lambda i: (0, i, 0)),
        ],
        out_shape=[
            jax.ShapeDtypeStruct((aux, w * band), bf),
            jax.ShapeDtypeStruct((times, aux, w * band), bf),
            jax.ShapeDtypeStruct((2 * times, aux, 2 * w * w), bf),
            jax.ShapeDtypeStruct((2 * times, aux, w * w), bf),
        ],
        scratch_shapes=[
            pltpu.VMEM((w, 2 * times * w), bf),
            pltpu.VMEM((2 * w, 3 * times * w), bf),
            pltpu.VMEM((2 * w, 2 * times * w), bf),
            pltpu.VMEM((times, 5, w, w), bf),
            pltpu.VMEM((AUX_STEP, w, band), bf),
            pltpu.VMEM((times, AUX_STEP, w, band), bf),
            pltpu.VMEM((2 * times, AUX_STEP, w, 2 * w), bf),
            pltpu.VMEM((2 * times, AUX_STEP, w, w), bf),
        ],
        compiler_params=pltpu.CompilerParams(vmem_limit_bytes=VMEM_LIMIT),
        cost_estimate=pl.CostEstimate(flops=flops, bytes_accessed=50_000_000, transcendentals=0),
        name="own_terms",
    )(tensor, mask_row, occ, vir, low, high)


def own_sum_kernel(times, aux, own_ref, flat_ref, out_ref):
    @pl.when(pl.program_id(0) == 0)
    def start():
        out_ref[...] = jnp.zeros_like(out_ref)

    out_ref[: times * aux] += dot_nt(
        own_ref[...].reshape(times * aux, own_ref.shape[2]), flat_ref[...]
    )


def own_sum(own, flat_rows):
    times, aux, length = own.shape
    step = length // 8
    return pl.pallas_call(
        functools.partial(own_sum_kernel, times, aux),
        grid=(8,),
        in_specs=[
            pl.BlockSpec((times, aux, step), lambda i: (0, 0, i)),
            pl.BlockSpec((aux, step), lambda i: (0, i)),
        ],
        out_specs=pl.BlockSpec((2 * times * aux, aux), lambda i: (0, 0)),
        out_shape=jax.ShapeDtypeStruct((2 * times * aux, aux), jnp.float32),
        compiler_params=pltpu.CompilerParams(vmem_limit_bytes=VMEM_LIMIT),
        cost_estimate=pl.CostEstimate(
            flops=2 * times * aux * aux * length, bytes_accessed=20_000_000, transcendentals=0
        ),
        name="own_sum",
    )(own, flat_rows)


def near_sum_kernel(last, times, aux, acc_ref, wide_ref, thin_ref, x_ref, l_ref, out_ref, total):
    step = pl.program_id(0)

    @pl.when(step == 0)
    def start():
        total[...] = acc_ref[...]

    slots = 2 * times * aux
    total[...] += dot_nt(wide_ref[...].reshape(slots, wide_ref.shape[2]), flat(x_ref[...])) + dot_nt(
        thin_ref[...].reshape(slots, thin_ref.shape[2]), flat(l_ref[...])
    )

    @pl.when(step == pl.num_programs(0) - 1)
    def finish():
        if last:
            for t in range(times):
                swapped = total[(times + t) * aux : (times + t + 1) * aux].T
                out_ref[t * aux : (t + 1) * aux] = total[t * aux : (t + 1) * aux] + swapped
        else:
            out_ref[...] = total[...]


def near_sum(acc, wide, thin, x, l, first_row, last):
    slots, aux, _ = wide.shape
    times = slots // 2
    rows, w = x.shape[1], l.shape[2]
    base = first_row // ROW_STEP
    out_rows = times * aux if last else slots * aux
    return pl.pallas_call(
        functools.partial(near_sum_kernel, last, times, aux),
        grid=(rows // ROW_STEP,),
        in_specs=[
            pl.BlockSpec((slots * aux, aux), lambda i: (0, 0)),
            pl.BlockSpec((slots, aux, ROW_STEP * 2 * w), lambda i: (0, 0, base + i)),
            pl.BlockSpec((slots, aux, ROW_STEP * w), lambda i: (0, 0, base + i)),
            pl.BlockSpec((aux, ROW_STEP, 2 * w), lambda i: (0, i, 0)),
            pl.BlockSpec((aux, ROW_STEP, w), lambda i: (0, i, 0)),
        ],
        out_specs=pl.BlockSpec((out_rows, aux), lambda i: (0, 0)),
        out_shape=jax.ShapeDtypeStruct((out_rows, aux), jnp.float32),
        scratch_shapes=[pltpu.VMEM((slots * aux, aux), jnp.float32)],
        compiler_params=pltpu.CompilerParams(vmem_limit_bytes=VMEM_LIMIT),
        cost_estimate=pl.CostEstimate(
            flops=2 * slots * aux * aux * rows * 3 * w,
            bytes_accessed=2 * (slots + 1) * aux * rows * 3 * w,
            transcendentals=0,
        ),
        name="near_sum",
    )(acc, wide, thin, x, l)


def scattered_sum(value, axis):
    count = lax.axis_size(axis)
    me = lax.axis_index(axis)
    share = value.shape[0] // count
    if count & (count - 1):
        return lax.dynamic_slice_in_dim(lax.psum(value, axis), me * share, share, 0)
    bits = count.bit_length() - 1
    current = value.reshape((2,) * bits + (share, value.shape[1]))
    for bit in range(bits):
        dim = bits - 1 - bit
        mine = (me >> bit) & 1
        keep = lax.dynamic_index_in_dim(current, mine, dim, keepdims=False)
        send = lax.dynamic_index_in_dim(current, 1 - mine, dim, keepdims=False)
        pairs = [(i, i ^ (1 << bit)) for i in range(count)]
        current = keep + lax.ppermute(send, axis, pairs)
    return current


def body(tensor, tensor_mask, occupied, occupied_mask, virtual, virtual_mask):
    w = tensor.shape[1]
    bf = jnp.bfloat16
    count = lax.axis_size("orb")
    forward = [(i, i + 1) for i in range(count - 1)]
    backward = [(i + 1, i) for i in range(count - 1)]

    def spread(flags):
        return jnp.repeat(flags.astype(bf), w, axis=-1)

    mask_row = spread(tensor_mask)[:, None, :]
    occ = occupied * spread(occupied_mask)
    vir = virtual * spread(virtual_mask)
    low = lax.ppermute(jnp.concatenate([vir[:, :, w:], occ[:, :, 2 * w :]], 2), "orb", forward)
    high = lax.ppermute(jnp.concatenate([vir[:, :, : 2 * w], occ[:, :, :w]], 2), "orb", backward)

    arrived = []
    begin = 0
    for end in CUTS:
        x = tensor[:, begin:end, w:] * mask_row[:, :, w:]
        l = tensor[:, begin:end, :w] * mask_row[:, :, :w]
        arrived.append((begin, lax.ppermute(x, "orb", forward), lax.ppermute(l, "orb", backward)))
        begin = end

    flat_rows, own, wide, thin = own_terms(tensor, mask_row, occ, vir, low, high)
    total = own_sum(own, flat_rows)
    for index, (begin, x, l) in enumerate(arrived):
        total = near_sum(total, wide, thin, x, l, begin, index == len(arrived) - 1)
    return scattered_sum(total, "orb")


def solution(mesh):
    return jax.shard_map(
        body,
        mesh=mesh,
        in_specs=(
            P("grp", "orb", None),
            P("orb", "grp"),
            P("grp", "orb", None),
            P("grp", "orb", None),
            P("grp", "orb", None),
            P("grp", "orb", None),
        ),
        out_specs=P("orb", "grp"),
        check_vma=False,
    )
```

profile of v0, /device:TPU:0, one launch (start us, length us, event | category | flops | bytes accessed | tf_op | source)
XLA Modules:
  0.0 167.8 jit_solution(7762466693167099428)
XLA Ops:
  0.0 0.7 convert_bitcast_fusion
  0.7 0.1 broadcast_in_dim.15
  0.8 0.0 copy-start.9
  0.8 0.0 copy-start.5
  0.8 4.6 %slice_multiply_fusion = (bf16[64,64,256]{2,1,0:T(8,128)(2,1)}, bf16[64,64,256]{2,1,0:T(8,128)(2,1)}) fusion(bf16[64,128,384]{2,1,0:T(8,128)(2,1)} %b_ref.1, bf16[256]{0:T(256)(128)(2,1)S(1)} %slice_reduce_fusion), kind=kLoop, calls=%fused_computation | loop fusion | flops 2097152 | bytes 8389120 | tf_op jit(solution)/shard_map/mul | solution.py:272
  5.5 3.7 %collective-permute-start.2 = (bf16[64,64,256]{2,1,0:T(8,128)(2,1)}, bf16[64,64,256]{2,1,0:T(8,128)(2,1)}, u32[]{:S(2)}, u32[]{:S(2)}) collective-permute-start(bf16[64,64,256]{2,1,0:T(8,128)(2,1)} %get-tuple-element.16), channel_id=1, source_target_pairs={{0,1},{1,2},{2,3},{3,4},{4,5},{5,6},{6,7},{7,8},{8,9},{9,10},{10,1... | collective-permute-start | bytes 6291464 | tf_op jit(solution)/shard_map/ppermute | solution.py:274
  9.2 3.3 %collective-permute-start.4 = (bf16[64,64,256]{2,1,0:T(8,128)(2,1)}, bf16[64,64,256]{2,1,0:T(8,128)(2,1)S(1)}, u32[]{:S(2)}, u32[]{:S(2)}) collective-permute-start(bf16[64,64,256]{2,1,0:T(8,128)(2,1)} %get-tuple-element.15), channel_id=1, source_target_pairs={{0,1},{1,2},{2,3},{3,4},{4,5},{5,6},{6,7},{7,8},{8,9},{9,10},{10,1... | collective-permute-start | bytes 6291464 | tf_op jit(solution)/shard_map/ppermute | solution.py:274
  12.5 0.1 broadcast_bitcast_fusion
  12.6 0.1 broadcast_bitcast_fusion.1
  12.9 1.3 collective-permute-start.1
  14.2 0.7 pad_maximum_fusion
  14.9 3.7 %collective-permute-start = (bf16[2,128,384]{2,1,0:T(8,128)(2,1)}, bf16[2,128,384]{2,1,0:T(8,128)(2,1)}, u32[]{:S(2)}, u32[]{:S(2)}) collective-permute-start(bf16[2,128,384]{2,1,0:T(8,128)(2,1)} %pad_maximum_fusion), channel_id=1, source_target_pairs={{0,1},{1,2},{2,3},{3,4},{4,5},{5,6},{6,7},{7,8},{8,9},{9,10},{10,1... | collective-permute-start | bytes 589832 | tf_op jit(solution)/shard_map/ppermute | solution.py:266
  18.6 3.0 %slice_multiply_fusion.2 = (bf16[64,64,128]{2,1,0:T(8,128)(2,1)}, bf16[64,64,128]{2,1,0:T(8,128)(2,1)}) fusion(bf16[64,128,384]{2,1,0:T(8,128)(2,1)} %b_ref.1, bf16[128]{0:T(256)(128)(2,1)S(1)} %slice_bitcast_fusion), kind=kLoop, calls=%fused_computation.2 | loop fusion | flops 1048576 | bytes 4194560 | tf_op jit(solution)/shard_map/mul | solution.py:273
  21.6 1.3 collective-permute-start.3
  22.9 1.3 collective-permute-start.5
  24.2 39.5 %own_terms.1 = (bf16[64,49152]{1,0:T(8,128)(2,1)}, bf16[2,64,49152]{2,1,0:T(8,128)(2,1)}, bf16[4,64,32768]{2,1,0:T(8,128)(2,1)}, bf16[4,64,16384]{2,1,0:T(8,128)(2,1)}) custom-call(bf16[64,128,384]{2,1,0:T(8,128)(2,1)} %b_ref.1, bf16[1,1,384]{2,1,0:T(2,128)(2,1)} %copy-done.7, bf16[2,128,384]{2,1,0:T(8,128)(2,1)} %copy-done.4, ...), custom_call_target="tpu_custom_call" | custom-call | flops 12348030976 | bytes 50000000 | tf_op jit(solution)/shard_map/own_terms/pallas_call | solution.py:118
  63.7 10.6 %own_sum.1.acc_ref = f32[256,64]{1,0:T(8,128)} custom-call(bf16[2,64,49152]{2,1,0:T(8,128)(2,1)} %get-tuple-element.9.own_ref, bf16[64,49152]{1,0:T(8,128)(2,1)} %get-tuple-element.10.flat_ref), custom_call_target="tpu_custom_call" | custom-call | flops 805306368 | bytes 20000000 | tf_op jit(solution)/shard_map/own_sum/pallas_call | solution.py:167
  74.3 1.0 copy-done.2
  75.3 8.2 %near_sum.2.acc_ref = f32[256,64]{1,0:T(8,128)} custom-call(f32[256,64]{1,0:T(8,128)} %own_sum.1.acc_ref, bf16[4,64,32768]{2,1,0:T(8,128)(2,1)} %get-tuple-element.11.wide_ref, bf16[4,64,16384]{2,1,0:T(8,128)(2,1)} %get-tuple-element.12.thin_ref, bf16[64,64,256]{2,1,0:T(8,128)(2,1)} %collective-permute-done.2.x_ref, bf16[64,64,128]{2,1,0:T(8,128)(2,1)} %copy-done.2), custom_call_target="tpu_custom_call" | custom-call | flops 805306368 | bytes 15728640 | tf_op jit(solution)/shard_map/near_sum/pallas_call | solution.py:212
  83.6 1.0 copy-done.3
  84.6 1.3 copy-done
  85.9 8.3 %near_sum.3 = f32[128,64]{1,0:T(8,128)} custom-call(f32[256,64]{1,0:T(8,128)} %near_sum.2.acc_ref, bf16[4,64,32768]{2,1,0:T(8,128)(2,1)} %get-tuple-element.11.wide_ref, bf16[4,64,16384]{2,1,0:T(8,128)(2,1)} %get-tuple-element.12.thin_ref, bf16[64,64,256]{2,1,0:T(8,128)(2,1)} %copy-done, bf16[64,64,128]{2,1,0:T(8,128)(2,1)} %copy-done.3), custom_call_target="tpu_custom_call" | custom-call | flops 805306368 | bytes 15728640 | tf_op jit(solution)/shard_map/near_sum/pallas_call | solution.py:212
  94.2 0.8 constant_dynamic-slice_fusion.1
  95.0 58.7 %collective-permute-start.6 = (f32[2,2,2,8,64]{4,3,1,0,2:T(8,128)S(1)}, f32[2,2,2,8,64]{4,3,1,0,2:T(8,128)S(1)}, u32[]{:S(2)}, u32[]{:S(2)}) collective-permute-start(f32[2,2,2,8,64]{4,3,1,0,2:T(8,128)S(1)} %bitcast.39), channel_id=1, source_target_pairs={{0,1},{1,0},{2,3},{3,2},{4,5},{5,4},{6,7},{7,6},{8,9},{9,8},{10,11... | collective-permute-start | bytes 49160 | tf_op jit(solution)/shard_map/ppermute | solution.py:249
  153.7 0.9 collective-permute-done.6
  154.5 2.8 %collective-permute-start.7 = (f32[2,2,8,64]{3,2,1,0:T(8,128)S(1)}, f32[2,2,8,64]{3,2,1,0:T(8,128)S(1)}, u32[]{:S(2)}, u32[]{:S(2)}) collective-permute-start(f32[2,2,8,64]{3,2,1,0:T(8,128)S(1)} %dynamic-slice_bitcast_fusion), channel_id=1, source_target_pairs={{0,2},{1,3},{2,0},{3,1},{4,6},{5,7},{6,4},{7,5},{8,10},{9,11},{10,... | collective-permute-start | bytes 24584 | tf_op jit(solution)/shard_map/ppermute | solution.py:249
  157.3 1.7 %collective-permute-done.7 = f32[2,2,8,64]{3,2,1,0:T(8,128)S(1)} collective-permute-done((f32[2,2,8,64]{3,2,1,0:T(8,128)S(1)}, f32[2,2,8,64]{3,2,1,0:T(8,128)S(1)}, u32[]{:S(2)}, u32[]{:S(2)}) %collective-permute-start.7) | collective-permute-done | bytes 8224 | tf_op jit(solution)/shard_map/ppermute | solution.py:249
  159.0 1.6 collective-permute-start.8
  160.6 2.1 %collective-permute-done.8 = f32[2,8,64]{2,1,0:T(8,128)S(1)} collective-permute-done((f32[2,8,64]{2,1,0:T(8,128)S(1)}, f32[2,8,64]{2,1,0:T(8,128)S(1)}, u32[]{:S(2)}, u32[]{:S(2)}) %collective-permute-start.8) | collective-permute-done | bytes 4128 | tf_op jit(solution)/shard_map/ppermute | solution.py:249
  162.7 2.6 %collective-permute-start.9 = (f32[8,64]{1,0:T(8,128)S(1)}, f32[8,64]{1,0:T(8,128)S(1)}, u32[]{:S(2)}, u32[]{:S(2)}) collective-permute-start(f32[8,64]{1,0:T(8,128)S(1)} %dynamic-slice_bitcast_fusion.2), channel_id=1, source_target_pairs={{0,8},{1,9},{2,10},{3,11},{4,12},{5,13},{6,14},{7,15},{8,0},{9,1},... | collective-permute-start | bytes 6152 | tf_op jit(solution)/shard_map/ppermute | solution.py:249
  165.3 1.9 %collective-permute-done.9 = f32[8,64]{1,0:T(8,128)S(1)} collective-permute-done((f32[8,64]{1,0:T(8,128)S(1)}, f32[8,64]{1,0:T(8,128)S(1)}, u32[]{:S(2)}, u32[]{:S(2)}) %collective-permute-start.9) | collective-permute-done | bytes 2080 | tf_op jit(solution)/shard_map/ppermute | solution.py:249
  167.2 0.6 bitcast_add_fusion.3
  (41 shorter events, 0.3 us)
Async XLA Ops:
  0.8 17.8 %copy-start.7 = (bf16[1,1,384]{2,1,0:T(2,128)(2,1)}, bf16[1,1,384]{2,1,0:T(2,128)(2,1)S(1)}, u32[]{:S(2)}) copy-start(bf16[1,1,384]{2,1,0:T(2,128)(2,1)S(1)} %broadcast_in_dim.16.mask_ref) | copy-start | bytes 2308
  0.8 11.7 %copy-start.8 = (s32[2,1,3]{2,1,0:T(1,128)S(1)}, s32[2,1,3]{2,1,0:T(1,128)}, u32[]{:S(2)}) copy-start(s32[2,1,3]{2,1,0:T(1,128)} %param.11) | copy-start | bytes 76
  0.8 11.8 %copy-start.9 = (s32[2,1,3]{2,1,0:T(1,128)S(1)}, s32[2,1,3]{2,1,0:T(1,128)}, u32[]{:S(2)}) copy-start(s32[2,1,3]{2,1,0:T(1,128)} %param.9) | copy-start | bytes 76
  0.8 11.9 %copy-start.5 = (bf16[2,128,384]{2,1,0:T(8,128)(2,1)S(1)}, bf16[2,128,384]{2,1,0:T(8,128)(2,1)}, u32[]{:S(2)}) copy-start(bf16[2,128,384]{2,1,0:T(8,128)(2,1)} %param.10) | copy-start | bytes 589828
  0.8 11.9 %copy-start.6 = (bf16[2,128,384]{2,1,0:T(8,128)(2,1)S(1)}, bf16[2,128,384]{2,1,0:T(8,128)(2,1)}, u32[]{:S(2)}) copy-start(bf16[2,128,384]{2,1,0:T(8,128)(2,1)} %param.8) | copy-start | bytes 589828
  5.5 68.9 %collective-permute-start.2 = (bf16[64,64,256]{2,1,0:T(8,128)(2,1)}, bf16[64,64,256]{2,1,0:T(8,128)(2,1)}, u32[]{:S(2)}, u32[]{:S(2)}) collective-permute-start(bf16[64,64,256]{2,1,0:T(8,128)(2,1)} %get-tuple-element.16), channel_id=1, source_target_pairs={{0,1},{1,2},{2,3},{3,4},{4,5},{5,6},{6,7},{7,8},{8,9},{9,10},{10,1... | collective-permute-start | bytes 6291464 | tf_op jit(solution)/shard_map/ppermute | solution.py:274
  9.2 74.4 %collective-permute-start.4 = (bf16[64,64,256]{2,1,0:T(8,128)(2,1)}, bf16[64,64,256]{2,1,0:T(8,128)(2,1)S(1)}, u32[]{:S(2)}, u32[]{:S(2)}) collective-permute-start(bf16[64,64,256]{2,1,0:T(8,128)(2,1)} %get-tuple-element.15), channel_id=1, source_target_pairs={{0,1},{1,2},{2,3},{3,4},{4,5},{5,6},{6,7},{7,8},{8,9},{9,10},{10,1... | collective-permute-start | bytes 6291464 | tf_op jit(solution)/shard_map/ppermute | solution.py:274
  12.8 8.8 %copy-start.1 = (bf16[2,128,384]{2,1,0:T(8,128)(2,1)}, bf16[2,128,384]{2,1,0:T(8,128)(2,1)S(1)}, u32[]{:S(2)}) copy-start(bf16[2,128,384]{2,1,0:T(8,128)(2,1)S(1)} %get-tuple-element.23.vir_ref) | copy-start | bytes 589828
  12.8 8.8 %copy-start.4 = (bf16[2,128,384]{2,1,0:T(8,128)(2,1)}, bf16[2,128,384]{2,1,0:T(8,128)(2,1)S(1)}, u32[]{:S(2)}) copy-start(bf16[2,128,384]{2,1,0:T(8,128)(2,1)S(1)} %get-tuple-element.24.occ_ref) | copy-start | bytes 589828
  12.9 10.0 %collective-permute-start.1 = (bf16[2,128,384]{2,1,0:T(8,128)(2,1)S(1)}, bf16[2,128,384]{2,1,0:T(8,128)(2,1)}, u32[]{:S(2)}, u32[]{:S(2)}) collective-permute-start(bf16[2,128,384]{2,1,0:T(8,128)(2,1)S(1)} %pad_maximum_fusion.1), channel_id=1, source_target_pairs={{1,0},{2,1},{3,2},{4,3},{5,4},{6,5},{7,6},{8,7},{9,8},{10,9},{11,1... | collective-permute-start | bytes 589832 | tf_op jit(solution)/shard_map/ppermute | solution.py:267
  14.9 9.3 %collective-permute-start = (bf16[2,128,384]{2,1,0:T(8,128)(2,1)}, bf16[2,128,384]{2,1,0:T(8,128)(2,1)}, u32[]{:S(2)}, u32[]{:S(2)}) collective-permute-start(bf16[2,128,384]{2,1,0:T(8,128)(2,1)} %pad_maximum_fusion), channel_id=1, source_target_pairs={{0,1},{1,2},{2,3},{3,4},{4,5},{5,6},{6,7},{7,8},{8,9},{9,10},{10,1... | collective-permute-start | bytes 589832 | tf_op jit(solution)/shard_map/ppermute | solution.py:266
  21.6 52.7 %collective-permute-start.3 = (bf16[64,64,128]{2,1,0:T(8,128)(2,1)}, bf16[64,64,128]{2,1,0:T(8,128)(2,1)S(1)}, u32[]{:S(2)}, u32[]{:S(2)}) collective-permute-start(bf16[64,64,128]{2,1,0:T(8,128)(2,1)} %get-tuple-element.14), channel_id=1, source_target_pairs={{1,0},{2,1},{3,2},{4,3},{5,4},{6,5},{7,6},{8,7},{9,8},{10,9},{11,1... | collective-permute-start | bytes 3145736 | tf_op jit(solution)/shard_map/ppermute | solution.py:274
  22.9 60.7 %collective-permute-start.5 = (bf16[64,64,128]{2,1,0:T(8,128)(2,1)}, bf16[64,64,128]{2,1,0:T(8,128)(2,1)S(1)}, u32[]{:S(2)}, u32[]{:S(2)}) collective-permute-start(bf16[64,64,128]{2,1,0:T(8,128)(2,1)} %get-tuple-element.13), channel_id=1, source_target_pairs={{1,0},{2,1},{3,2},{4,3},{5,4},{6,5},{7,6},{8,7},{9,8},{10,9},{11,1... | collective-permute-start | bytes 3145736 | tf_op jit(solution)/shard_map/ppermute | solution.py:274
  74.3 1.0 copy-start.2
  83.6 1.0 copy-start.3
  84.6 1.3 copy-start
  95.0 59.6 %collective-permute-start.6 = (f32[2,2,2,8,64]{4,3,1,0,2:T(8,128)S(1)}, f32[2,2,2,8,64]{4,3,1,0,2:T(8,128)S(1)}, u32[]{:S(2)}, u32[]{:S(2)}) collective-permute-start(f32[2,2,2,8,64]{4,3,1,0,2:T(8,128)S(1)} %bitcast.39), channel_id=1, source_target_pairs={{0,1},{1,0},{2,3},{3,2},{4,5},{5,4},{6,7},{7,6},{8,9},{9,8},{10,11... | collective-permute-start | bytes 49160 | tf_op jit(solution)/shard_map/ppermute | solution.py:249
  154.5 4.5 %collective-permute-start.7 = (f32[2,2,8,64]{3,2,1,0:T(8,128)S(1)}, f32[2,2,8,64]{3,2,1,0:T(8,128)S(1)}, u32[]{:S(2)}, u32[]{:S(2)}) collective-permute-start(f32[2,2,8,64]{3,2,1,0:T(8,128)S(1)} %dynamic-slice_bitcast_fusion), channel_id=1, source_target_pairs={{0,2},{1,3},{2,0},{3,1},{4,6},{5,7},{6,4},{7,5},{8,10},{9,11},{10,... | collective-permute-start | bytes 24584 | tf_op jit(solution)/shard_map/ppermute | solution.py:249
  159.0 3.7 %collective-permute-start.8 = (f32[2,8,64]{2,1,0:T(8,128)S(1)}, f32[2,8,64]{2,1,0:T(8,128)S(1)}, u32[]{:S(2)}, u32[]{:S(2)}) collective-permute-start(f32[2,8,64]{2,1,0:T(8,128)S(1)} %dynamic-slice_bitcast_fusion.1), channel_id=1, source_target_pairs={{0,4},{1,5},{2,6},{3,7},{4,0},{5,1},{6,2},{7,3},{8,12},{9,13},{10,... | collective-permute-start | bytes 12296 | tf_op jit(solution)/shard_map/ppermute | solution.py:249
  162.7 4.5 %collective-permute-start.9 = (f32[8,64]{1,0:T(8,128)S(1)}, f32[8,64]{1,0:T(8,128)S(1)}, u32[]{:S(2)}, u32[]{:S(2)}) collective-permute-start(f32[8,64]{1,0:T(8,128)S(1)} %dynamic-slice_bitcast_fusion.2), channel_id=1, source_target_pairs={{0,8},{1,9},{2,10},{3,11},{4,12},{5,13},{6,14},{7,15},{8,0},{9,1},... | collective-permute-start | bytes 6152 | tf_op jit(solution)/shard_map/ppermute | solution.py:249
where the time goes:
time: 168 us
  starting transfers between devices  80.2 us (48%)
  Pallas kernels  66.6 us (40%)
  other arithmetic  9.69 us (6%)
  waiting for transfers between devices  6.57 us (4%)
  local copies, waits for them, and re-layouts  4.5 us (3%)
    ppermute x4, starting transfers between devices, scattered_sum(): current = keep + lax.ppermute(send, axis, pairs)  65.7 us
    pallas_call x1, Pallas kernels, own_terms(): pl.pallas_call(functools.partial(own_kernel, times, w), grid=(aux // AUX_...  39.5 us
    pallas_call x2, Pallas kernels, near_sum(): pl.pallas_call(functools.partial(near_sum_kernel, last, times, aux), grid...  16.5 us
    pallas_call x1, Pallas kernels, own_sum(): pl.pallas_call(functools.partial(own_sum_kernel, times, aux), grid=(8,),...  10.6 us
    ppermute x2, starting transfers between devices, body(): lax.ppermute(x, 'orb', forward)  7.02 us
    ppermute x4, waiting for transfers between devices, scattered_sum(): current = keep + lax.ppermute(send, axis, pairs)  6.55 us
    mul x1, other arithmetic, body(): x = tensor[:, begin:end, w:] * mask_row[:, :, w:]  4.65 us
    ppermute x1, starting transfers between devices, body(): lax.ppermute(jnp.concatenate([vir[:, :, w:], occ[:, :, 2 * w:]], 2), 'orb...  3.69 us
  transfers between devices with their start and end apart: 10, of which 4 were waited for; matrix products, arithmetic and copies ran while one was open for 2% of the time, Pallas kernels for 35%

commit v1 on v0

v1 whole, which is shorter than its diff:
```python
import functools

import jax
import jax.numpy as jnp
from jax import lax
from jax.experimental import pallas as pl
from jax.experimental.pallas import tpu as pltpu
from jax.sharding import PartitionSpec as P

CUTS = ((96, 32), (0, 80), (80, 16))
AUX_STEP = 16
GROUP = 4
ROW_STEP = 16
VMEM_LIMIT = 60 * 1024 * 1024
HBM = pl.BlockSpec(memory_space=pltpu.HBM)
SMEM = pl.BlockSpec(memory_space=pltpu.SMEM)


def dot(lhs, rhs):
    return jnp.dot(lhs, rhs, preferred_element_type=jnp.float32)


def dot_nt(lhs, rhs):
    return lax.dot_general(
        lhs, rhs, (((1,), (1,)), ((), ())), preferred_element_type=jnp.float32
    )


def flat(block):
    return pltpu.einshape("plc->p(lc)", block)


def kept(flag, block):
    return jnp.where(flag != 0, block, jnp.zeros_like(block))


def part(ref, t, k, width, flag):
    return kept(flag[t, 0, k], ref[t, :, k * width : (k + 1) * width])


def cut_blocks(width, b_ref, flag_ref, x_ref, l_ref):
    w = width
    l_ref[...] = kept(flag_ref[0, 0], b_ref[:, :, :w])
    x_ref[:, :, :w] = kept(flag_ref[0, 1], b_ref[:, :, w : 2 * w])
    x_ref[:, :, w:] = kept(flag_ref[0, 2], b_ref[:, :, 2 * w :])


def first_cut_kernel(
    times, width, rows, b_ref, flag_ref, occ_ref, vir_ref, occ_flag, vir_flag, x_ref, l_ref
):
    w, pieces = width, width // rows
    occ = functools.partial(part, occ_ref, width=w, flag=occ_flag)
    vir = functools.partial(part, vir_ref, width=w, flag=vir_flag)
    sent_up = [(vir(t, 1), vir(t, 2)) for t in range(times)]
    flat_occ = [occ(t, 2) for t in range(times)]
    sent_up += list(zip(flat_occ[::2], flat_occ[1::2], strict=True))
    for n, (one, two) in enumerate(sent_up):
        where = slice(n * pieces, (n + 1) * pieces)
        x_ref[where, :, :w] = one.reshape(pieces, rows, w)
        x_ref[where, :, w:] = two.reshape(pieces, rows, w)
    sent_down = [f(t, k) for t in range(times) for f, k in ((vir, 0), (vir, 1), (occ, 0))]
    for n, one in enumerate(sent_down):
        l_ref[n * pieces : (n + 1) * pieces] = one.reshape(pieces, rows, w)
    x_head, l_head = heads(times, w, rows)
    cut_blocks(w, b_ref, flag_ref, x_ref.at[x_head:], l_ref.at[l_head:])


def heads(times, width, rows):
    pieces = width // rows
    return 3 * times // 2 * pieces, 3 * times * pieces


def first_cut(tensor, flag, occ, vir, occ_flag, vir_flag):
    aux, w, band = tensor.shape
    times = occ.shape[0]
    begin, rows = CUTS[0]
    x_head, l_head = heads(times, w, rows)
    whole = pl.BlockSpec(occ.shape, lambda i: (0, 0, 0))
    x_shape, l_shape = (x_head + aux, rows, 2 * w), (l_head + aux, rows, w)
    return pl.pallas_call(
        functools.partial(first_cut_kernel, times, w, rows),
        grid=(1,),
        in_specs=[
            pl.BlockSpec((aux, rows, band), lambda i: (0, begin // rows, 0)),
            SMEM, whole, whole, SMEM, SMEM,
        ],
        out_specs=[pl.BlockSpec(n, lambda i: (0, 0, 0)) for n in (x_shape, l_shape)],
        out_shape=[jax.ShapeDtypeStruct(n, tensor.dtype) for n in (x_shape, l_shape)],
        compiler_params=pltpu.CompilerParams(vmem_limit_bytes=VMEM_LIMIT),
        name="first_cut",
    )(tensor, flag, occ, vir, occ_flag, vir_flag)


def later_cut(tensor, flag, begin, rows):
    aux, w, band = tensor.shape
    return pl.pallas_call(
        functools.partial(cut_blocks, w),
        grid=(aux // AUX_STEP,),
        in_specs=[pl.BlockSpec((AUX_STEP, rows, band), lambda i: (i, begin // rows, 0)), SMEM],
        out_specs=[
            pl.BlockSpec((AUX_STEP, rows, 2 * w), lambda i: (i, 0, 0)),
            pl.BlockSpec((AUX_STEP, rows, w), lambda i: (i, 0, 0)),
        ],
        out_shape=[
            jax.ShapeDtypeStruct((aux, rows, 2 * w), tensor.dtype),
            jax.ShapeDtypeStruct((aux, rows, w), tensor.dtype),
        ],
        compiler_params=pltpu.CompilerParams(vmem_limit_bytes=VMEM_LIMIT),
        name="later_cut",
    )(tensor, flag)


def own_kernel(
    times, width, b_ref, flag_ref, occ_ref, vir_ref, occ_flag, vir_flag, up_ref, down_ref,
    sum_ref, wide_ref, thin_ref,
    left_w, right_w, low_w, occ_w, masked, u, x, left, own_n, wide_n, thin_n, flat_own, flat_b,
):
    w = width
    step = pl.program_id(0)

    @pl.when(step == 0)
    def build():
        pieces = w // up_ref.shape[1]

        def got(ref, n, lanes=slice(None)):
            return ref[n * pieces : (n + 1) * pieces, :, lanes].reshape(w, w)

        one, two = slice(None, w), slice(w, None)
        for t in range(times):
            v_low, v_own, v_high = (part(vir_ref, t, k, w, vir_flag) for k in range(3))
            o_low, o_own, o_high = (part(occ_ref, t, k, w, occ_flag) for k in range(3))
            below_own, below_up = got(up_ref, t, one), got(up_ref, t, two)
            below_occ = got(up_ref, times + t // 2, (one, two)[t % 2])
            above_down, above_own, above_occ = (got(down_ref, 3 * t + n) for n in range(3))

            def cols(slot):
                return slice((slot * times + t) * w, (slot * times + t + 1) * w)

            left_w[:, cols(0)] = v_low.T
            left_w[:, cols(1)] = below_up
            right_w[:w, cols(0)] = v_own.T
            right_w[w:, cols(0)] = v_high.T
            right_w[:w, cols(1)] = v_own
            right_w[w:, cols(1)] = above_down
            right_w[:w, cols(2)] = above_down.T
            right_w[w:, cols(2)] = above_own.T
            low_w[:w, cols(0)] = below_own.T
            low_w[w:, cols(0)] = below_up.T
            low_w[:w, cols(1)] = below_own
            low_w[w:, cols(1)] = v_low

            occ_w[t, 0] = o_own
            occ_w[t, 1] = below_occ
            occ_w[t, 2] = o_low.T
            occ_w[t, 3] = above_occ
            occ_w[t, 4] = o_high.T

    bf = jnp.bfloat16
    for k in range(3):
        block = slice(k * w, (k + 1) * w)
        masked[:, :, block] = kept(flag_ref[0, k], b_ref[:, :, block])

    loops = AUX_STEP // GROUP
    rows = w // loops
    here = pl.ds(pl.multiple_of(step * AUX_STEP, AUX_STEP), AUX_STEP)

    def lay(g, source, target):
        first = pl.multiple_of(g * rows, rows)
        length = rows * source.shape[2]
        at = pl.ds(pl.multiple_of(g * length, length), length)
        target(at, flat(source[:, pl.ds(first, rows), :]))

    def to_own(t):
        def store(at, value):
            flat_own[t, here, at] = value

        return store

    def to_b(at, value):
        flat_b[here, at] = value

    def to_out(ref, slot):
        def store(at, value):
            ref[slot, :, at] = value

        return store

    def virtual_phase(g):
        group = pl.ds(g * GROUP, GROUP)
        lhs = masked[group].reshape(GROUP * w, 3 * w)
        from_left = dot(lhs[:, :w], left_w[...])
        from_right = dot(lhs[:, w:], right_w[...])
        from_low = dot(lhs[:, : 2 * w], low_w[...])

        def piece(product, slot, t):
            return product[:, (slot * times + t) * w : (slot * times + t + 1) * w]

        def put(ref, t, lanes, value):
            ref[t, group, :, lanes] = value.astype(bf).reshape(GROUP, w, w)

        one, two, three = slice(None, w), slice(w, 2 * w), slice(2 * w, None)
        for t in range(times):
            left_c, left_b = piece(from_left, 0, t), piece(from_left, 1, t)
            put(u, t, one, piece(from_low, 0, t))
            put(u, t, two, piece(from_right, 0, t) + left_c)
            put(u, t, three, piece(from_right, 2, t))
            put(x, t, one, piece(from_low, 1, t))
            put(x, t, two, piece(from_right, 1, t) + left_b)
            put(left, t, one, left_c)
            put(left, t, two, left_b)

    def pairs(g):
        return [(g * GROUP + j, g * GROUP + j + 1) for j in range(0, GROUP, 2)]

    def in_pair(occ, source, lanes, target, lanes_to, p, q):
        both = dot(occ, jnp.concatenate([source[p, :, lanes], source[q, :, lanes]], axis=1))
        both = both.astype(bf)
        target[p, :, lanes_to] = both[:, :w]
        target[q, :, lanes_to] = both[:, w:]

    def own_phase(t, g):
        occ = occ_w[t, 0:2].reshape(2 * w, w)
        for j in range(GROUP):
            p = g * GROUP + j
            both = dot(occ, u[t, p, :, : 2 * w]).astype(bf)
            own_n[t, p, :, : 2 * w] = both[:w]
            wide_n[t, p] = both[w:]
        last = slice(2 * w, 3 * w)
        for p, q in pairs(g):
            in_pair(occ_w[t, 0], u.at[t], last, own_n.at[t], last, p, q)

    def other_phase(t, g):
        for j in range(GROUP):
            p = g * GROUP + j
            wide_n[times + t, p] = dot(occ_w[t, 2], x[t, p]).astype(bf)
        for p, q in pairs(g):
            every = slice(None)
            in_pair(occ_w[t, 3], left.at[t], slice(None, w), thin_n.at[t], every, p, q)
            in_pair(occ_w[t, 4], left.at[t], slice(w, None), thin_n.at[times + t], every, p, q)

    def lay_b(g):
        lay(g, masked, to_b)

    def lay_own(t, g):
        lay(g, own_n.at[t], to_own(t))
        lay(g, wide_n.at[t], to_out(wide_ref, t))

    def lay_other(t, g):
        lay(g, wide_n.at[times + t], to_out(wide_ref, times + t))
        lay(g, thin_n.at[t], to_out(thin_ref, t))
        lay(g, thin_n.at[times + t], to_out(thin_ref, times + t))

    work, laying = [virtual_phase], [lay_b]
    for t in range(times):
        work += [functools.partial(own_phase, t), functools.partial(other_phase, t)]
        laying += [functools.partial(lay_own, t), functools.partial(lay_other, t)]
    for n, phase in enumerate(work):

        def both(g, carry, phase=phase, before=laying[n - 1] if n else None):
            phase(g)
            if before is not None:
                before(g)
            return carry

        lax.fori_loop(0, loops, both, 0)
    for g in range(loops):
        laying[-1](g)

    @pl.when(step == pl.num_programs(0) - 1)
    def add_up():
        count = times * flat_own.shape[1]
        length = flat_own.shape[2]
        share = length // 8
        total = None
        for n in range(8):
            at = slice(n * share, (n + 1) * share)
            term = dot_nt(flat_own[:, :, at].reshape(count, share), flat_b[:, at])
            total = term if total is None else total + term
        sum_ref[...] = total


def own_terms(tensor, flag, occ, vir, occ_flag, vir_flag, up, down):
    aux, w, band = tensor.shape
    times = occ.shape[0]
    bf = jnp.bfloat16
    x_head, l_head = heads(times, w, CUTS[0][1])

    def whole(shape):
        return pl.BlockSpec(shape, lambda i: (0, 0, 0))

    flops = 2 * aux * w * w * w * (14 * times + 9 * times)
    return pl.pallas_call(
        functools.partial(own_kernel, times, w),
        grid=(aux // AUX_STEP,),
        in_specs=[
            pl.BlockSpec((AUX_STEP, w, band), lambda i: (i, 0, 0)),
            SMEM, whole(occ.shape), whole(vir.shape), SMEM, SMEM,
            whole((x_head, *up.shape[1:])), whole((l_head, *down.shape[1:])),
        ],
        out_specs=[
            pl.BlockSpec((times * aux, aux), lambda i: (0, 0)),
            pl.BlockSpec((2 * times, AUX_STEP, 2 * w * w), lambda i: (0, i, 0)),
            pl.BlockSpec((2 * times, AUX_STEP, w * w), lambda i: (0, i, 0)),
        ],
        out_shape=[
            jax.ShapeDtypeStruct((times * aux, aux), jnp.float32),
            jax.ShapeDtypeStruct((2 * times, aux, 2 * w * w), bf),
            jax.ShapeDtypeStruct((2 * times, aux, w * w), bf),
        ],
        scratch_shapes=[
            pltpu.VMEM((w, 2 * times * w), bf),
            pltpu.VMEM((2 * w, 3 * times * w), bf),
            pltpu.VMEM((2 * w, 2 * times * w), bf),
            pltpu.VMEM((times, 5, w, w), bf),
            pltpu.VMEM((AUX_STEP, w, band), bf),
            pltpu.VMEM((times, AUX_STEP, w, band), bf),
            pltpu.VMEM((times, AUX_STEP, w, 2 * w), bf),
            pltpu.VMEM((times, AUX_STEP, w, 2 * w), bf),
            pltpu.VMEM((times, AUX_STEP, w, band), bf),
            pltpu.VMEM((2 * times, AUX_STEP, w, 2 * w), bf),
            pltpu.VMEM((2 * times, AUX_STEP, w, w), bf),
            pltpu.VMEM((times, aux, w * band), bf),
            pltpu.VMEM((aux, w * band), bf),
        ],
        compiler_params=pltpu.CompilerParams(vmem_limit_bytes=VMEM_LIMIT),
        cost_estimate=pl.CostEstimate(flops=flops, bytes_accessed=50_000_000, transcendentals=0),
        name="own_terms",
    )(tensor, flag, occ, vir, occ_flag, vir_flag, up, down)


def near_kernel(begin, steps, skips, earlier, wide_hbm, thin_hbm, x_hbm, l_hbm, *rest):
    before, rest = rest[:earlier], rest[earlier:]
    out_ref, wide, thin, x, l, held, sems, held_sems = rest
    slots, aux, w = wide.shape[1], wide.shape[2], l.shape[3]
    times = slots // 2

    def copies(s):
        rows = pl.ds(s * ROW_STEP, ROW_STEP)
        far = begin + s * ROW_STEP
        return [
            pltpu.make_async_copy(
                wide_hbm.at[:, :, pl.ds(far * 2 * w, ROW_STEP * 2 * w)], wide.at[s], sems.at[s, 0]
            ),
            pltpu.make_async_copy(
                thin_hbm.at[:, :, pl.ds(far * w, ROW_STEP * w)], thin.at[s], sems.at[s, 1]
            ),
            pltpu.make_async_copy(x_hbm.at[pl.ds(skips[0], aux), rows], x.at[s], sems.at[s, 2]),
            pltpu.make_async_copy(l_hbm.at[pl.ds(skips[1], aux), rows], l.at[s], sems.at[s, 3]),
        ]

    fetch = []
    for n, ref in enumerate(before):
        size = ref.shape[0]
        fetch.append(
            pltpu.make_async_copy(ref, held.at[n, pl.ds(0, size)], held_sems.at[n])
        )
    for s in range(steps):
        for copy in copies(s):
            copy.start()
    for copy in fetch:
        copy.start()
    total = None
    for s in range(steps):
        for copy in copies(s):
            copy.wait()
        wide_s = wide[s].reshape(slots * aux, ROW_STEP * 2 * w)
        thin_s = thin[s].reshape(slots * aux, ROW_STEP * w)
        term = dot_nt(wide_s, flat(x[s])) + dot_nt(thin_s, flat(l[s]))
        total = term if total is None else total + term
    if not earlier:
        out_ref[...] = total
        return
    for copy in fetch:
        copy.wait()
    half = times * aux
    for n in range(1, earlier):
        total = total + held[n]
    for t in range(times):
        rows = slice(t * aux, (t + 1) * aux)
        out_ref[rows] = held[0, rows] + total[rows] + total[half + t * aux : half + (t + 1) * aux].T


def near_sum(wide, thin, x, l, begin, rows, before=()):
    slots, aux, _ = wide.shape
    w = l.shape[2]
    steps = rows // ROW_STEP
    skips = (x.shape[0] - aux, l.shape[0] - aux)
    shape = (slots // 2 * aux if before else slots * aux, aux)
    bf = jnp.bfloat16
    return pl.pallas_call(
        functools.partial(near_kernel, begin, steps, skips, len(before)),
        in_specs=[HBM] * (4 + len(before)),
        out_specs=pl.BlockSpec(memory_space=pltpu.VMEM),
        out_shape=jax.ShapeDtypeStruct(shape, jnp.float32),
        scratch_shapes=[
            pltpu.VMEM((steps, slots, aux, ROW_STEP * 2 * w), bf),
            pltpu.VMEM((steps, slots, aux, ROW_STEP * w), bf),
            pltpu.VMEM((steps, aux, ROW_STEP, 2 * w), bf),
            pltpu.VMEM((steps, aux, ROW_STEP, w), bf),
            pltpu.VMEM((max(len(before), 1), slots * aux, aux), jnp.float32),
            pltpu.SemaphoreType.DMA((steps, 4)),
            pltpu.SemaphoreType.DMA((max(len(before), 1),)),
        ],
        compiler_params=pltpu.CompilerParams(vmem_limit_bytes=VMEM_LIMIT),
        cost_estimate=pl.CostEstimate(
            flops=2 * slots * aux * aux * rows * 3 * w,
            bytes_accessed=2 * (slots + 1) * aux * rows * 3 * w,
            transcendentals=0,
        ),
        name="near_sum",
    )(wide, thin, x, l, *before)


def scattered_sum(value, axis):
    count = lax.axis_size(axis)
    me = lax.axis_index(axis)
    share = value.shape[0] // count
    if count & (count - 1):
        return lax.dynamic_slice_in_dim(lax.psum(value, axis), me * share, share, 0)
    bits = count.bit_length() - 1
    current = value.reshape((2,) * bits + (share, value.shape[1]))
    left = list(range(bits))
    while left:
        chosen = left[-2:]

        def pick(flips):
            block = current
            for bit in chosen:
                dim = len(left) - 1 - left.index(bit)
                at = ((me >> bit) & 1) ^ ((flips >> bit) & 1)
                block = lax.dynamic_slice_in_dim(block, at, 1, dim)
            return block.reshape((2,) * (len(left) - len(chosen)) + (share, value.shape[1]))

        total = pick(0)
        for code in range(1, 1 << len(chosen)):
            flips = sum(((code >> j) & 1) << bit for j, bit in enumerate(chosen))
            pairs = [(i, i ^ flips) for i in range(count)]
            total = total + lax.ppermute(pick(flips), axis, pairs)
        current = total
        left = left[: len(left) - len(chosen)]
    return current


def body(tensor, tensor_mask, occupied, occupied_mask, virtual, virtual_mask):
    count = lax.axis_size("orb")
    forward = [(i, i + 1) for i in range(count - 1)]
    backward = [(i + 1, i) for i in range(count - 1)]

    arrived = []
    source = tensor
    for begin, rows in CUTS:
        if not arrived:
            x, l = first_cut(
                tensor, tensor_mask, occupied, virtual, occupied_mask, virtual_mask
            )
        else:
            x, l = later_cut(source, tensor_mask, begin, rows)
        source, x, l = lax.optimization_barrier((source, x, l))
        arrived.append((lax.ppermute(x, "orb", forward), lax.ppermute(l, "orb", backward)))

    total, wide, thin = own_terms(
        tensor, tensor_mask, occupied, virtual, occupied_mask, virtual_mask, *arrived[0]
    )
    before = [total]
    for (begin, rows), (x, l) in zip(CUTS, arrived, strict=True):
        last = len(before) == len(CUTS)
        before.append(near_sum(wide, thin, x, l, begin, rows, before if last else ()))
    return scattered_sum(before[-1], "orb")


def solution(mesh):
    return jax.shard_map(
        body,
        mesh=mesh,
        in_specs=(
            P("grp", "orb", None),
            P("orb", "grp"),
            P("grp", "orb", None),
            P("grp", "orb", None),
            P("grp", "orb", None),
            P("grp", "orb", None),
        ),
        out_specs=P("orb", "grp"),
        check_vma=False,
    )
```

time: 168 us -> 166 us (0.988)
  Pallas kernels: 66.6 us -> 78.7 us
  other arithmetic: 9.69 us -> 1.32 us
  starting transfers between devices: 80.2 us -> 73.6 us
  waiting for transfers between devices: 6.57 us -> 8.39 us
    ppermute x6, starting transfers between devices: 70.6 us -> 57.3 us  [scattered_sum(): total = total + lax.ppermute(pick(flips), axis, pairs)]
    mul x3 -> x0, other arithmetic: 7.69 us -> none  [the longest x1 4.65 us: body(): x = tensor[:, begin:end, w:] * mask_row[:, :, w:]]
    pallas_call x1, Pallas kernels: 39.5 us -> 46.4 us  [own_terms(): pl.pallas_call(functools.partial(own_kernel, times, w), grid=(aux // AUX_...]
    ppermute x2 -> x3, starting transfers between devices: 7.02 us -> 12.4 us  [body(): lax.ppermute(x, 'orb', forward)]
    pallas_call x3 -> x6, Pallas kernels: 27.1 us -> 32.2 us  [the longest x3 20.8 us: near_sum(): pl.pallas_call(functools.partial(near_kernel, begin, steps, skips, len(be...]
    ppermute x6, waiting for transfers between devices: 6.56 us -> 8.37 us  [scattered_sum(): total = total + lax.ppermute(pick(flips), axis, pairs)]
    ppermute x2 -> x3, starting transfers between devices: 2.57 us -> 3.85 us  [body(): lax.ppermute(l, 'orb', backward)]
    unnamed x26 -> x6, local copies, waits for them, and re-layouts: 3.53 us -> 2.26 us
  transfers between devices with their start and end apart: 10 -> 12, of which waited for: 4 -> 4; matrix products, arithmetic and copies ran while one was open for 2% -> 0% of each run, Pallas kernels for 35% -> 40%
where the time goes in v1:
time: 166 us; the launch traced here: 165 us
  Pallas kernels  78.7 us (47%)
  starting transfers between devices  73.6 us (44%)
  waiting for transfers between devices  8.39 us (5%)
  local copies, waits for them, and re-layouts  3.03 us (2%)
    ppermute x6, starting transfers between devices, scattered_sum(): total = total + lax.ppermute(pick(flips), axis, pairs)  57.3 us
    pallas_call x1, Pallas kernels, own_terms(): pl.pallas_call(functools.partial(own_kernel, times, w), grid=(aux // AUX_...  46.4 us
    pallas_call x3, Pallas kernels, near_sum(): pl.pallas_call(functools.partial(near_kernel, begin, steps, skips, len(be...  20.8 us
    ppermute x3, starting transfers between devices, body(): lax.ppermute(x, 'orb', forward)  12.4 us
    ppermute x6, waiting for transfers between devices, scattered_sum(): total = total + lax.ppermute(pick(flips), axis, pairs)  8.37 us
    pallas_call x2, Pallas kernels, later_cut(): pl.pallas_call(functools.partial(cut_blocks, w), grid=(aux // AUX_STEP,),...  8.27 us
    ppermute x3, starting transfers between devices, body(): lax.ppermute(l, 'orb', backward)  3.85 us
  transfers between devices with their start and end apart: 12, of which 4 were waited for; matrix products, arithmetic and copies ran while one was open for 0% of the time, Pallas kernels for 40%

profile of v1, /device:TPU:0, one launch (start us, length us, event | category | flops | bytes accessed | tf_op | source)
XLA Modules:
  0.0 165.1 jit_solution(15943638337923644251)
XLA Ops:
  0.0 3.2 %first_cut.1 = (bf16[76,32,256]{2,1,0:T(8,128)(2,1)}, bf16[88,32,128]{2,1,0:T(8,128)(2,1)}) custom-call(bf16[64,128,384]{2,1,0:T(8,128)(2,1)} %b_ref.5, s32[1,3]{1,0:T(1,128)} %flag_ref.7, bf16[2,128,384]{2,1,0:T(8,128)(2,1)} %occ_ref.3, bf16[2,128,384]{2,1,0:T(8,128)(2,1)} %vir_ref.3, s32[2,1,3]{2,1,0:T(1,128)} %occ_flag.3, s32[2,1,3]{2,1,0:T(1,128)} %vir_flag.3), custom_call_target="tpu_custom_call" | custom-call | tf_op jit(solution)/shard_map/first_cut/pallas_call | solution.py:80
  3.2 4.9 %later_cut.2 = (bf16[64,80,256]{2,1,0:T(8,128)(2,1)}, bf16[64,80,128]{2,1,0:T(8,128)(2,1)}) custom-call(bf16[64,128,384]{2,1,0:T(8,128)(2,1)} %b_ref.5, s32[1,3]{1,0:T(1,128)} %flag_ref.7), custom_call_target="tpu_custom_call" | custom-call | tf_op jit(solution)/shard_map/later_cut/pallas_call | solution.py:96
  8.1 2.5 %collective-permute-start.4 = (bf16[64,80,256]{2,1,0:T(8,128)(2,1)}, bf16[64,80,256]{2,1,0:T(8,128)(2,1)S(1)}, u32[]{:S(2)}, u32[]{:S(2)}) collective-permute-start(bf16[64,80,256]{2,1,0:T(8,128)(2,1)} %get-tuple-element.37), channel_id=1, source_target_pairs={{0,1},{1,2},{2,3},{3,4},{4,5},{5,6},{6,7},{7,8},{8,9},{9,10},{10,1... | collective-permute-start | bytes 7864328 | tf_op jit(solution)/shard_map/ppermute | solution.py:459
  10.6 5.4 %collective-permute-start = (bf16[76,32,256]{2,1,0:T(8,128)(2,1)}, bf16[76,32,256]{2,1,0:T(8,128)(2,1)}, u32[]{:S(2)}, u32[]{:S(2)}) collective-permute-start(bf16[76,32,256]{2,1,0:T(8,128)(2,1)} %get-tuple-element.24), channel_id=1, source_target_pairs={{0,1},{1,2},{2,3},{3,4},{4,5},{5,6},{6,7},{7,8},{8,9},{9,10},{10,1... | collective-permute-start | bytes 3735560 | tf_op jit(solution)/shard_map/ppermute | solution.py:459
  16.0 1.3 collective-permute-start.1
  17.3 1.3 collective-permute-start.5
  18.6 3.4 %later_cut.3 = (bf16[64,16,256]{2,1,0:T(8,128)(2,1)}, bf16[64,16,128]{2,1,0:T(8,128)(2,1)}) custom-call(bf16[64,128,384]{2,1,0:T(8,128)(2,1)} %b_ref.5, s32[1,3]{1,0:T(1,128)} %flag_ref.7), custom_call_target="tpu_custom_call" | custom-call | tf_op jit(solution)/shard_map/later_cut/pallas_call | solution.py:96
  22.0 4.5 %collective-permute-start.2 = (bf16[64,16,256]{2,1,0:T(8,128)(2,1)}, bf16[64,16,256]{2,1,0:T(8,128)(2,1)}, u32[]{:S(2)}, u32[]{:S(2)}) collective-permute-start(bf16[64,16,256]{2,1,0:T(8,128)(2,1)} %get-tuple-element.34), channel_id=1, source_target_pairs={{0,1},{1,2},{2,3},{3,4},{4,5},{5,6},{6,7},{7,8},{8,9},{9,10},{10,1... | collective-permute-start | bytes 1572872 | tf_op jit(solution)/shard_map/ppermute | solution.py:459
  26.5 1.3 collective-permute-start.3
  27.8 0.0 collective-permute-done.up_ref.x_hbm
  27.8 46.4 %own_terms.1 = (f32[128,64]{1,0:T(8,128)}, bf16[4,64,32768]{2,1,0:T(8,128)(2,1)}, bf16[4,64,16384]{2,1,0:T(8,128)(2,1)}) custom-call(bf16[64,128,384]{2,1,0:T(8,128)(2,1)} %b_ref.5, s32[1,3]{1,0:T(1,128)} %flag_ref.7, bf16[2,128,384]{2,1,0:T(8,128)(2,1)} %occ_ref.3, bf16[2,128,384]{2,1,0:T(8,128)(2,1)} %vir_ref.3, s32[2,1,3]{2,1,0:T(1,128)} %occ_flag.3, ...), custom_call_target="tpu_custom_call" | custom-call | flops 12348030976 | bytes 50000000 | tf_op jit(solution)/shard_map/own_terms/pallas_call | solution.py:292
  74.2 6.3 %near_sum.3.rest_1_ = f32[256,64]{1,0:T(8,128)} custom-call(bf16[4,64,32768]{2,1,0:T(8,128)(2,1)} %get-tuple-element.26.wide_hbm, bf16[4,64,16384]{2,1,0:T(8,128)(2,1)} %get-tuple-element.27.thin_hbm, bf16[76,32,256]{2,1,0:T(8,128)(2,1)} %collective-permute-done.up_ref.x_hbm, bf16[88,32,128]{2,1,0:T(8,128)(2,1)} %copy-done.1), custom_call_target="tpu_custom_call" | custom-call | flops 402653184 | bytes 7864320 | tf_op jit(solution)/shard_map/near_sum/pallas_call | solution.py:390
  80.6 0.0 collective-permute-done.4.x_hbm
  80.6 1.6 copy-done
  82.2 10.6 %near_sum.4.rest_2_ = f32[256,64]{1,0:T(8,128)} custom-call(bf16[4,64,32768]{2,1,0:T(8,128)(2,1)} %get-tuple-element.26.wide_hbm, bf16[4,64,16384]{2,1,0:T(8,128)(2,1)} %get-tuple-element.27.thin_hbm, bf16[64,80,256]{2,1,0:T(8,128)(2,1)} %copy-done, bf16[64,80,128]{2,1,0:T(8,128)(2,1)} %collective-permute-done.5.l_hbm), custom_call_target="tpu_custom_call" | custom-call | flops 1006632960 | bytes 19660800 | tf_op jit(solution)/shard_map/near_sum/pallas_call | solution.py:390
  92.7 0.0 collective-permute-done.3.l_hbm
  92.8 0.7 copy-done.2
  93.5 3.9 %near_sum.5 = f32[128,64]{1,0:T(8,128)} custom-call(bf16[4,64,32768]{2,1,0:T(8,128)(2,1)} %get-tuple-element.26.wide_hbm, bf16[4,64,16384]{2,1,0:T(8,128)(2,1)} %get-tuple-element.27.thin_hbm, bf16[64,16,256]{2,1,0:T(8,128)(2,1)} %collective-permute-done.2.x_hbm, bf16[64,16,128]{2,1,0:T(8,128)(2,1)} %copy-done.2, f32[128,64]{1,0:T(8,128)} %get-tuple-element.36.rest_0_, ...), custom_call_target="tpu_custom_call" | custom-call | flops 201326592 | bytes 3932160 | tf_op jit(solution)/shard_map/near_sum/pallas_call | solution.py:390
  97.3 0.8 dynamic-slice_bitcast_fusion.2
  98.1 30.9 %collective-permute-start.6 = (f32[2,2,8,64]{3,2,1,0:T(8,128)S(1)}, f32[2,2,8,64]{3,2,1,0:T(8,128)S(1)}, u32[]{:S(2)}, u32[]{:S(2)}) collective-permute-start(f32[2,2,8,64]{3,2,1,0:T(8,128)S(1)} %get-tuple-element.39), channel_id=1, source_target_pairs={{0,4},{1,5},{2,6},{3,7},{4,0},{5,1},{6,2},{7,3},{8,12},{9,13},{10,... | collective-permute-start | bytes 24584 | tf_op jit(solution)/shard_map/ppermute | solution.py:438
  129.0 2.6 %collective-permute-start.7 = (f32[2,2,8,64]{3,2,1,0:T(8,128)S(1)}, f32[2,2,8,64]{3,2,1,0:T(8,128)S(1)}, u32[]{:S(2)}, u32[]{:S(2)}) collective-permute-start(f32[2,2,8,64]{3,2,1,0:T(8,128)S(1)} %get-tuple-element.41), channel_id=1, source_target_pairs={{0,8},{1,9},{2,10},{3,11},{4,12},{5,13},{6,14},{7,15},{8,0},{9,1},... | collective-permute-start | bytes 24584 | tf_op jit(solution)/shard_map/ppermute | solution.py:438
  131.6 0.0 collective-permute-done.6
  131.6 2.0 %collective-permute-done.7 = f32[2,2,8,64]{3,2,1,0:T(8,128)S(1)} collective-permute-done((f32[2,2,8,64]{3,2,1,0:T(8,128)S(1)}, f32[2,2,8,64]{3,2,1,0:T(8,128)S(1)}, u32[]{:S(2)}, u32[]{:S(2)}) %collective-permute-start.7) | collective-permute-done | bytes 8224 | tf_op jit(solution)/shard_map/ppermute | solution.py:438
  133.6 3.5 %collective-permute-done.8 = f32[2,2,8,64]{3,2,1,0:T(8,128)S(1)} collective-permute-done((f32[2,2,8,64]{3,2,1,0:T(8,128)S(1)}, f32[2,2,8,64]{3,2,1,0:T(8,128)S(1)}, u32[]{:S(2)}, u32[]{:S(2)}) %collective-permute-start.8) | collective-permute-done | bytes 8224 | tf_op jit(solution)/shard_map/ppermute | solution.py:438
  137.1 0.7 fusion.1
  137.9 23.6 %collective-permute-start.10 = (f32[8,64]{1,0:T(8,128)S(1)}, f32[8,64]{1,0:T(8,128)S(1)}, u32[]{:S(2)}, u32[]{:S(2)}) collective-permute-start(f32[8,64]{1,0:T(8,128)S(1)} %get-tuple-element.44), channel_id=1, source_target_pairs={{0,2},{1,3},{2,0},{3,1},{4,6},{5,7},{6,4},{7,5},{8,10},{9,11},{10,... | collective-permute-start | bytes 6152 | tf_op jit(solution)/shard_map/ppermute | solution.py:438
  161.5 0.0 collective-permute-start.11
  161.5 0.2 collective-permute-start.9
  161.7 1.4 collective-permute-done.10
  163.1 1.4 collective-permute-done.11
  164.5 0.0 collective-permute-done.9
  164.5 0.6 fusion.3
  (9 shorter events, 0.0 us)
Async XLA Ops:
  8.1 72.5 %collective-permute-start.4 = (bf16[64,80,256]{2,1,0:T(8,128)(2,1)}, bf16[64,80,256]{2,1,0:T(8,128)(2,1)S(1)}, u32[]{:S(2)}, u32[]{:S(2)}) collective-permute-start(bf16[64,80,256]{2,1,0:T(8,128)(2,1)} %get-tuple-element.37), channel_id=1, source_target_pairs={{0,1},{1,2},{2,3},{3,4},{4,5},{5,6},{6,7},{7,8},{8,9},{9,10},{10,1... | collective-permute-start | bytes 7864328 | tf_op jit(solution)/shard_map/ppermute | solution.py:459
  10.6 17.2 %collective-permute-start = (bf16[76,32,256]{2,1,0:T(8,128)(2,1)}, bf16[76,32,256]{2,1,0:T(8,128)(2,1)}, u32[]{:S(2)}, u32[]{:S(2)}) collective-permute-start(bf16[76,32,256]{2,1,0:T(8,128)(2,1)} %get-tuple-element.24), channel_id=1, source_target_pairs={{0,1},{1,2},{2,3},{3,4},{4,5},{5,6},{6,7},{7,8},{8,9},{9,10},{10,1... | collective-permute-start | bytes 3735560 | tf_op jit(solution)/shard_map/ppermute | solution.py:459
  16.0 10.5 %collective-permute-start.1 = (bf16[88,32,128]{2,1,0:T(8,128)(2,1)}, bf16[88,32,128]{2,1,0:T(8,128)(2,1)S(1)}, u32[]{:S(2)}, u32[]{:S(2)}) collective-permute-start(bf16[88,32,128]{2,1,0:T(8,128)(2,1)} %get-tuple-element.25), channel_id=1, source_target_pairs={{1,0},{2,1},{3,2},{4,3},{5,4},{6,5},{7,6},{8,7},{9,8},{10,9},{11,1... | collective-permute-start | bytes 2162696 | tf_op jit(solution)/shard_map/ppermute | solution.py:459
  17.3 63.3 %collective-permute-start.5 = (bf16[64,80,128]{2,1,0:T(8,128)(2,1)}, bf16[64,80,128]{2,1,0:T(8,128)(2,1)}, u32[]{:S(2)}, u32[]{:S(2)}) collective-permute-start(bf16[64,80,128]{2,1,0:T(8,128)(2,1)} %get-tuple-element.38), channel_id=1, source_target_pairs={{1,0},{2,1},{3,2},{4,3},{5,4},{6,5},{7,6},{8,7},{9,8},{10,9},{11,1... | collective-permute-start | bytes 3932168 | tf_op jit(solution)/shard_map/ppermute | solution.py:459
  22.0 70.8 %collective-permute-start.2 = (bf16[64,16,256]{2,1,0:T(8,128)(2,1)}, bf16[64,16,256]{2,1,0:T(8,128)(2,1)}, u32[]{:S(2)}, u32[]{:S(2)}) collective-permute-start(bf16[64,16,256]{2,1,0:T(8,128)(2,1)} %get-tuple-element.34), channel_id=1, source_target_pairs={{0,1},{1,2},{2,3},{3,4},{4,5},{5,6},{6,7},{7,8},{8,9},{9,10},{10,1... | collective-permute-start | bytes 1572872 | tf_op jit(solution)/shard_map/ppermute | solution.py:459
  26.5 1.3 copy-start.1
  26.5 66.2 %collective-permute-start.3 = (bf16[64,16,128]{2,1,0:T(8,128)(2,1)}, bf16[64,16,128]{2,1,0:T(8,128)(2,1)S(1)}, u32[]{:S(2)}, u32[]{:S(2)}) collective-permute-start(bf16[64,16,128]{2,1,0:T(8,128)(2,1)} %get-tuple-element.35), channel_id=1, source_target_pairs={{1,0},{2,1},{3,2},{4,3},{5,4},{6,5},{7,6},{8,7},{9,8},{10,9},{11,1... | collective-permute-start | bytes 786440 | tf_op jit(solution)/shard_map/ppermute | solution.py:459
  80.6 1.6 copy-start
  92.7 0.7 copy-start.2
  98.1 33.5 %collective-permute-start.6 = (f32[2,2,8,64]{3,2,1,0:T(8,128)S(1)}, f32[2,2,8,64]{3,2,1,0:T(8,128)S(1)}, u32[]{:S(2)}, u32[]{:S(2)}) collective-permute-start(f32[2,2,8,64]{3,2,1,0:T(8,128)S(1)} %get-tuple-element.39), channel_id=1, source_target_pairs={{0,4},{1,5},{2,6},{3,7},{4,0},{5,1},{6,2},{7,3},{8,12},{9,13},{10,... | collective-permute-start | bytes 24584 | tf_op jit(solution)/shard_map/ppermute | solution.py:438
  129.0 4.6 %collective-permute-start.7 = (f32[2,2,8,64]{3,2,1,0:T(8,128)S(1)}, f32[2,2,8,64]{3,2,1,0:T(8,128)S(1)}, u32[]{:S(2)}, u32[]{:S(2)}) collective-permute-start(f32[2,2,8,64]{3,2,1,0:T(8,128)S(1)} %get-tuple-element.41), channel_id=1, source_target_pairs={{0,8},{1,9},{2,10},{3,11},{4,12},{5,13},{6,14},{7,15},{8,0},{9,1},... | collective-permute-start | bytes 24584 | tf_op jit(solution)/shard_map/ppermute | solution.py:438
  131.6 5.5 %collective-permute-start.8 = (f32[2,2,8,64]{3,2,1,0:T(8,128)S(1)}, f32[2,2,8,64]{3,2,1,0:T(8,128)S(1)}, u32[]{:S(2)}, u32[]{:S(2)}) collective-permute-start(f32[2,2,8,64]{3,2,1,0:T(8,128)S(1)} %get-tuple-element.40), channel_id=1, source_target_pairs={{0,12},{1,13},{2,14},{3,15},{4,8},{5,9},{6,10},{7,11},{8,4},{9,5},... | collective-permute-start | bytes 24584 | tf_op jit(solution)/shard_map/ppermute | solution.py:438
  137.9 25.2 %collective-permute-start.10 = (f32[8,64]{1,0:T(8,128)S(1)}, f32[8,64]{1,0:T(8,128)S(1)}, u32[]{:S(2)}, u32[]{:S(2)}) collective-permute-start(f32[8,64]{1,0:T(8,128)S(1)} %get-tuple-element.44), channel_id=1, source_target_pairs={{0,2},{1,3},{2,0},{3,1},{4,6},{5,7},{6,4},{7,5},{8,10},{9,11},{10,... | collective-permute-start | bytes 6152 | tf_op jit(solution)/shard_map/ppermute | solution.py:438
  161.5 3.0 %collective-permute-start.11 = (f32[8,64]{1,0:T(8,128)S(1)}, f32[8,64]{1,0:T(8,128)S(1)}, u32[]{:S(2)}, u32[]{:S(2)}) collective-permute-start(f32[8,64]{1,0:T(8,128)S(1)} %get-tuple-element.43), channel_id=1, source_target_pairs={{0,3},{1,2},{2,1},{3,0},{4,7},{5,6},{6,5},{7,4},{8,11},{9,10},{10,... | collective-permute-start | bytes 6152 | tf_op jit(solution)/shard_map/ppermute | solution.py:438
  161.5 3.0 %collective-permute-start.9 = (f32[8,64]{1,0:T(8,128)S(1)}, f32[8,64]{1,0:T(8,128)S(1)}, u32[]{:S(2)}, u32[]{:S(2)}) collective-permute-start(f32[8,64]{1,0:T(8,128)S(1)} %get-tuple-element.42), channel_id=1, source_target_pairs={{0,1},{1,0},{2,3},{3,2},{4,5},{5,4},{6,7},{7,6},{8,9},{9,8},{10,11... | collective-permute-start | bytes 6152 | tf_op jit(solution)/shard_map/ppermute | solution.py:438

commit v2 on v1

--- a/solution.py
+++ b/solution.py
@@ -7,7 +7,7 @@
 from jax.experimental.pallas import tpu as pltpu
 from jax.sharding import PartitionSpec as P
 
-CUTS = ((96, 32), (0, 80), (80, 16))
+CUTS = ((112, 16), (0, 96), (96, 16))
 AUX_STEP = 16
 GROUP = 4
 ROW_STEP = 16
@@ -323,7 +323,7 @@
             pltpu.VMEM((aux, w * band), bf),
         ],
         compiler_params=pltpu.CompilerParams(vmem_limit_bytes=VMEM_LIMIT),
-        cost_estimate=pl.CostEstimate(flops=flops, bytes_accessed=50_000_000, transcendentals=0),
+        cost_estimate=pl.CostEstimate(flops=20 * flops, bytes_accessed=800_000_000, transcendentals=0),
         name="own_terms",
     )(tensor, flag, occ, vir, occ_flag, vir_flag, up, down)
 
@@ -456,7 +456,9 @@
         else:
             x, l = later_cut(source, tensor_mask, begin, rows)
         source, x, l = lax.optimization_barrier((source, x, l))
-        arrived.append((lax.ppermute(x, "orb", forward), lax.ppermute(l, "orb", backward)))
+        if arrived:
+            x, l, *arrived[0] = lax.optimization_barrier((x, l, *arrived[0]))
+        arrived.append([lax.ppermute(x, "orb", forward), lax.ppermute(l, "orb", backward)])
 
     total, wide, thin = own_terms(
         tensor, tensor_mask, occupied, virtual, occupied_mask, virtual_mask, *arrived[0]

time: 166 us -> 119 us (0.72)
  starting transfers between devices: 73.6 us -> 30.3 us
  local copies, waits for them, and re-layouts: 3.03 us -> 0.78 us
    ppermute x6, starting transfers between devices: 57.3 us -> 8.91 us  [scattered_sum(): total = total + lax.ppermute(pick(flips), axis, pairs)]
    ppermute x3, starting transfers between devices: 12.4 us -> 17.5 us  [body(): lax.ppermute(x, 'orb', forward)]
    unnamed x6 -> x4, local copies, waits for them, and re-layouts: 2.26 us -> 0.01 us
  transfers between devices with their start and end apart: 12 -> 12, of which waited for: 4 -> 5; matrix products, arithmetic and copies ran while one was open for 0% -> 0% of each run, Pallas kernels for 40% -> 61%
where the time goes in v2:
time: 119 us
  Pallas kernels  78.4 us (66%)
  starting transfers between devices  30.3 us (25%)
  waiting for transfers between devices  7.92 us (7%)
  other arithmetic  1.32 us (1%)
    pallas_call x1, Pallas kernels, own_terms(): pl.pallas_call(functools.partial(own_kernel, times, w), grid=(aux // AUX_...  46.5 us
    pallas_call x3, Pallas kernels, near_sum(): pl.pallas_call(functools.partial(near_kernel, begin, steps, skips, len(be...  20.7 us
    ppermute x3, starting transfers between devices, body(): lax.ppermute(x, 'orb', forward)  17.5 us
    ppermute x6, starting transfers between devices, scattered_sum(): total = total + lax.ppermute(pick(flips), axis, pairs)  8.91 us
    pallas_call x2, Pallas kernels, later_cut(): pl.pallas_call(functools.partial(cut_blocks, w), grid=(aux // AUX_STEP,),...  8.74 us
    ppermute x6, waiting for transfers between devices, scattered_sum(): total = total + lax.ppermute(pick(flips), axis, pairs)  7.9 us
    ppermute x3, starting transfers between devices, body(): lax.ppermute(l, 'orb', backward)  3.86 us
    pallas_call x1, Pallas kernels, first_cut(): pl.pallas_call(functools.partial(first_cut_kernel, times, w, rows), grid=...  2.52 us
  transfers between devices with their start and end apart: 12, of which 5 were waited for; matrix products, arithmetic and copies ran while one was open for 0% of the time, Pallas kernels for 61%

profile of v2, /device:TPU:0, one launch (start us, length us, event | category | flops | bytes accessed | tf_op | source)
XLA Modules:
  0.0 118.9 jit_solution(10032328096842222253)
XLA Ops:
  0.0 2.5 %first_cut.1 = (bf16[88,16,256]{2,1,0:T(8,128)(2,1)}, bf16[112,16,128]{2,1,0:T(8,128)(2,1)}) custom-call(bf16[64,128,384]{2,1,0:T(8,128)(2,1)} %b_ref.5, s32[1,3]{1,0:T(1,128)} %flag_ref.7, bf16[2,128,384]{2,1,0:T(8,128)(2,1)} %occ_ref.3, bf16[2,128,384]{2,1,0:T(8,128)(2,1)} %vir_ref.3, s32[2,1,3]{2,1,0:T(1,128)} %occ_flag.3, s32[2,1,3]{2,1,0:T(1,128)} %vir_flag.3), custom_call_target="tpu_custom_call" | custom-call | tf_op jit(solution)/shard_map/first_cut/pallas_call | solution.py:80
  2.5 2.4 %collective-permute-start = (bf16[88,16,256]{2,1,0:T(8,128)(2,1)}, bf16[88,16,256]{2,1,0:T(8,128)(2,1)S(1)}, u32[]{:S(2)}, u32[]{:S(2)}) collective-permute-start(bf16[88,16,256]{2,1,0:T(8,128)(2,1)} %get-tuple-element.42), channel_id=1, source_target_pairs={{0,1},{1,2},{2,3},{3,4},{4,5},{5,6},{6,7},{7,8},{8,9},{9,10},{10,1... | collective-permute-start | bytes 2162696 | tf_op jit(solution)/shard_map/ppermute | solution.py:461
  4.9 1.3 %collective-permute-start.1 = (bf16[112,16,128]{2,1,0:T(8,128)(2,1)}, bf16[112,16,128]{2,1,0:T(8,128)(2,1)S(1)}, u32[]{:S(2)}, u32[]{:S(2)}) collective-permute-start(bf16[112,16,128]{2,1,0:T(8,128)(2,1)} %get-tuple-element.43), channel_id=1, source_target_pairs={{1,0},{2,1},{3,2},{4,3},{5,4},{6,5},{7,6},{8,7},{9,8},{10,9},{11,1... | collective-permute-start | bytes 1376264 | tf_op jit(solution)/shard_map/ppermute | solution.py:461
  6.2 5.4 %later_cut.2 = (bf16[64,96,256]{2,1,0:T(8,128)(2,1)}, bf16[64,96,128]{2,1,0:T(8,128)(2,1)}) custom-call(bf16[64,128,384]{2,1,0:T(8,128)(2,1)} %b_ref.5, s32[1,3]{1,0:T(1,128)} %flag_ref.7), custom_call_target="tpu_custom_call" | custom-call | tf_op jit(solution)/shard_map/later_cut/pallas_call | solution.py:96
  11.6 3.4 %later_cut.3 = (bf16[64,16,256]{2,1,0:T(8,128)(2,1)}, bf16[64,16,128]{2,1,0:T(8,128)(2,1)}) custom-call(bf16[64,128,384]{2,1,0:T(8,128)(2,1)} %b_ref.5, s32[1,3]{1,0:T(1,128)} %flag_ref.7), custom_call_target="tpu_custom_call" | custom-call | tf_op jit(solution)/shard_map/later_cut/pallas_call | solution.py:96
  15.0 0.0 collective-permute-done.up_ref.x_hbm
  15.0 1.3 %collective-permute-start.3 = (bf16[64,16,128]{2,1,0:T(8,128)(2,1)}, bf16[64,16,128]{2,1,0:T(8,128)(2,1)}, u32[]{:S(2)}, u32[]{:S(2)}) collective-permute-start(bf16[64,16,128]{2,1,0:T(8,128)(2,1)} %get-tuple-element.51), channel_id=1, source_target_pairs={{1,0},{2,1},{3,2},{4,3},{5,4},{6,5},{7,6},{8,7},{9,8},{10,9},{11,1... | collective-permute-start | bytes 786440 | tf_op jit(solution)/shard_map/ppermute | solution.py:461
  16.3 9.3 %collective-permute-start.2 = (bf16[64,16,256]{2,1,0:T(8,128)(2,1)}, bf16[64,16,256]{2,1,0:T(8,128)(2,1)}, u32[]{:S(2)}, u32[]{:S(2)}) collective-permute-start(bf16[64,16,256]{2,1,0:T(8,128)(2,1)} %get-tuple-element.50), channel_id=1, source_target_pairs={{0,1},{1,2},{2,3},{3,4},{4,5},{5,6},{6,7},{7,8},{8,9},{9,10},{10,1... | collective-permute-start | bytes 1572872 | tf_op jit(solution)/shard_map/ppermute | solution.py:461
  25.6 1.3 %collective-permute-start.5 = (bf16[64,96,128]{2,1,0:T(8,128)(2,1)}, bf16[64,96,128]{2,1,0:T(8,128)(2,1)}, u32[]{:S(2)}, u32[]{:S(2)}) collective-permute-start(bf16[64,96,128]{2,1,0:T(8,128)(2,1)} %get-tuple-element.54), channel_id=1, source_target_pairs={{1,0},{2,1},{3,2},{4,3},{5,4},{6,5},{7,6},{8,7},{9,8},{10,9},{11,1... | collective-permute-start | bytes 4718600 | tf_op jit(solution)/shard_map/ppermute | solution.py:461
  26.9 5.9 %collective-permute-start.4 = (bf16[64,96,256]{2,1,0:T(8,128)(2,1)}, bf16[64,96,256]{2,1,0:T(8,128)(2,1)}, u32[]{:S(2)}, u32[]{:S(2)}) collective-permute-start(bf16[64,96,256]{2,1,0:T(8,128)(2,1)} %get-tuple-element.53), channel_id=1, source_target_pairs={{0,1},{1,2},{2,3},{3,4},{4,5},{5,6},{6,7},{7,8},{8,9},{9,10},{10,1... | collective-permute-start | bytes 9437192 | tf_op jit(solution)/shard_map/ppermute | solution.py:461
  32.7 46.5 %own_terms.1 = (f32[128,64]{1,0:T(8,128)}, bf16[4,64,32768]{2,1,0:T(8,128)(2,1)}, bf16[4,64,16384]{2,1,0:T(8,128)(2,1)}) custom-call(bf16[64,128,384]{2,1,0:T(8,128)(2,1)} %b_ref.5, s32[1,3]{1,0:T(1,128)} %flag_ref.7, bf16[2,128,384]{2,1,0:T(8,128)(2,1)} %occ_ref.3, bf16[2,128,384]{2,1,0:T(8,128)(2,1)} %vir_ref.3, s32[2,1,3]{2,1,0:T(1,128)} %occ_flag.3, ...), custom_call_target="tpu_custom_call" | custom-call | flops 246960619520 | bytes 800000000 | tf_op jit(solution)/shard_map/own_terms/pallas_call | solution.py:292
  79.2 3.8 %near_sum.3.rest_1_ = f32[256,64]{1,0:T(8,128)} custom-call(bf16[4,64,32768]{2,1,0:T(8,128)(2,1)} %get-tuple-element.48.wide_hbm, bf16[4,64,16384]{2,1,0:T(8,128)(2,1)} %get-tuple-element.49.thin_hbm, bf16[88,16,256]{2,1,0:T(8,128)(2,1)} %copy-done, bf16[112,16,128]{2,1,0:T(8,128)(2,1)} %copy-done.1), custom_call_target="tpu_custom_call" | custom-call | flops 201326592 | bytes 3932160 | tf_op jit(solution)/shard_map/near_sum/pallas_call | solution.py:390
  83.0 0.0 collective-permute-done.5.l_hbm
  83.0 0.0 collective-permute-done.4.x_hbm
  83.0 13.0 %near_sum.4.rest_2_ = f32[256,64]{1,0:T(8,128)} custom-call(bf16[4,64,32768]{2,1,0:T(8,128)(2,1)} %get-tuple-element.48.wide_hbm, bf16[4,64,16384]{2,1,0:T(8,128)(2,1)} %get-tuple-element.49.thin_hbm, bf16[64,96,256]{2,1,0:T(8,128)(2,1)} %collective-permute-done.4.x_hbm, bf16[64,96,128]{2,1,0:T(8,128)(2,1)} %collective-permute-done.5.l_hbm), custom_call_target="tpu_custom_call" | custom-call | flops 1207959552 | bytes 23592960 | tf_op jit(solution)/shard_map/near_sum/pallas_call | solution.py:390
  96.1 0.0 collective-permute-done.3.l_hbm
  96.1 3.9 %near_sum.5 = f32[128,64]{1,0:T(8,128)} custom-call(bf16[4,64,32768]{2,1,0:T(8,128)(2,1)} %get-tuple-element.48.wide_hbm, bf16[4,64,16384]{2,1,0:T(8,128)(2,1)} %get-tuple-element.49.thin_hbm, bf16[64,16,256]{2,1,0:T(8,128)(2,1)} %collective-permute-done.2.x_hbm, bf16[64,16,128]{2,1,0:T(8,128)(2,1)} %collective-permute-done.3.l_hbm, ...), custom_call_target="tpu_custom_call" | custom-call | flops 201326592 | bytes 3932160 | tf_op jit(solution)/shard_map/near_sum/pallas_call | solution.py:390
  100.0 0.8 dynamic-slice_bitcast_fusion.2
  100.7 0.7 collective-permute-start.6
  101.4 2.5 %collective-permute-start.8 = (f32[2,2,8,64]{3,2,1,0:T(8,128)S(1)}, f32[2,2,8,64]{3,2,1,0:T(8,128)S(1)}, u32[]{:S(2)}, u32[]{:S(2)}) collective-permute-start(f32[2,2,8,64]{3,2,1,0:T(8,128)S(1)} %get-tuple-element.56), channel_id=1, source_target_pairs={{0,12},{1,13},{2,14},{3,15},{4,8},{5,9},{6,10},{7,11},{8,4},{9,5},... | collective-permute-start | bytes 24584 | tf_op jit(solution)/shard_map/ppermute | solution.py:438
  103.9 0.3 collective-permute-start.7
  104.2 0.2 collective-permute-done.6
  104.5 2.6 %collective-permute-done.8 = f32[2,2,8,64]{3,2,1,0:T(8,128)S(1)} collective-permute-done((f32[2,2,8,64]{3,2,1,0:T(8,128)S(1)}, f32[2,2,8,64]{3,2,1,0:T(8,128)S(1)}, u32[]{:S(2)}, u32[]{:S(2)}) %collective-permute-start.8) | collective-permute-done | bytes 8224 | tf_op jit(solution)/shard_map/ppermute | solution.py:438
  107.1 1.5 %collective-permute-done.7 = f32[2,2,8,64]{3,2,1,0:T(8,128)S(1)} collective-permute-done((f32[2,2,8,64]{3,2,1,0:T(8,128)S(1)}, f32[2,2,8,64]{3,2,1,0:T(8,128)S(1)}, u32[]{:S(2)}, u32[]{:S(2)}) %collective-permute-start.7) | collective-permute-done | bytes 8224 | tf_op jit(solution)/shard_map/ppermute | solution.py:438
  108.6 0.7 fusion.1
  109.3 2.8 %collective-permute-start.9 = (f32[8,64]{1,0:T(8,128)S(1)}, f32[8,64]{1,0:T(8,128)S(1)}, u32[]{:S(2)}, u32[]{:S(2)}) collective-permute-start(f32[8,64]{1,0:T(8,128)S(1)} %get-tuple-element.58), channel_id=1, source_target_pairs={{0,1},{1,0},{2,3},{3,2},{4,5},{5,4},{6,7},{7,6},{8,9},{9,8},{10,11... | collective-permute-start | bytes 6152 | tf_op jit(solution)/shard_map/ppermute | solution.py:438
  112.1 2.6 %collective-permute-start.11 = (f32[8,64]{1,0:T(8,128)S(1)}, f32[8,64]{1,0:T(8,128)S(1)}, u32[]{:S(2)}, u32[]{:S(2)}) collective-permute-start(f32[8,64]{1,0:T(8,128)S(1)} %get-tuple-element.59), channel_id=1, source_target_pairs={{0,3},{1,2},{2,1},{3,0},{4,7},{5,6},{6,5},{7,4},{8,11},{9,10},{10,... | collective-permute-start | bytes 6152 | tf_op jit(solution)/shard_map/ppermute | solution.py:438
  114.7 0.0 collective-permute-start.10
  114.7 0.0 collective-permute-done.9
  114.7 1.3 %collective-permute-done.11 = f32[8,64]{1,0:T(8,128)S(1)} collective-permute-done((f32[8,64]{1,0:T(8,128)S(1)}, f32[8,64]{1,0:T(8,128)S(1)}, u32[]{:S(2)}, u32[]{:S(2)}) %collective-permute-start.11) | collective-permute-done | bytes 2080 | tf_op jit(solution)/shard_map/ppermute | solution.py:438
  116.0 2.3 %collective-permute-done.10 = f32[8,64]{1,0:T(8,128)S(1)} collective-permute-done((f32[8,64]{1,0:T(8,128)S(1)}, f32[8,64]{1,0:T(8,128)S(1)}, u32[]{:S(2)}, u32[]{:S(2)}) %collective-permute-start.10) | collective-permute-done | bytes 2080 | tf_op jit(solution)/shard_map/ppermute | solution.py:438
  118.3 0.6 fusion.3
  (7 shorter events, 0.0 us)
Async XLA Ops:
  2.5 12.5 %collective-permute-start = (bf16[88,16,256]{2,1,0:T(8,128)(2,1)}, bf16[88,16,256]{2,1,0:T(8,128)(2,1)S(1)}, u32[]{:S(2)}, u32[]{:S(2)}) collective-permute-start(bf16[88,16,256]{2,1,0:T(8,128)(2,1)} %get-tuple-element.42), channel_id=1, source_target_pairs={{0,1},{1,2},{2,3},{3,4},{4,5},{5,6},{6,7},{7,8},{8,9},{9,10},{10,1... | collective-permute-start | bytes 2162696 | tf_op jit(solution)/shard_map/ppermute | solution.py:461
  4.9 10.1 %collective-permute-start.1 = (bf16[112,16,128]{2,1,0:T(8,128)(2,1)}, bf16[112,16,128]{2,1,0:T(8,128)(2,1)S(1)}, u32[]{:S(2)}, u32[]{:S(2)}) collective-permute-start(bf16[112,16,128]{2,1,0:T(8,128)(2,1)} %get-tuple-element.43), channel_id=1, source_target_pairs={{1,0},{2,1},{3,2},{4,3},{5,4},{6,5},{7,6},{8,7},{9,8},{10,9},{11,1... | collective-permute-start | bytes 1376264 | tf_op jit(solution)/shard_map/ppermute | solution.py:461
  15.0 17.8 %copy-start.1 = (bf16[112,16,128]{2,1,0:T(8,128)(2,1)}, bf16[112,16,128]{2,1,0:T(8,128)(2,1)S(1)}, u32[]{:S(2)}) copy-start(bf16[112,16,128]{2,1,0:T(8,128)(2,1)S(1)} %collective-permute-done.1.down_ref.l_hbm) | copy-start | bytes 1376260
  15.0 17.7 %copy-start = (bf16[88,16,256]{2,1,0:T(8,128)(2,1)}, bf16[88,16,256]{2,1,0:T(8,128)(2,1)S(1)}, u32[]{:S(2)}) copy-start(bf16[88,16,256]{2,1,0:T(8,128)(2,1)S(1)} %collective-permute-done.up_ref.x_hbm) | copy-start | bytes 2162692
  15.0 81.0 %collective-permute-start.3 = (bf16[64,16,128]{2,1,0:T(8,128)(2,1)}, bf16[64,16,128]{2,1,0:T(8,128)(2,1)}, u32[]{:S(2)}, u32[]{:S(2)}) collective-permute-start(bf16[64,16,128]{2,1,0:T(8,128)(2,1)} %get-tuple-element.51), channel_id=1, source_target_pairs={{1,0},{2,1},{3,2},{4,3},{5,4},{6,5},{7,6},{8,7},{9,8},{10,9},{11,1... | collective-permute-start | bytes 786440 | tf_op jit(solution)/shard_map/ppermute | solution.py:461
  16.3 79.8 %collective-permute-start.2 = (bf16[64,16,256]{2,1,0:T(8,128)(2,1)}, bf16[64,16,256]{2,1,0:T(8,128)(2,1)}, u32[]{:S(2)}, u32[]{:S(2)}) collective-permute-start(bf16[64,16,256]{2,1,0:T(8,128)(2,1)} %get-tuple-element.50), channel_id=1, source_target_pairs={{0,1},{1,2},{2,3},{3,4},{4,5},{5,6},{6,7},{7,8},{8,9},{9,10},{10,1... | collective-permute-start | bytes 1572872 | tf_op jit(solution)/shard_map/ppermute | solution.py:461
  25.6 57.4 %collective-permute-start.5 = (bf16[64,96,128]{2,1,0:T(8,128)(2,1)}, bf16[64,96,128]{2,1,0:T(8,128)(2,1)}, u32[]{:S(2)}, u32[]{:S(2)}) collective-permute-start(bf16[64,96,128]{2,1,0:T(8,128)(2,1)} %get-tuple-element.54), channel_id=1, source_target_pairs={{1,0},{2,1},{3,2},{4,3},{5,4},{6,5},{7,6},{8,7},{9,8},{10,9},{11,1... | collective-permute-start | bytes 4718600 | tf_op jit(solution)/shard_map/ppermute | solution.py:461
  26.9 56.1 %collective-permute-start.4 = (bf16[64,96,256]{2,1,0:T(8,128)(2,1)}, bf16[64,96,256]{2,1,0:T(8,128)(2,1)}, u32[]{:S(2)}, u32[]{:S(2)}) collective-permute-start(bf16[64,96,256]{2,1,0:T(8,128)(2,1)} %get-tuple-element.53), channel_id=1, source_target_pairs={{0,1},{1,2},{2,3},{3,4},{4,5},{5,6},{6,7},{7,8},{8,9},{9,10},{10,1... | collective-permute-start | bytes 9437192 | tf_op jit(solution)/shard_map/ppermute | solution.py:461
  100.7 3.7 %collective-permute-start.6 = (f32[2,2,8,64]{3,2,1,0:T(8,128)S(1)}, f32[2,2,8,64]{3,2,1,0:T(8,128)S(1)}, u32[]{:S(2)}, u32[]{:S(2)}) collective-permute-start(f32[2,2,8,64]{3,2,1,0:T(8,128)S(1)} %get-tuple-element.55), channel_id=1, source_target_pairs={{0,4},{1,5},{2,6},{3,7},{4,0},{5,1},{6,2},{7,3},{8,12},{9,13},{10,... | collective-permute-start | bytes 24584 | tf_op jit(solution)/shard_map/ppermute | solution.py:438
  101.4 5.6 %collective-permute-start.8 = (f32[2,2,8,64]{3,2,1,0:T(8,128)S(1)}, f32[2,2,8,64]{3,2,1,0:T(8,128)S(1)}, u32[]{:S(2)}, u32[]{:S(2)}) collective-permute-start(f32[2,2,8,64]{3,2,1,0:T(8,128)S(1)} %get-tuple-element.56), channel_id=1, source_target_pairs={{0,12},{1,13},{2,14},{3,15},{4,8},{5,9},{6,10},{7,11},{8,4},{9,5},... | collective-permute-start | bytes 24584 | tf_op jit(solution)/shard_map/ppermute | solution.py:438
  103.9 4.6 %collective-permute-start.7 = (f32[2,2,8,64]{3,2,1,0:T(8,128)S(1)}, f32[2,2,8,64]{3,2,1,0:T(8,128)S(1)}, u32[]{:S(2)}, u32[]{:S(2)}) collective-permute-start(f32[2,2,8,64]{3,2,1,0:T(8,128)S(1)} %get-tuple-element.57), channel_id=1, source_target_pairs={{0,8},{1,9},{2,10},{3,11},{4,12},{5,13},{6,14},{7,15},{8,0},{9,1},... | collective-permute-start | bytes 24584 | tf_op jit(solution)/shard_map/ppermute | solution.py:438
  109.3 5.4 %collective-permute-start.9 = (f32[8,64]{1,0:T(8,128)S(1)}, f32[8,64]{1,0:T(8,128)S(1)}, u32[]{:S(2)}, u32[]{:S(2)}) collective-permute-start(f32[8,64]{1,0:T(8,128)S(1)} %get-tuple-element.58), channel_id=1, source_target_pairs={{0,1},{1,0},{2,3},{3,2},{4,5},{5,4},{6,7},{7,6},{8,9},{9,8},{10,11... | collective-permute-start | bytes 6152 | tf_op jit(solution)/shard_map/ppermute | solution.py:438
  112.1 3.9 %collective-permute-start.11 = (f32[8,64]{1,0:T(8,128)S(1)}, f32[8,64]{1,0:T(8,128)S(1)}, u32[]{:S(2)}, u32[]{:S(2)}) collective-permute-start(f32[8,64]{1,0:T(8,128)S(1)} %get-tuple-element.59), channel_id=1, source_target_pairs={{0,3},{1,2},{2,1},{3,0},{4,7},{5,6},{6,5},{7,4},{8,11},{9,10},{10,... | collective-permute-start | bytes 6152 | tf_op jit(solution)/shard_map/ppermute | solution.py:438
  114.7 3.6 %collective-permute-start.10 = (f32[8,64]{1,0:T(8,128)S(1)}, f32[8,64]{1,0:T(8,128)S(1)}, u32[]{:S(2)}, u32[]{:S(2)}) collective-permute-start(f32[8,64]{1,0:T(8,128)S(1)} %get-tuple-element.60), channel_id=1, source_target_pairs={{0,2},{1,3},{2,0},{3,1},{4,6},{5,7},{6,4},{7,5},{8,10},{9,11},{10,... | collective-permute-start | bytes 6152 | tf_op jit(solution)/shard_map/ppermute | solution.py:438

commit v3 on v1

--- a/solution.py
+++ b/solution.py
@@ -1,4 +1,5 @@
 import functools
+import math
 
 import jax
 import jax.numpy as jnp
@@ -7,12 +8,14 @@
 from jax.experimental.pallas import tpu as pltpu
 from jax.sharding import PartitionSpec as P
 
-CUTS = ((96, 32), (0, 80), (80, 16))
+CUTS = ((0, 80), (80, 48))
 AUX_STEP = 16
-GROUP = 4
+GROUP = 8
 ROW_STEP = 16
+AHEAD = 2
 VMEM_LIMIT = 60 * 1024 * 1024
-HBM = pl.BlockSpec(memory_space=pltpu.HBM)
+NEAR_LIMIT = 12 * 1024 * 1024
+ANY = pl.BlockSpec(memory_space=pl.ANY)
 SMEM = pl.BlockSpec(memory_space=pltpu.SMEM)
 
 
@@ -38,75 +41,57 @@
     return kept(flag[t, 0, k], ref[t, :, k * width : (k + 1) * width])
 
 
-def cut_blocks(width, b_ref, flag_ref, x_ref, l_ref):
+def edge_kernel(times, width, occ_ref, vir_ref, occ_flag, vir_flag, up_ref, down_ref):
+    w = width
+    for t in range(times):
+        up_ref[t, :, :w] = part(vir_ref, t, 1, w, vir_flag)
+        up_ref[t, :, w : 2 * w] = part(vir_ref, t, 2, w, vir_flag)
+        up_ref[t, :, 2 * w :] = part(occ_ref, t, 2, w, occ_flag)
+        down_ref[t, :, :w] = part(vir_ref, t, 0, w, vir_flag)
+        down_ref[t, :, w : 2 * w] = part(vir_ref, t, 1, w, vir_flag)
+        down_ref[t, :, 2 * w :] = part(occ_ref, t, 0, w, occ_flag)
+
+
+def edges(occ, vir, occ_flag, vir_flag):
+    times, w, _ = occ.shape
+    whole = pl.BlockSpec(occ.shape, lambda i: (0, 0, 0))
+    return pl.pallas_call(
+        functools.partial(edge_kernel, times, w),
+        grid=(1,),
+        in_specs=[whole, whole, SMEM, SMEM],
+        out_specs=[whole, whole],
+        out_shape=[jax.ShapeDtypeStruct(occ.shape, occ.dtype)] * 2,
+        name="edges",
+    )(occ, vir, occ_flag, vir_flag)
+
+
+def cut_kernel(width, b_ref, flag_ref, x_ref, l_ref):
     w = width
     l_ref[...] = kept(flag_ref[0, 0], b_ref[:, :, :w])
     x_ref[:, :, :w] = kept(flag_ref[0, 1], b_ref[:, :, w : 2 * w])
     x_ref[:, :, w:] = kept(flag_ref[0, 2], b_ref[:, :, 2 * w :])
 
 
-def first_cut_kernel(
-    times, width, rows, b_ref, flag_ref, occ_ref, vir_ref, occ_flag, vir_flag, x_ref, l_ref
-):
-    w, pieces = width, width // rows
-    occ = functools.partial(part, occ_ref, width=w, flag=occ_flag)
-    vir = functools.partial(part, vir_ref, width=w, flag=vir_flag)
-    sent_up = [(vir(t, 1), vir(t, 2)) for t in range(times)]
-    flat_occ = [occ(t, 2) for t in range(times)]
-    sent_up += list(zip(flat_occ[::2], flat_occ[1::2], strict=True))
-    for n, (one, two) in enumerate(sent_up):
-        where = slice(n * pieces, (n + 1) * pieces)
-        x_ref[where, :, :w] = one.reshape(pieces, rows, w)
-        x_ref[where, :, w:] = two.reshape(pieces, rows, w)
-    sent_down = [f(t, k) for t in range(times) for f, k in ((vir, 0), (vir, 1), (occ, 0))]
-    for n, one in enumerate(sent_down):
-        l_ref[n * pieces : (n + 1) * pieces] = one.reshape(pieces, rows, w)
-    x_head, l_head = heads(times, w, rows)
-    cut_blocks(w, b_ref, flag_ref, x_ref.at[x_head:], l_ref.at[l_head:])
-
-
-def heads(times, width, rows):
-    pieces = width // rows
-    return 3 * times // 2 * pieces, 3 * times * pieces
-
-
-def first_cut(tensor, flag, occ, vir, occ_flag, vir_flag):
+def cut(tensor, flag, begin, rows):
     aux, w, band = tensor.shape
-    times = occ.shape[0]
-    begin, rows = CUTS[0]
-    x_head, l_head = heads(times, w, rows)
-    whole = pl.BlockSpec(occ.shape, lambda i: (0, 0, 0))
-    x_shape, l_shape = (x_head + aux, rows, 2 * w), (l_head + aux, rows, w)
+    size = math.gcd(begin, rows)
+    step = aux if size <= ROW_STEP else AUX_STEP
+    base = begin // size
+
+    def spec(lanes, first):
+        return pl.BlockSpec((step, size, lanes), lambda i, j: (i, first + j, 0))
+
     return pl.pallas_call(
-        functools.partial(first_cut_kernel, times, w, rows),
-        grid=(1,),
-        in_specs=[
-            pl.BlockSpec((aux, rows, band), lambda i: (0, begin // rows, 0)),
-            SMEM, whole, whole, SMEM, SMEM,
-        ],
-        out_specs=[pl.BlockSpec(n, lambda i: (0, 0, 0)) for n in (x_shape, l_shape)],
-        out_shape=[jax.ShapeDtypeStruct(n, tensor.dtype) for n in (x_shape, l_shape)],
-        compiler_params=pltpu.CompilerParams(vmem_limit_bytes=VMEM_LIMIT),
-        name="first_cut",
-    )(tensor, flag, occ, vir, occ_flag, vir_flag)
-
-
-def later_cut(tensor, flag, begin, rows):
-    aux, w, band = tensor.shape
-    return pl.pallas_call(
-        functools.partial(cut_blocks, w),
-        grid=(aux // AUX_STEP,),
-        in_specs=[pl.BlockSpec((AUX_STEP, rows, band), lambda i: (i, begin // rows, 0)), SMEM],
-        out_specs=[
-            pl.BlockSpec((AUX_STEP, rows, 2 * w), lambda i: (i, 0, 0)),
-            pl.BlockSpec((AUX_STEP, rows, w), lambda i: (i, 0, 0)),
-        ],
+        functools.partial(cut_kernel, w),
+        grid=(aux // step, rows // size),
+        in_specs=[spec(band, base), SMEM],
+        out_specs=[spec(2 * w, 0), spec(w, 0)],
         out_shape=[
             jax.ShapeDtypeStruct((aux, rows, 2 * w), tensor.dtype),
             jax.ShapeDtypeStruct((aux, rows, w), tensor.dtype),
         ],
         compiler_params=pltpu.CompilerParams(vmem_limit_bytes=VMEM_LIMIT),
-        name="later_cut",
+        name="cut",
     )(tensor, flag)
 
 
@@ -120,18 +105,15 @@
 
     @pl.when(step == 0)
     def build():
-        pieces = w // up_ref.shape[1]
-
-        def got(ref, n, lanes=slice(None)):
-            return ref[n * pieces : (n + 1) * pieces, :, lanes].reshape(w, w)
-
-        one, two = slice(None, w), slice(w, None)
         for t in range(times):
             v_low, v_own, v_high = (part(vir_ref, t, k, w, vir_flag) for k in range(3))
             o_low, o_own, o_high = (part(occ_ref, t, k, w, occ_flag) for k in range(3))
-            below_own, below_up = got(up_ref, t, one), got(up_ref, t, two)
-            below_occ = got(up_ref, times + t // 2, (one, two)[t % 2])
-            above_down, above_own, above_occ = (got(down_ref, 3 * t + n) for n in range(3))
+            below_own, below_up, below_occ = (
+                up_ref[t, :, k * w : (k + 1) * w] for k in range(3)
+            )
+            above_down, above_own, above_occ = (
+                down_ref[t, :, k * w : (k + 1) * w] for k in range(3)
+            )
 
             def cols(slot):
                 return slice((slot * times + t) * w, (slot * times + t + 1) * w)
@@ -256,13 +238,13 @@
         laying += [functools.partial(lay_own, t), functools.partial(lay_other, t)]
     for n, phase in enumerate(work):
 
-        def both(g, carry, phase=phase, before=laying[n - 1] if n else None):
+        def both(g, phase=phase, before=laying[n - 1] if n else None):
             phase(g)
             if before is not None:
                 before(g)
-            return carry
-
-        lax.fori_loop(0, loops, both, 0)
+
+        for g in range(loops):
+            both(g)
     for g in range(loops):
         laying[-1](g)
 
@@ -283,10 +265,7 @@
     aux, w, band = tensor.shape
     times = occ.shape[0]
     bf = jnp.bfloat16
-    x_head, l_head = heads(times, w, CUTS[0][1])
-
-    def whole(shape):
-        return pl.BlockSpec(shape, lambda i: (0, 0, 0))
+    whole = pl.BlockSpec(occ.shape, lambda i: (0, 0, 0))
 
     flops = 2 * aux * w * w * w * (14 * times + 9 * times)
     return pl.pallas_call(
@@ -294,8 +273,7 @@
         grid=(aux // AUX_STEP,),
         in_specs=[
             pl.BlockSpec((AUX_STEP, w, band), lambda i: (i, 0, 0)),
-            SMEM, whole(occ.shape), whole(vir.shape), SMEM, SMEM,
-            whole((x_head, *up.shape[1:])), whole((l_head, *down.shape[1:])),
+            SMEM, whole, whole, SMEM, SMEM, whole, whole,
         ],
         out_specs=[
             pl.BlockSpec((times * aux, aux), lambda i: (0, 0)),
@@ -323,29 +301,54 @@
             pltpu.VMEM((aux, w * band), bf),
         ],
         compiler_params=pltpu.CompilerParams(vmem_limit_bytes=VMEM_LIMIT),
-        cost_estimate=pl.CostEstimate(flops=flops, bytes_accessed=50_000_000, transcendentals=0),
+        cost_estimate=pl.CostEstimate(flops=flops // 50, bytes_accessed=1_000_000, transcendentals=0),
         name="own_terms",
     )(tensor, flag, occ, vir, occ_flag, vir_flag, up, down)
 
 
-def near_kernel(begin, steps, skips, earlier, wide_hbm, thin_hbm, x_hbm, l_hbm, *rest):
+def hold_kernel(parts, wide_hbm, thin_hbm, wide_ref, thin_ref, sems):
+    copies = []
+    for n, (source, target) in enumerate(((wide_hbm, wide_ref), (thin_hbm, thin_ref))):
+        share = source.shape[2] // parts
+        for j in range(parts):
+            at = pl.ds(j * share, share)
+            copies.append(
+                pltpu.make_async_copy(source.at[:, :, at], target.at[:, :, at], sems.at[n, j])
+            )
+    for copy in copies:
+        copy.start()
+    for copy in copies:
+        copy.wait()
+
+
+def hold(wide, thin):
+    parts = 4
+    return pl.pallas_call(
+        functools.partial(hold_kernel, parts),
+        in_specs=[ANY, ANY],
+        out_specs=[pl.BlockSpec(memory_space=pltpu.VMEM)] * 2,
+        out_shape=[pltpu.VMEM(wide.shape, wide.dtype), pltpu.VMEM(thin.shape, thin.dtype)],
+        scratch_shapes=[pltpu.SemaphoreType.DMA((2, parts))],
+        compiler_params=pltpu.CompilerParams(vmem_limit_bytes=NEAR_LIMIT),
+        name="hold",
+    )(wide, thin)
+
+
+def in_vmem(value):
+    return pltpu.with_memory_space_constraint(value, pltpu.VMEM)
+
+
+def near_kernel(begin, steps, earlier, wide, thin, x_hbm, l_hbm, *rest):
     before, rest = rest[:earlier], rest[earlier:]
-    out_ref, wide, thin, x, l, held, sems, held_sems = rest
-    slots, aux, w = wide.shape[1], wide.shape[2], l.shape[3]
+    out_ref, x, l, total, held, sems, held_sems = rest
+    slots, aux, w = wide.shape[0], wide.shape[1], l.shape[3]
     times = slots // 2
 
     def copies(s):
         rows = pl.ds(s * ROW_STEP, ROW_STEP)
-        far = begin + s * ROW_STEP
         return [
-            pltpu.make_async_copy(
-                wide_hbm.at[:, :, pl.ds(far * 2 * w, ROW_STEP * 2 * w)], wide.at[s], sems.at[s, 0]
-            ),
-            pltpu.make_async_copy(
-                thin_hbm.at[:, :, pl.ds(far * w, ROW_STEP * w)], thin.at[s], sems.at[s, 1]
-            ),
-            pltpu.make_async_copy(x_hbm.at[pl.ds(skips[0], aux), rows], x.at[s], sems.at[s, 2]),
-            pltpu.make_async_copy(l_hbm.at[pl.ds(skips[1], aux), rows], l.at[s], sems.at[s, 3]),
+            pltpu.make_async_copy(x_hbm.at[:, rows], x.at[s], sems.at[s, 0]),
+            pltpu.make_async_copy(l_hbm.at[:, rows], l.at[s], sems.at[s, 1]),
         ]
 
     fetch = []
@@ -354,27 +357,32 @@
         fetch.append(
             pltpu.make_async_copy(ref, held.at[n, pl.ds(0, size)], held_sems.at[n])
         )
-    for s in range(steps):
+    for s in range(min(AHEAD, steps)):
         for copy in copies(s):
             copy.start()
     for copy in fetch:
         copy.start()
-    total = None
+    total[...] = jnp.zeros_like(total)
     for s in range(steps):
+        if s + AHEAD < steps:
+            for copy in copies(s + AHEAD):
+                copy.start()
         for copy in copies(s):
             copy.wait()
-        wide_s = wide[s].reshape(slots * aux, ROW_STEP * 2 * w)
-        thin_s = thin[s].reshape(slots * aux, ROW_STEP * w)
-        term = dot_nt(wide_s, flat(x[s])) + dot_nt(thin_s, flat(l[s]))
-        total = term if total is None else total + term
+        far = begin + s * ROW_STEP
+        wide_s = wide[:, :, far * 2 * w : (far + ROW_STEP) * 2 * w]
+        thin_s = thin[:, :, far * w : (far + ROW_STEP) * w]
+        total[...] += dot_nt(wide_s.reshape(slots * aux, ROW_STEP * 2 * w), flat(x[s])) + dot_nt(
+            thin_s.reshape(slots * aux, ROW_STEP * w), flat(l[s])
+        )
     if not earlier:
-        out_ref[...] = total
+        out_ref[...] = total[...]
         return
     for copy in fetch:
         copy.wait()
     half = times * aux
     for n in range(1, earlier):
-        total = total + held[n]
+        total[...] += held[n]
     for t in range(times):
         rows = slice(t * aux, (t + 1) * aux)
         out_ref[rows] = held[0, rows] + total[rows] + total[half + t * aux : half + (t + 1) * aux].T
@@ -384,31 +392,30 @@
     slots, aux, _ = wide.shape
     w = l.shape[2]
     steps = rows // ROW_STEP
-    skips = (x.shape[0] - aux, l.shape[0] - aux)
     shape = (slots // 2 * aux if before else slots * aux, aux)
     bf = jnp.bfloat16
+    vmem = pl.BlockSpec(memory_space=pltpu.VMEM)
     return pl.pallas_call(
-        functools.partial(near_kernel, begin, steps, skips, len(before)),
-        in_specs=[HBM] * (4 + len(before)),
-        out_specs=pl.BlockSpec(memory_space=pltpu.VMEM),
+        functools.partial(near_kernel, begin, steps, len(before)),
+        in_specs=[vmem, vmem] + [ANY] * (2 + len(before)),
+        out_specs=vmem,
         out_shape=jax.ShapeDtypeStruct(shape, jnp.float32),
         scratch_shapes=[
-            pltpu.VMEM((steps, slots, aux, ROW_STEP * 2 * w), bf),
-            pltpu.VMEM((steps, slots, aux, ROW_STEP * w), bf),
             pltpu.VMEM((steps, aux, ROW_STEP, 2 * w), bf),
             pltpu.VMEM((steps, aux, ROW_STEP, w), bf),
+            pltpu.VMEM((slots * aux, aux), jnp.float32),
             pltpu.VMEM((max(len(before), 1), slots * aux, aux), jnp.float32),
-            pltpu.SemaphoreType.DMA((steps, 4)),
+            pltpu.SemaphoreType.DMA((steps, 2)),
             pltpu.SemaphoreType.DMA((max(len(before), 1),)),
         ],
-        compiler_params=pltpu.CompilerParams(vmem_limit_bytes=VMEM_LIMIT),
+        compiler_params=pltpu.CompilerParams(vmem_limit_bytes=NEAR_LIMIT),
         cost_estimate=pl.CostEstimate(
-            flops=2 * slots * aux * aux * rows * 3 * w,
-            bytes_accessed=2 * (slots + 1) * aux * rows * 3 * w,
+            flops=20 * slots * aux * aux * rows * 3 * w,
+            bytes_accessed=20 * (slots + 1) * aux * rows * 3 * w,
             transcendentals=0,
         ),
         name="near_sum",
-    )(wide, thin, x, l, *before)
+    )(in_vmem(wide), in_vmem(thin), x, l, *before)
 
 
 def scattered_sum(value, axis):
@@ -446,21 +453,20 @@
     forward = [(i, i + 1) for i in range(count - 1)]
     backward = [(i + 1, i) for i in range(count - 1)]
 
+    up, down = edges(occupied, virtual, occupied_mask, virtual_mask)
+    source, up, down = lax.optimization_barrier((tensor, up, down))
+    up = lax.ppermute(up, "orb", forward)
+    down = lax.ppermute(down, "orb", backward)
     arrived = []
-    source = tensor
     for begin, rows in CUTS:
-        if not arrived:
-            x, l = first_cut(
-                tensor, tensor_mask, occupied, virtual, occupied_mask, virtual_mask
-            )
-        else:
-            x, l = later_cut(source, tensor_mask, begin, rows)
-        source, x, l = lax.optimization_barrier((source, x, l))
+        x, l = cut(source, tensor_mask, begin, rows)
+        source, x, l, up, down = lax.optimization_barrier((source, x, l, up, down))
         arrived.append((lax.ppermute(x, "orb", forward), lax.ppermute(l, "orb", backward)))
 
     total, wide, thin = own_terms(
-        tensor, tensor_mask, occupied, virtual, occupied_mask, virtual_mask, *arrived[0]
+        tensor, tensor_mask, occupied, virtual, occupied_mask, virtual_mask, up, down
     )
+    wide, thin = hold(wide, thin)
     before = [total]
     for (begin, rows), (x, l) in zip(CUTS, arrived, strict=True):
         last = len(before) == len(CUTS)

time: 166 us -> 105 us (0.63)
  starting transfers between devices: 73.6 us -> 31.2 us
  Pallas kernels: 78.7 us -> 61.2 us
    ppermute x6, starting transfers between devices: 57.3 us -> 14.8 us  [scattered_sum(): total = total + lax.ppermute(pick(flips), axis, pairs)]
    pallas_call x1, Pallas kernels: 46.4 us -> 34.2 us  [own_terms(): pl.pallas_call(functools.partial(own_kernel, times, w), grid=(aux // AUX_...]
    pallas_call x6, Pallas kernels: 32.2 us -> 26.9 us  [the longest x2 9.94 us: near_sum(): pl.pallas_call(functools.partial(near_kernel, begin, steps, len(before)),...]
    ppermute x0 -> x2, starting transfers between devices: none -> 3.65 us  [the longest x1 2.36 us: body(): up = lax.ppermute(up, 'orb', forward)]
    ppermute x3 -> x2, starting transfers between devices: 12.4 us -> 10.2 us  [body(): lax.ppermute(x, 'orb', forward)]
    ppermute x3 -> x2, starting transfers between devices: 3.85 us -> 2.57 us  [body(): lax.ppermute(l, 'orb', backward)]
    unnamed x6 -> x8, local copies, waits for them, and re-layouts: 2.26 us -> 3.39 us
  transfers between devices with their start and end apart: 12 -> 12, of which waited for: 4 -> 4; matrix products, arithmetic and copies ran while one was open for 0% -> 0% of each run, Pallas kernels for 40% -> 53%
where the time goes in v3:
time: 105 us
  Pallas kernels  61.2 us (58%)
  starting transfers between devices  31.2 us (30%)
  waiting for transfers between devices  8.39 us (8%)
  local copies, waits for them, and re-layouts  3.43 us (3%)
    pallas_call x1, Pallas kernels, own_terms(): pl.pallas_call(functools.partial(own_kernel, times, w), grid=(aux // AUX_...  34.2 us
    ppermute x6, starting transfers between devices, scattered_sum(): total = total + lax.ppermute(pick(flips), axis, pairs)  14.8 us
    ppermute x2, starting transfers between devices, body(): lax.ppermute(x, 'orb', forward)  10.2 us
    pallas_call x2, Pallas kernels, near_sum(): pl.pallas_call(functools.partial(near_kernel, begin, steps, len(before)),...  9.94 us
    pallas_call x2, Pallas kernels, cut(): pl.pallas_call(functools.partial(cut_kernel, w), grid=(aux // step, rows...  9.19 us
    ppermute x6, waiting for transfers between devices, scattered_sum(): total = total + lax.ppermute(pick(flips), axis, pairs)  8.37 us
    pallas_call x1, Pallas kernels, hold(): pl.pallas_call(functools.partial(hold_kernel, parts), in_specs=[ANY, ANY]...  5.93 us
    unnamed x8, local copies, waits for them, and re-layouts  3.39 us
  transfers between devices with their start and end apart: 12, of which 4 were waited for; matrix products, arithmetic and copies ran while one was open for 0% of the time, Pallas kernels for 53%

profile of v3, /device:TPU:0, one launch (start us, length us, event | category | flops | bytes accessed | tf_op | source)
XLA Modules:
  0.0 105.0 jit_solution(15171205471902063835)
XLA Ops:
  0.0 1.9 %edges.1 = (bf16[2,128,384]{2,1,0:T(8,128)(2,1)}, bf16[2,128,384]{2,1,0:T(8,128)(2,1)}) custom-call(bf16[2,128,384]{2,1,0:T(8,128)(2,1)} %occ_ref.3, bf16[2,128,384]{2,1,0:T(8,128)(2,1)} %vir_ref.3, s32[2,1,3]{2,1,0:T(1,128)} %occ_flag.3, s32[2,1,3]{2,1,0:T(1,128)} %vir_flag.3), custom_call_target="tpu_custom_call" | custom-call | tf_op jit(solution)/shard_map/edges/pallas_call | solution.py:58
  1.9 2.4 %collective-permute-start = (bf16[2,128,384]{2,1,0:T(8,128)(2,1)}, bf16[2,128,384]{2,1,0:T(8,128)(2,1)S(1)}, u32[]{:S(2)}, u32[]{:S(2)}) collective-permute-start(bf16[2,128,384]{2,1,0:T(8,128)(2,1)} %get-tuple-element.33), channel_id=1, source_target_pairs={{0,1},{1,2},{2,3},{3,4},{4,5},{5,6},{6,7},{7,8},{8,9},{9,10},{10,1... | collective-permute-start | bytes 589832 | tf_op jit(solution)/shard_map/ppermute | solution.py:458
  4.2 1.3 %collective-permute-start.1 = (bf16[2,128,384]{2,1,0:T(8,128)(2,1)}, bf16[2,128,384]{2,1,0:T(8,128)(2,1)S(1)}, u32[]{:S(2)}, u32[]{:S(2)}) collective-permute-start(bf16[2,128,384]{2,1,0:T(8,128)(2,1)} %get-tuple-element.34), channel_id=1, source_target_pairs={{1,0},{2,1},{3,2},{4,3},{5,4},{6,5},{7,6},{8,7},{9,8},{10,9},{11,1... | collective-permute-start | bytes 589832 | tf_op jit(solution)/shard_map/ppermute | solution.py:459
  5.5 5.0 %cut.2 = (bf16[64,80,256]{2,1,0:T(8,128)(2,1)}, bf16[64,80,128]{2,1,0:T(8,128)(2,1)}) custom-call(bf16[64,128,384]{2,1,0:T(8,128)(2,1)} %b_ref.3, s32[1,3]{1,0:T(1,128)} %flag_ref.5), custom_call_target="tpu_custom_call" | custom-call | tf_op jit(solution)/shard_map/cut/pallas_call | solution.py:84
  10.5 0.0 collective-permute-done.up_ref
  10.5 0.0 collective-permute-done.1.down_ref
  10.5 7.0 %collective-permute-start.4 = (bf16[64,80,256]{2,1,0:T(8,128)(2,1)}, bf16[64,80,256]{2,1,0:T(8,128)(2,1)}, u32[]{:S(2)}, u32[]{:S(2)}) collective-permute-start(bf16[64,80,256]{2,1,0:T(8,128)(2,1)} %get-tuple-element.49), channel_id=1, source_target_pairs={{0,1},{1,2},{2,3},{3,4},{4,5},{5,6},{6,7},{7,8},{8,9},{9,10},{10,1... | collective-permute-start | bytes 7864328 | tf_op jit(solution)/shard_map/ppermute | solution.py:464
  17.6 1.3 %collective-permute-start.5 = (bf16[64,80,128]{2,1,0:T(8,128)(2,1)}, bf16[64,80,128]{2,1,0:T(8,128)(2,1)}, u32[]{:S(2)}, u32[]{:S(2)}) collective-permute-start(bf16[64,80,128]{2,1,0:T(8,128)(2,1)} %get-tuple-element.50), channel_id=1, source_target_pairs={{1,0},{2,1},{3,2},{4,3},{5,4},{6,5},{7,6},{8,7},{9,8},{10,9},{11,1... | collective-permute-start | bytes 3932168 | tf_op jit(solution)/shard_map/ppermute | solution.py:464
  18.9 4.2 %cut.3 = (bf16[64,48,256]{2,1,0:T(8,128)(2,1)}, bf16[64,48,128]{2,1,0:T(8,128)(2,1)}) custom-call(bf16[64,128,384]{2,1,0:T(8,128)(2,1)} %b_ref.3, s32[1,3]{1,0:T(1,128)} %flag_ref.5), custom_call_target="tpu_custom_call" | custom-call | tf_op jit(solution)/shard_map/cut/pallas_call | solution.py:84
  23.1 3.1 %collective-permute-start.2 = (bf16[64,48,256]{2,1,0:T(8,128)(2,1)}, bf16[64,48,256]{2,1,0:T(8,128)(2,1)S(1)}, u32[]{:S(2)}, u32[]{:S(2)}) collective-permute-start(bf16[64,48,256]{2,1,0:T(8,128)(2,1)} %get-tuple-element.46), channel_id=1, source_target_pairs={{0,1},{1,2},{2,3},{3,4},{4,5},{5,6},{6,7},{7,8},{8,9},{9,10},{10,1... | collective-permute-start | bytes 4718600 | tf_op jit(solution)/shard_map/ppermute | solution.py:464
  26.3 1.3 %collective-permute-start.3 = (bf16[64,48,128]{2,1,0:T(8,128)(2,1)}, bf16[64,48,128]{2,1,0:T(8,128)(2,1)S(1)}, u32[]{:S(2)}, u32[]{:S(2)}) collective-permute-start(bf16[64,48,128]{2,1,0:T(8,128)(2,1)} %get-tuple-element.47), channel_id=1, source_target_pairs={{1,0},{2,1},{3,2},{4,3},{5,4},{6,5},{7,6},{8,7},{9,8},{10,9},{11,1... | collective-permute-start | bytes 2359304 | tf_op jit(solution)/shard_map/ppermute | solution.py:464
  27.6 34.2 %own_terms.1 = (f32[128,64]{1,0:T(8,128)}, bf16[4,64,32768]{2,1,0:T(8,128)(2,1)}, bf16[4,64,16384]{2,1,0:T(8,128)(2,1)}) custom-call(bf16[64,128,384]{2,1,0:T(8,128)(2,1)} %b_ref.3, s32[1,3]{1,0:T(1,128)} %flag_ref.5, bf16[2,128,384]{2,1,0:T(8,128)(2,1)} %occ_ref.3, bf16[2,128,384]{2,1,0:T(8,128)(2,1)} %vir_ref.3, s32[2,1,3]{2,1,0:T(1,128)} %occ_flag.3, ...), custom_call_target="tpu_custom_call" | custom-call | flops 246960624 | bytes 1000000 | tf_op jit(solution)/shard_map/own_terms/pallas_call | solution.py:271
  61.8 3.4 %copy-done = bf16[4,64,16384]{2,1,0:T(8,128)(2,1)S(1)} copy-done((bf16[4,64,16384]{2,1,0:T(8,128)(2,1)S(1)}, bf16[4,64,16384]{2,1,0:T(8,128)(2,1)}, u32[]{:S(2)}) %copy-start) | copy-done | bytes 8388632
  65.2 5.9 %hold.1 = (bf16[4,64,32768]{2,1,0:T(8,128)(2,1)S(1)}, bf16[4,64,16384]{2,1,0:T(8,128)(2,1)S(1)}) custom-call(bf16[4,64,32768]{2,1,0:T(8,128)(2,1)} %get-tuple-element.42.wide_hbm, bf16[4,64,16384]{2,1,0:T(8,128)(2,1)S(1)} %copy-done), custom_call_target="tpu_custom_call" | custom-call | tf_op jit(solution)/shard_map/hold/pallas_call | solution.py:326
  71.1 0.0 collective-permute-done.5.l_hbm
  71.1 0.0 collective-permute-done.4.x_hbm
  71.1 6.3 %near_sum.2.rest_1_ = f32[256,64]{1,0:T(8,128)S(1)} custom-call(bf16[4,64,32768]{2,1,0:T(8,128)(2,1)S(1)} %get-tuple-element.44.wide, bf16[4,64,16384]{2,1,0:T(8,128)(2,1)S(1)} %get-tuple-element.45.thin, bf16[64,80,256]{2,1,0:T(8,128)(2,1)} %collective-permute-done.4.x_hbm, bf16[64,80,128]{2,1,0:T(8,128)(2,1)} %collective-permute-done.5.l_hbm), custom_call_target="tpu_custom_call" | custom-call | flops 10066329600 | bytes 196608000 | tf_op jit(solution)/shard_map/near_sum/pallas_call | solution.py:398
  77.5 0.0 collective-permute-done.3.l_hbm
  77.5 0.0 collective-permute-done.2.x_hbm
  77.5 3.6 %near_sum.3 = f32[128,64]{1,0:T(8,128)S(1)} custom-call(bf16[4,64,32768]{2,1,0:T(8,128)(2,1)S(1)} %get-tuple-element.44.wide, bf16[4,64,16384]{2,1,0:T(8,128)(2,1)S(1)} %get-tuple-element.45.thin, bf16[64,48,256]{2,1,0:T(8,128)(2,1)S(1)} %collective-permute-done.2.x_hbm, bf16[64,48,128]{2,1,0:T(8,128)(2,1)S(1)} %collective-permute-done.3.l_hbm, ...), custom_call_target="tpu_custom_call" | custom-call | flops 6039797760 | bytes 117964800 | tf_op jit(solution)/shard_map/near_sum/pallas_call | solution.py:398
  81.2 6.1 %collective-permute-start.6 = (f32[2,2,8,64]{3,2,1,0:T(8,128)S(1)}, f32[2,2,8,64]{3,2,1,0:T(8,128)S(1)}, u32[]{:S(2)}, u32[]{:S(2)}) collective-permute-start(f32[2,2,8,64]{3,2,1,0:T(8,128)S(1)} %get-tuple-element.51), channel_id=1, source_target_pairs={{0,4},{1,5},{2,6},{3,7},{4,0},{5,1},{6,2},{7,3},{8,12},{9,13},{10,... | collective-permute-start | bytes 24584 | tf_op jit(solution)/shard_map/ppermute | solution.py:445
  87.2 2.6 %collective-permute-start.7 = (f32[2,2,8,64]{3,2,1,0:T(8,128)S(1)}, f32[2,2,8,64]{3,2,1,0:T(8,128)S(1)}, u32[]{:S(2)}, u32[]{:S(2)}) collective-permute-start(f32[2,2,8,64]{3,2,1,0:T(8,128)S(1)} %get-tuple-element.53), channel_id=1, source_target_pairs={{0,8},{1,9},{2,10},{3,11},{4,12},{5,13},{6,14},{7,15},{8,0},{9,1},... | collective-permute-start | bytes 24584 | tf_op jit(solution)/shard_map/ppermute | solution.py:445
  89.8 0.0 collective-permute-start.8
  89.8 0.0 collective-permute-done.6
  89.8 2.0 %collective-permute-done.7 = f32[2,2,8,64]{3,2,1,0:T(8,128)S(1)} collective-permute-done((f32[2,2,8,64]{3,2,1,0:T(8,128)S(1)}, f32[2,2,8,64]{3,2,1,0:T(8,128)S(1)}, u32[]{:S(2)}, u32[]{:S(2)}) %collective-permute-start.7) | collective-permute-done | bytes 8224 | tf_op jit(solution)/shard_map/ppermute | solution.py:445
  91.9 3.5 %collective-permute-done.8 = f32[2,2,8,64]{3,2,1,0:T(8,128)S(1)} collective-permute-done((f32[2,2,8,64]{3,2,1,0:T(8,128)S(1)}, f32[2,2,8,64]{3,2,1,0:T(8,128)S(1)}, u32[]{:S(2)}, u32[]{:S(2)}) %collective-permute-start.8) | collective-permute-done | bytes 8224 | tf_op jit(solution)/shard_map/ppermute | solution.py:445
  95.4 6.0 %collective-permute-start.10 = (f32[8,64]{1,0:T(8,128)S(1)}, f32[8,64]{1,0:T(8,128)S(1)}, u32[]{:S(2)}, u32[]{:S(2)}) collective-permute-start(f32[8,64]{1,0:T(8,128)S(1)} %get-tuple-element.56), channel_id=1, source_target_pairs={{0,2},{1,3},{2,0},{3,1},{4,6},{5,7},{6,4},{7,5},{8,10},{9,11},{10,... | collective-permute-start | bytes 6152 | tf_op jit(solution)/shard_map/ppermute | solution.py:445
  101.4 0.0 collective-permute-start.11
  101.4 0.2 collective-permute-start.9
  101.6 1.4 %collective-permute-done.10 = f32[8,64]{1,0:T(8,128)S(1)} collective-permute-done((f32[8,64]{1,0:T(8,128)S(1)}, f32[8,64]{1,0:T(8,128)S(1)}, u32[]{:S(2)}, u32[]{:S(2)}) %collective-permute-start.10) | collective-permute-done | bytes 2080 | tf_op jit(solution)/shard_map/ppermute | solution.py:445
  103.0 1.4 %collective-permute-done.11 = f32[8,64]{1,0:T(8,128)S(1)} collective-permute-done((f32[8,64]{1,0:T(8,128)S(1)}, f32[8,64]{1,0:T(8,128)S(1)}, u32[]{:S(2)}, u32[]{:S(2)}) %collective-permute-start.11) | collective-permute-done | bytes 2080 | tf_op jit(solution)/shard_map/ppermute | solution.py:445
  104.4 0.6 fusion.3
  (11 shorter events, 0.1 us)
Async XLA Ops:
  1.9 8.6 %collective-permute-start = (bf16[2,128,384]{2,1,0:T(8,128)(2,1)}, bf16[2,128,384]{2,1,0:T(8,128)(2,1)S(1)}, u32[]{:S(2)}, u32[]{:S(2)}) collective-permute-start(bf16[2,128,384]{2,1,0:T(8,128)(2,1)} %get-tuple-element.33), channel_id=1, source_target_pairs={{0,1},{1,2},{2,3},{3,4},{4,5},{5,6},{6,7},{7,8},{8,9},{9,10},{10,1... | collective-permute-start | bytes 589832 | tf_op jit(solution)/shard_map/ppermute | solution.py:458
  4.2 6.3 %collective-permute-start.1 = (bf16[2,128,384]{2,1,0:T(8,128)(2,1)}, bf16[2,128,384]{2,1,0:T(8,128)(2,1)S(1)}, u32[]{:S(2)}, u32[]{:S(2)}) collective-permute-start(bf16[2,128,384]{2,1,0:T(8,128)(2,1)} %get-tuple-element.34), channel_id=1, source_target_pairs={{1,0},{2,1},{3,2},{4,3},{5,4},{6,5},{7,6},{8,7},{9,8},{10,9},{11,1... | collective-permute-start | bytes 589832 | tf_op jit(solution)/shard_map/ppermute | solution.py:459
  10.5 12.6 %copy-start.2 = (bf16[2,128,384]{2,1,0:T(8,128)(2,1)}, bf16[2,128,384]{2,1,0:T(8,128)(2,1)S(1)}, u32[]{:S(2)}) copy-start(bf16[2,128,384]{2,1,0:T(8,128)(2,1)S(1)} %collective-permute-done.up_ref) | copy-start | bytes 589828
  10.5 12.6 %copy-start.3 = (bf16[2,128,384]{2,1,0:T(8,128)(2,1)}, bf16[2,128,384]{2,1,0:T(8,128)(2,1)S(1)}, u32[]{:S(2)}) copy-start(bf16[2,128,384]{2,1,0:T(8,128)(2,1)S(1)} %collective-permute-done.1.down_ref) | copy-start | bytes 589828
  10.5 60.6 %collective-permute-start.4 = (bf16[64,80,256]{2,1,0:T(8,128)(2,1)}, bf16[64,80,256]{2,1,0:T(8,128)(2,1)}, u32[]{:S(2)}, u32[]{:S(2)}) collective-permute-start(bf16[64,80,256]{2,1,0:T(8,128)(2,1)} %get-tuple-element.49), channel_id=1, source_target_pairs={{0,1},{1,2},{2,3},{3,4},{4,5},{5,6},{6,7},{7,8},{8,9},{9,10},{10,1... | collective-permute-start | bytes 7864328 | tf_op jit(solution)/shard_map/ppermute | solution.py:464
  17.6 53.5 %collective-permute-start.5 = (bf16[64,80,128]{2,1,0:T(8,128)(2,1)}, bf16[64,80,128]{2,1,0:T(8,128)(2,1)}, u32[]{:S(2)}, u32[]{:S(2)}) collective-permute-start(bf16[64,80,128]{2,1,0:T(8,128)(2,1)} %get-tuple-element.50), channel_id=1, source_target_pairs={{1,0},{2,1},{3,2},{4,3},{5,4},{6,5},{7,6},{8,7},{9,8},{10,9},{11,1... | collective-permute-start | bytes 3932168 | tf_op jit(solution)/shard_map/ppermute | solution.py:464
  23.1 54.4 %collective-permute-start.2 = (bf16[64,48,256]{2,1,0:T(8,128)(2,1)}, bf16[64,48,256]{2,1,0:T(8,128)(2,1)S(1)}, u32[]{:S(2)}, u32[]{:S(2)}) collective-permute-start(bf16[64,48,256]{2,1,0:T(8,128)(2,1)} %get-tuple-element.46), channel_id=1, source_target_pairs={{0,1},{1,2},{2,3},{3,4},{4,5},{5,6},{6,7},{7,8},{8,9},{9,10},{10,1... | collective-permute-start | bytes 4718600 | tf_op jit(solution)/shard_map/ppermute | solution.py:464
  26.3 51.2 %collective-permute-start.3 = (bf16[64,48,128]{2,1,0:T(8,128)(2,1)}, bf16[64,48,128]{2,1,0:T(8,128)(2,1)S(1)}, u32[]{:S(2)}, u32[]{:S(2)}) collective-permute-start(bf16[64,48,128]{2,1,0:T(8,128)(2,1)} %get-tuple-element.47), channel_id=1, source_target_pairs={{1,0},{2,1},{3,2},{4,3},{5,4},{6,5},{7,6},{8,7},{9,8},{10,9},{11,1... | collective-permute-start | bytes 2359304 | tf_op jit(solution)/shard_map/ppermute | solution.py:464
  61.8 3.4 %copy-start = (bf16[4,64,16384]{2,1,0:T(8,128)(2,1)S(1)}, bf16[4,64,16384]{2,1,0:T(8,128)(2,1)}, u32[]{:S(2)}) copy-start(bf16[4,64,16384]{2,1,0:T(8,128)(2,1)} %get-tuple-element.43.thin_hbm) | copy-start | bytes 25165828
  71.1 6.4 %copy-start.1 = (f32[128,64]{1,0:T(8,128)S(1)}, f32[128,64]{1,0:T(8,128)}, u32[]{:S(2)}) copy-start(f32[128,64]{1,0:T(8,128)} %get-tuple-element.48.rest_0_) | copy-start | bytes 98308
  81.2 8.7 %collective-permute-start.6 = (f32[2,2,8,64]{3,2,1,0:T(8,128)S(1)}, f32[2,2,8,64]{3,2,1,0:T(8,128)S(1)}, u32[]{:S(2)}, u32[]{:S(2)}) collective-permute-start(f32[2,2,8,64]{3,2,1,0:T(8,128)S(1)} %get-tuple-element.51), channel_id=1, source_target_pairs={{0,4},{1,5},{2,6},{3,7},{4,0},{5,1},{6,2},{7,3},{8,12},{9,13},{10,... | collective-permute-start | bytes 24584 | tf_op jit(solution)/shard_map/ppermute | solution.py:445
  87.2 4.6 %collective-permute-start.7 = (f32[2,2,8,64]{3,2,1,0:T(8,128)S(1)}, f32[2,2,8,64]{3,2,1,0:T(8,128)S(1)}, u32[]{:S(2)}, u32[]{:S(2)}) collective-permute-start(f32[2,2,8,64]{3,2,1,0:T(8,128)S(1)} %get-tuple-element.53), channel_id=1, source_target_pairs={{0,8},{1,9},{2,10},{3,11},{4,12},{5,13},{6,14},{7,15},{8,0},{9,1},... | collective-permute-start | bytes 24584 | tf_op jit(solution)/shard_map/ppermute | solution.py:445
  89.8 5.5 %collective-permute-start.8 = (f32[2,2,8,64]{3,2,1,0:T(8,128)S(1)}, f32[2,2,8,64]{3,2,1,0:T(8,128)S(1)}, u32[]{:S(2)}, u32[]{:S(2)}) collective-permute-start(f32[2,2,8,64]{3,2,1,0:T(8,128)S(1)} %get-tuple-element.52), channel_id=1, source_target_pairs={{0,12},{1,13},{2,14},{3,15},{4,8},{5,9},{6,10},{7,11},{8,4},{9,5},... | collective-permute-start | bytes 24584 | tf_op jit(solution)/shard_map/ppermute | solution.py:445
  95.4 7.6 %collective-permute-start.10 = (f32[8,64]{1,0:T(8,128)S(1)}, f32[8,64]{1,0:T(8,128)S(1)}, u32[]{:S(2)}, u32[]{:S(2)}) collective-permute-start(f32[8,64]{1,0:T(8,128)S(1)} %get-tuple-element.56), channel_id=1, source_target_pairs={{0,2},{1,3},{2,0},{3,1},{4,6},{5,7},{6,4},{7,5},{8,10},{9,11},{10,... | collective-permute-start | bytes 6152 | tf_op jit(solution)/shard_map/ppermute | solution.py:445
  101.4 3.0 %collective-permute-start.11 = (f32[8,64]{1,0:T(8,128)S(1)}, f32[8,64]{1,0:T(8,128)S(1)}, u32[]{:S(2)}, u32[]{:S(2)}) collective-permute-start(f32[8,64]{1,0:T(8,128)S(1)} %get-tuple-element.55), channel_id=1, source_target_pairs={{0,3},{1,2},{2,1},{3,0},{4,7},{5,6},{6,5},{7,4},{8,11},{9,10},{10,... | collective-permute-start | bytes 6152 | tf_op jit(solution)/shard_map/ppermute | solution.py:445
  101.4 3.0 %collective-permute-start.9 = (f32[8,64]{1,0:T(8,128)S(1)}, f32[8,64]{1,0:T(8,128)S(1)}, u32[]{:S(2)}, u32[]{:S(2)}) collective-permute-start(f32[8,64]{1,0:T(8,128)S(1)} %get-tuple-element.54), channel_id=1, source_target_pairs={{0,1},{1,0},{2,3},{3,2},{4,5},{5,4},{6,7},{7,6},{8,9},{9,8},{10,11... | collective-permute-start | bytes 6152 | tf_op jit(solution)/shard_map/ppermute | solution.py:445

commit v4 on v3

--- a/solution.py
+++ b/solution.py
@@ -41,28 +41,40 @@
     return kept(flag[t, 0, k], ref[t, :, k * width : (k + 1) * width])
 
 
-def edge_kernel(times, width, occ_ref, vir_ref, occ_flag, vir_flag, up_ref, down_ref):
+def edge_kernel(times, width, odd_ref, occ_ref, vir_ref, occ_flag, vir_flag, even_pair, odd_pair):
     w = width
-    for t in range(times):
-        up_ref[t, :, :w] = part(vir_ref, t, 1, w, vir_flag)
-        up_ref[t, :, w : 2 * w] = part(vir_ref, t, 2, w, vir_flag)
-        up_ref[t, :, 2 * w :] = part(occ_ref, t, 2, w, occ_flag)
-        down_ref[t, :, :w] = part(vir_ref, t, 0, w, vir_flag)
-        down_ref[t, :, w : 2 * w] = part(vir_ref, t, 1, w, vir_flag)
-        down_ref[t, :, 2 * w :] = part(occ_ref, t, 0, w, occ_flag)
-
-
-def edges(occ, vir, occ_flag, vir_flag):
+
+    def put(ref, blocks):
+        for t in range(times):
+            for n, (source, flag, k) in enumerate(blocks):
+                ref[t, :, n * w : (n + 1) * w] = part(source, t, k, w, flag)
+
+    vir, occ = (vir_ref, vir_flag), (occ_ref, occ_flag)
+    up = [(*vir, 1), (*vir, 2), (*occ, 2)]
+    down = [(*vir, 0), (*vir, 1), (*occ, 0)]
+
+    @pl.when(odd_ref[0] == 0)
+    def first_of_pair():
+        put(even_pair, up)
+        put(odd_pair, down)
+
+    @pl.when(odd_ref[0] != 0)
+    def second_of_pair():
+        put(even_pair, down)
+        put(odd_pair, up)
+
+
+def edges(odd, occ, vir, occ_flag, vir_flag):
     times, w, _ = occ.shape
     whole = pl.BlockSpec(occ.shape, lambda i: (0, 0, 0))
     return pl.pallas_call(
         functools.partial(edge_kernel, times, w),
         grid=(1,),
-        in_specs=[whole, whole, SMEM, SMEM],
+        in_specs=[SMEM, whole, whole, SMEM, SMEM],
         out_specs=[whole, whole],
         out_shape=[jax.ShapeDtypeStruct(occ.shape, occ.dtype)] * 2,
         name="edges",
-    )(occ, vir, occ_flag, vir_flag)
+    )(odd, occ, vir, occ_flag, vir_flag)
 
 
 def cut_kernel(width, b_ref, flag_ref, x_ref, l_ref):
@@ -96,7 +108,7 @@
 
 
 def own_kernel(
-    times, width, b_ref, flag_ref, occ_ref, vir_ref, occ_flag, vir_flag, up_ref, down_ref,
+    times, width, odd_ref, b_ref, flag_ref, occ_ref, vir_ref, occ_flag, vir_flag, even_pair, odd_pair,
     sum_ref, wide_ref, thin_ref,
     left_w, right_w, low_w, occ_w, masked, u, x, left, own_n, wide_n, thin_n, flat_own, flat_b,
 ):
@@ -108,11 +120,14 @@
         for t in range(times):
             v_low, v_own, v_high = (part(vir_ref, t, k, w, vir_flag) for k in range(3))
             o_low, o_own, o_high = (part(occ_ref, t, k, w, occ_flag) for k in range(3))
+            from_even = [even_pair[t, :, k * w : (k + 1) * w] for k in range(3)]
+            from_odd = [odd_pair[t, :, k * w : (k + 1) * w] for k in range(3)]
+            odd = odd_ref[0] != 0
             below_own, below_up, below_occ = (
-                up_ref[t, :, k * w : (k + 1) * w] for k in range(3)
+                jnp.where(odd, one, two) for one, two in zip(from_even, from_odd, strict=True)
             )
             above_down, above_own, above_occ = (
-                down_ref[t, :, k * w : (k + 1) * w] for k in range(3)
+                jnp.where(odd, two, one) for one, two in zip(from_even, from_odd, strict=True)
             )
 
             def cols(slot):
@@ -261,7 +276,7 @@
         sum_ref[...] = total
 
 
-def own_terms(tensor, flag, occ, vir, occ_flag, vir_flag, up, down):
+def own_terms(odd, tensor, flag, occ, vir, occ_flag, vir_flag, even_pair, odd_pair):
     aux, w, band = tensor.shape
     times = occ.shape[0]
     bf = jnp.bfloat16
@@ -272,6 +287,7 @@
         functools.partial(own_kernel, times, w),
         grid=(aux // AUX_STEP,),
         in_specs=[
+            SMEM,
             pl.BlockSpec((AUX_STEP, w, band), lambda i: (i, 0, 0)),
             SMEM, whole, whole, SMEM, SMEM, whole, whole,
         ],
@@ -303,7 +319,7 @@
         compiler_params=pltpu.CompilerParams(vmem_limit_bytes=VMEM_LIMIT),
         cost_estimate=pl.CostEstimate(flops=flops // 50, bytes_accessed=1_000_000, transcendentals=0),
         name="own_terms",
-    )(tensor, flag, occ, vir, occ_flag, vir_flag, up, down)
+    )(odd, tensor, flag, occ, vir, occ_flag, vir_flag, even_pair, odd_pair)
 
 
 def hold_kernel(parts, wide_hbm, thin_hbm, wide_ref, thin_ref, sems):
@@ -439,7 +455,7 @@
             return block.reshape((2,) * (len(left) - len(chosen)) + (share, value.shape[1]))
 
         total = pick(0)
-        for code in range(1, 1 << len(chosen)):
+        for code in reversed(range(1, 1 << len(chosen))):
             flips = sum(((code >> j) & 1) << bit for j, bit in enumerate(chosen))
             pairs = [(i, i ^ flips) for i in range(count)]
             total = total + lax.ppermute(pick(flips), axis, pairs)
@@ -453,18 +469,24 @@
     forward = [(i, i + 1) for i in range(count - 1)]
     backward = [(i + 1, i) for i in range(count - 1)]
 
-    up, down = edges(occupied, virtual, occupied_mask, virtual_mask)
-    source, up, down = lax.optimization_barrier((tensor, up, down))
-    up = lax.ppermute(up, "orb", forward)
-    down = lax.ppermute(down, "orb", backward)
+    odd = (lax.axis_index("orb") & 1).astype(jnp.int32).reshape(1)
+    even_pair, odd_pair = edges(odd, occupied, virtual, occupied_mask, virtual_mask)
+    source, even_pair, odd_pair = lax.optimization_barrier((tensor, even_pair, odd_pair))
+    swaps = [[], []]
+    for i, j in forward:
+        swaps[i % 2] += [(i, j), (j, i)]
+    odd_pair = lax.ppermute(odd_pair, "orb", swaps[1])
+    even_pair = lax.ppermute(even_pair, "orb", swaps[0])
     arrived = []
     for begin, rows in CUTS:
         x, l = cut(source, tensor_mask, begin, rows)
-        source, x, l, up, down = lax.optimization_barrier((source, x, l, up, down))
+        source, x, l, even_pair, odd_pair = lax.optimization_barrier(
+            (source, x, l, even_pair, odd_pair)
+        )
         arrived.append((lax.ppermute(x, "orb", forward), lax.ppermute(l, "orb", backward)))
 
     total, wide, thin = own_terms(
-        tensor, tensor_mask, occupied, virtual, occupied_mask, virtual_mask, up, down
+        odd, tensor, tensor_mask, occupied, virtual, occupied_mask, virtual_mask, even_pair, odd_pair
     )
     wide, thin = hold(wide, thin)
     before = [total]

time: 105 us -> 101 us (0.962)
  starting transfers between devices: 31.2 us -> 28.6 us
  waiting for transfers between devices: 8.39 us -> 6.84 us
    ppermute x2, starting transfers between devices: 3.65 us -> 1.11 us  [the longest x1 0.66 us: body(): odd_pair = lax.ppermute(odd_pair, 'orb', swaps[1])]
    ppermute x6, waiting for transfers between devices: 8.37 us -> 6.82 us  [scattered_sum(): total = total + lax.ppermute(pick(flips), axis, pairs)]
  transfers between devices with their start and end apart: 12 -> 12, of which waited for: 4 -> 4; matrix products, arithmetic and copies ran while one was open for 0% -> 0% of each run, Pallas kernels for 53% -> 55%
where the time goes in v4:
time: 101 us
  Pallas kernels  61.2 us (61%)
  starting transfers between devices  28.6 us (28%)
  waiting for transfers between devices  6.84 us (7%)
  local copies, waits for them, and re-layouts  3.43 us (3%)
    pallas_call x1, Pallas kernels, own_terms(): pl.pallas_call(functools.partial(own_kernel, times, w), grid=(aux // AUX_...  34.2 us
    ppermute x6, starting transfers between devices, scattered_sum(): total = total + lax.ppermute(pick(flips), axis, pairs)  14.1 us
    ppermute x2, starting transfers between devices, body(): lax.ppermute(x, 'orb', forward)  10.8 us
    pallas_call x2, Pallas kernels, near_sum(): pl.pallas_call(functools.partial(near_kernel, begin, steps, len(before)),...  9.94 us
    pallas_call x2, Pallas kernels, cut(): pl.pallas_call(functools.partial(cut_kernel, w), grid=(aux // step, rows...  9.19 us
    ppermute x6, waiting for transfers between devices, scattered_sum(): total = total + lax.ppermute(pick(flips), axis, pairs)  6.82 us
    pallas_call x1, Pallas kernels, hold(): pl.pallas_call(functools.partial(hold_kernel, parts), in_specs=[ANY, ANY]...  5.93 us
    unnamed x8, local copies, waits for them, and re-layouts  3.39 us
  transfers between devices with their start and end apart: 12, of which 4 were waited for; matrix products, arithmetic and copies ran while one was open for 0% of the time, Pallas kernels for 55%

profile of v4, /device:TPU:0, one launch (start us, length us, event | category | flops | bytes accessed | tf_op | source)
XLA Modules:
  0.0 100.9 jit_solution(4112451859662592576)
XLA Ops:
  0.0 1.9 %edges.1 = (bf16[2,128,384]{2,1,0:T(8,128)(2,1)}, bf16[2,128,384]{2,1,0:T(8,128)(2,1)}) custom-call(s32[1]{0:T(128)} %bitcast.odd_ref, bf16[2,128,384]{2,1,0:T(8,128)(2,1)} %occ_ref.3, bf16[2,128,384]{2,1,0:T(8,128)(2,1)} %vir_ref.3, s32[2,1,3]{2,1,0:T(1,128)} %occ_flag.3, s32[2,1,3]{2,1,0:T(1,128)} %vir_flag.3), custom_call_target="tpu_custom_call" | custom-call | tf_op jit(solution)/shard_map/edges/pallas_call | solution.py:70
  1.9 0.5 collective-permute-start
  2.4 0.7 collective-permute-start.1
  3.0 5.0 %cut.2 = (bf16[64,80,256]{2,1,0:T(8,128)(2,1)}, bf16[64,80,128]{2,1,0:T(8,128)(2,1)}) custom-call(bf16[64,128,384]{2,1,0:T(8,128)(2,1)} %b_ref.3, s32[1,3]{1,0:T(1,128)} %flag_ref.5), custom_call_target="tpu_custom_call" | custom-call | tf_op jit(solution)/shard_map/cut/pallas_call | solution.py:96
  8.0 0.0 collective-permute-done.even_pair
  8.0 0.0 collective-permute-done.1.odd_pair
  8.0 7.4 %collective-permute-start.4 = (bf16[64,80,256]{2,1,0:T(8,128)(2,1)}, bf16[64,80,256]{2,1,0:T(8,128)(2,1)}, u32[]{:S(2)}, u32[]{:S(2)}) collective-permute-start(bf16[64,80,256]{2,1,0:T(8,128)(2,1)} %get-tuple-element.49), channel_id=1, source_target_pairs={{0,1},{1,2},{2,3},{3,4},{4,5},{5,6},{6,7},{7,8},{8,9},{9,10},{10,1... | collective-permute-start | bytes 7864328 | tf_op jit(solution)/shard_map/ppermute | solution.py:486
  15.5 1.3 %collective-permute-start.5 = (bf16[64,80,128]{2,1,0:T(8,128)(2,1)}, bf16[64,80,128]{2,1,0:T(8,128)(2,1)}, u32[]{:S(2)}, u32[]{:S(2)}) collective-permute-start(bf16[64,80,128]{2,1,0:T(8,128)(2,1)} %get-tuple-element.50), channel_id=1, source_target_pairs={{1,0},{2,1},{3,2},{4,3},{5,4},{6,5},{7,6},{8,7},{9,8},{10,9},{11,1... | collective-permute-start | bytes 3932168 | tf_op jit(solution)/shard_map/ppermute | solution.py:486
  16.7 4.2 %cut.3 = (bf16[64,48,256]{2,1,0:T(8,128)(2,1)}, bf16[64,48,128]{2,1,0:T(8,128)(2,1)}) custom-call(bf16[64,128,384]{2,1,0:T(8,128)(2,1)} %b_ref.3, s32[1,3]{1,0:T(1,128)} %flag_ref.5), custom_call_target="tpu_custom_call" | custom-call | tf_op jit(solution)/shard_map/cut/pallas_call | solution.py:96
  21.0 3.4 %collective-permute-start.2 = (bf16[64,48,256]{2,1,0:T(8,128)(2,1)}, bf16[64,48,256]{2,1,0:T(8,128)(2,1)S(1)}, u32[]{:S(2)}, u32[]{:S(2)}) collective-permute-start(bf16[64,48,256]{2,1,0:T(8,128)(2,1)} %get-tuple-element.46), channel_id=1, source_target_pairs={{0,1},{1,2},{2,3},{3,4},{4,5},{5,6},{6,7},{7,8},{8,9},{9,10},{10,1... | collective-permute-start | bytes 4718600 | tf_op jit(solution)/shard_map/ppermute | solution.py:486
  24.4 1.3 %collective-permute-start.3 = (bf16[64,48,128]{2,1,0:T(8,128)(2,1)}, bf16[64,48,128]{2,1,0:T(8,128)(2,1)S(1)}, u32[]{:S(2)}, u32[]{:S(2)}) collective-permute-start(bf16[64,48,128]{2,1,0:T(8,128)(2,1)} %get-tuple-element.47), channel_id=1, source_target_pairs={{1,0},{2,1},{3,2},{4,3},{5,4},{6,5},{7,6},{8,7},{9,8},{10,9},{11,1... | collective-permute-start | bytes 2359304 | tf_op jit(solution)/shard_map/ppermute | solution.py:486
  25.7 34.2 %own_terms.1 = (f32[128,64]{1,0:T(8,128)}, bf16[4,64,32768]{2,1,0:T(8,128)(2,1)}, bf16[4,64,16384]{2,1,0:T(8,128)(2,1)}) custom-call(s32[1]{0:T(128)} %bitcast.odd_ref, bf16[64,128,384]{2,1,0:T(8,128)(2,1)} %b_ref.3, s32[1,3]{1,0:T(1,128)} %flag_ref.5, bf16[2,128,384]{2,1,0:T(8,128)(2,1)} %occ_ref.3, bf16[2,128,384]{2,1,0:T(8,128)(2,1)} %vir_ref.3, ...), custom_call_target="tpu_custom_call" | custom-call | flops 246960624 | bytes 1000000 | tf_op jit(solution)/shard_map/own_terms/pallas_call | solution.py:286
  59.9 3.4 %copy-done = bf16[4,64,16384]{2,1,0:T(8,128)(2,1)S(1)} copy-done((bf16[4,64,16384]{2,1,0:T(8,128)(2,1)S(1)}, bf16[4,64,16384]{2,1,0:T(8,128)(2,1)}, u32[]{:S(2)}) %copy-start) | copy-done | bytes 8388632
  63.3 5.9 %hold.1 = (bf16[4,64,32768]{2,1,0:T(8,128)(2,1)S(1)}, bf16[4,64,16384]{2,1,0:T(8,128)(2,1)S(1)}) custom-call(bf16[4,64,32768]{2,1,0:T(8,128)(2,1)} %get-tuple-element.42.wide_hbm, bf16[4,64,16384]{2,1,0:T(8,128)(2,1)S(1)} %copy-done), custom_call_target="tpu_custom_call" | custom-call | tf_op jit(solution)/shard_map/hold/pallas_call | solution.py:342
  69.2 0.0 collective-permute-done.5.l_hbm
  69.3 0.0 collective-permute-done.4.x_hbm
  69.3 6.3 %near_sum.2.rest_1_ = f32[256,64]{1,0:T(8,128)S(1)} custom-call(bf16[4,64,32768]{2,1,0:T(8,128)(2,1)S(1)} %get-tuple-element.44.wide, bf16[4,64,16384]{2,1,0:T(8,128)(2,1)S(1)} %get-tuple-element.45.thin, bf16[64,80,256]{2,1,0:T(8,128)(2,1)} %collective-permute-done.4.x_hbm, bf16[64,80,128]{2,1,0:T(8,128)(2,1)} %collective-permute-done.5.l_hbm), custom_call_target="tpu_custom_call" | custom-call | flops 10066329600 | bytes 196608000 | tf_op jit(solution)/shard_map/near_sum/pallas_call | solution.py:414
  75.6 0.0 collective-permute-done.3.l_hbm
  75.6 0.0 collective-permute-done.2.x_hbm
  75.6 3.6 %near_sum.3 = f32[128,64]{1,0:T(8,128)S(1)} custom-call(bf16[4,64,32768]{2,1,0:T(8,128)(2,1)S(1)} %get-tuple-element.44.wide, bf16[4,64,16384]{2,1,0:T(8,128)(2,1)S(1)} %get-tuple-element.45.thin, bf16[64,48,256]{2,1,0:T(8,128)(2,1)S(1)} %collective-permute-done.2.x_hbm, bf16[64,48,128]{2,1,0:T(8,128)(2,1)S(1)} %collective-permute-done.3.l_hbm, ...), custom_call_target="tpu_custom_call" | custom-call | flops 6039797760 | bytes 117964800 | tf_op jit(solution)/shard_map/near_sum/pallas_call | solution.py:414
  79.3 7.0 %collective-permute-start.6 = (f32[2,2,8,64]{3,2,1,0:T(8,128)S(1)}, f32[2,2,8,64]{3,2,1,0:T(8,128)S(1)}, u32[]{:S(2)}, u32[]{:S(2)}) collective-permute-start(f32[2,2,8,64]{3,2,1,0:T(8,128)S(1)} %get-tuple-element.51), channel_id=1, source_target_pairs={{0,12},{1,13},{2,14},{3,15},{4,8},{5,9},{6,10},{7,11},{8,4},{9,5},... | collective-permute-start | bytes 24584 | tf_op jit(solution)/shard_map/ppermute | solution.py:461
  86.3 0.0 collective-permute-start.7
  86.3 0.6 collective-permute-start.8
  86.9 1.1 %collective-permute-done.6 = f32[2,2,8,64]{3,2,1,0:T(8,128)S(1)} collective-permute-done((f32[2,2,8,64]{3,2,1,0:T(8,128)S(1)}, f32[2,2,8,64]{3,2,1,0:T(8,128)S(1)}, u32[]{:S(2)}, u32[]{:S(2)}) %collective-permute-start.6) | collective-permute-done | bytes 8224 | tf_op jit(solution)/shard_map/ppermute | solution.py:461
  88.0 2.9 %collective-permute-done.7 = f32[2,2,8,64]{3,2,1,0:T(8,128)S(1)} collective-permute-done((f32[2,2,8,64]{3,2,1,0:T(8,128)S(1)}, f32[2,2,8,64]{3,2,1,0:T(8,128)S(1)}, u32[]{:S(2)}, u32[]{:S(2)}) %collective-permute-start.7) | collective-permute-done | bytes 8224 | tf_op jit(solution)/shard_map/ppermute | solution.py:461
  90.9 0.0 collective-permute-done.8
  90.9 6.3 %collective-permute-start.10 = (f32[8,64]{1,0:T(8,128)S(1)}, f32[8,64]{1,0:T(8,128)S(1)}, u32[]{:S(2)}, u32[]{:S(2)}) collective-permute-start(f32[8,64]{1,0:T(8,128)S(1)} %get-tuple-element.56), channel_id=1, source_target_pairs={{0,2},{1,3},{2,0},{3,1},{4,6},{5,7},{6,4},{7,5},{8,10},{9,11},{10,... | collective-permute-start | bytes 6152 | tf_op jit(solution)/shard_map/ppermute | solution.py:461
  97.3 0.2 collective-permute-start.9
  97.5 1.4 %collective-permute-done.10 = f32[8,64]{1,0:T(8,128)S(1)} collective-permute-done((f32[8,64]{1,0:T(8,128)S(1)}, f32[8,64]{1,0:T(8,128)S(1)}, u32[]{:S(2)}, u32[]{:S(2)}) %collective-permute-start.10) | collective-permute-done | bytes 2080 | tf_op jit(solution)/shard_map/ppermute | solution.py:461
  98.8 0.0 collective-permute-done.11
  98.8 1.4 %collective-permute-done.9 = f32[8,64]{1,0:T(8,128)S(1)} collective-permute-done((f32[8,64]{1,0:T(8,128)S(1)}, f32[8,64]{1,0:T(8,128)S(1)}, u32[]{:S(2)}, u32[]{:S(2)}) %collective-permute-start.9) | collective-permute-done | bytes 2080 | tf_op jit(solution)/shard_map/ppermute | solution.py:461
  100.3 0.6 fusion.3
  (11 shorter events, 0.1 us)
Async XLA Ops:
  1.9 6.1 %collective-permute-start = (bf16[2,128,384]{2,1,0:T(8,128)(2,1)}, bf16[2,128,384]{2,1,0:T(8,128)(2,1)S(1)}, u32[]{:S(2)}, u32[]{:S(2)}) collective-permute-start(bf16[2,128,384]{2,1,0:T(8,128)(2,1)} %get-tuple-element.33), channel_id=1, source_target_pairs={{0,1},{1,0},{2,3},{3,2},{4,5},{5,4},{6,7},{7,6},{8,9},{9,8},{10,11... | collective-permute-start | bytes 589832 | tf_op jit(solution)/shard_map/ppermute | solution.py:479
  2.4 5.6 %collective-permute-start.1 = (bf16[2,128,384]{2,1,0:T(8,128)(2,1)}, bf16[2,128,384]{2,1,0:T(8,128)(2,1)S(1)}, u32[]{:S(2)}, u32[]{:S(2)}) collective-permute-start(bf16[2,128,384]{2,1,0:T(8,128)(2,1)} %get-tuple-element.34), channel_id=1, source_target_pairs={{1,2},{2,1},{3,4},{4,3},{5,6},{6,5},{7,8},{8,7},{9,10},{10,9},{11,... | collective-permute-start | bytes 589832 | tf_op jit(solution)/shard_map/ppermute | solution.py:478
  8.0 13.0 %copy-start.2 = (bf16[2,128,384]{2,1,0:T(8,128)(2,1)}, bf16[2,128,384]{2,1,0:T(8,128)(2,1)S(1)}, u32[]{:S(2)}) copy-start(bf16[2,128,384]{2,1,0:T(8,128)(2,1)S(1)} %collective-permute-done.even_pair) | copy-start | bytes 589828
  8.0 13.0 %copy-start.3 = (bf16[2,128,384]{2,1,0:T(8,128)(2,1)}, bf16[2,128,384]{2,1,0:T(8,128)(2,1)S(1)}, u32[]{:S(2)}) copy-start(bf16[2,128,384]{2,1,0:T(8,128)(2,1)S(1)} %collective-permute-done.1.odd_pair) | copy-start | bytes 589828
  8.0 61.3 %collective-permute-start.4 = (bf16[64,80,256]{2,1,0:T(8,128)(2,1)}, bf16[64,80,256]{2,1,0:T(8,128)(2,1)}, u32[]{:S(2)}, u32[]{:S(2)}) collective-permute-start(bf16[64,80,256]{2,1,0:T(8,128)(2,1)} %get-tuple-element.49), channel_id=1, source_target_pairs={{0,1},{1,2},{2,3},{3,4},{4,5},{5,6},{6,7},{7,8},{8,9},{9,10},{10,1... | collective-permute-start | bytes 7864328 | tf_op jit(solution)/shard_map/ppermute | solution.py:486
  15.5 53.8 %collective-permute-start.5 = (bf16[64,80,128]{2,1,0:T(8,128)(2,1)}, bf16[64,80,128]{2,1,0:T(8,128)(2,1)}, u32[]{:S(2)}, u32[]{:S(2)}) collective-permute-start(bf16[64,80,128]{2,1,0:T(8,128)(2,1)} %get-tuple-element.50), channel_id=1, source_target_pairs={{1,0},{2,1},{3,2},{4,3},{5,4},{6,5},{7,6},{8,7},{9,8},{10,9},{11,1... | collective-permute-start | bytes 3932168 | tf_op jit(solution)/shard_map/ppermute | solution.py:486
  21.0 54.6 %collective-permute-start.2 = (bf16[64,48,256]{2,1,0:T(8,128)(2,1)}, bf16[64,48,256]{2,1,0:T(8,128)(2,1)S(1)}, u32[]{:S(2)}, u32[]{:S(2)}) collective-permute-start(bf16[64,48,256]{2,1,0:T(8,128)(2,1)} %get-tuple-element.46), channel_id=1, source_target_pairs={{0,1},{1,2},{2,3},{3,4},{4,5},{5,6},{6,7},{7,8},{8,9},{9,10},{10,1... | collective-permute-start | bytes 4718600 | tf_op jit(solution)/shard_map/ppermute | solution.py:486
  24.4 51.2 %collective-permute-start.3 = (bf16[64,48,128]{2,1,0:T(8,128)(2,1)}, bf16[64,48,128]{2,1,0:T(8,128)(2,1)S(1)}, u32[]{:S(2)}, u32[]{:S(2)}) collective-permute-start(bf16[64,48,128]{2,1,0:T(8,128)(2,1)} %get-tuple-element.47), channel_id=1, source_target_pairs={{1,0},{2,1},{3,2},{4,3},{5,4},{6,5},{7,6},{8,7},{9,8},{10,9},{11,1... | collective-permute-start | bytes 2359304 | tf_op jit(solution)/shard_map/ppermute | solution.py:486
  59.9 3.4 %copy-start = (bf16[4,64,16384]{2,1,0:T(8,128)(2,1)S(1)}, bf16[4,64,16384]{2,1,0:T(8,128)(2,1)}, u32[]{:S(2)}) copy-start(bf16[4,64,16384]{2,1,0:T(8,128)(2,1)} %get-tuple-element.43.thin_hbm) | copy-start | bytes 25165828
  69.3 6.4 %copy-start.1 = (f32[128,64]{1,0:T(8,128)S(1)}, f32[128,64]{1,0:T(8,128)}, u32[]{:S(2)}) copy-start(f32[128,64]{1,0:T(8,128)} %get-tuple-element.48.rest_0_) | copy-start | bytes 98308
  79.3 8.7 %collective-permute-start.6 = (f32[2,2,8,64]{3,2,1,0:T(8,128)S(1)}, f32[2,2,8,64]{3,2,1,0:T(8,128)S(1)}, u32[]{:S(2)}, u32[]{:S(2)}) collective-permute-start(f32[2,2,8,64]{3,2,1,0:T(8,128)S(1)} %get-tuple-element.51), channel_id=1, source_target_pairs={{0,12},{1,13},{2,14},{3,15},{4,8},{5,9},{6,10},{7,11},{8,4},{9,5},... | collective-permute-start | bytes 24584 | tf_op jit(solution)/shard_map/ppermute | solution.py:461
  86.3 4.6 %collective-permute-start.7 = (f32[2,2,8,64]{3,2,1,0:T(8,128)S(1)}, f32[2,2,8,64]{3,2,1,0:T(8,128)S(1)}, u32[]{:S(2)}, u32[]{:S(2)}) collective-permute-start(f32[2,2,8,64]{3,2,1,0:T(8,128)S(1)} %get-tuple-element.53), channel_id=1, source_target_pairs={{0,8},{1,9},{2,10},{3,11},{4,12},{5,13},{6,14},{7,15},{8,0},{9,1},... | collective-permute-start | bytes 24584 | tf_op jit(solution)/shard_map/ppermute | solution.py:461
  86.3 4.6 %collective-permute-start.8 = (f32[2,2,8,64]{3,2,1,0:T(8,128)S(1)}, f32[2,2,8,64]{3,2,1,0:T(8,128)S(1)}, u32[]{:S(2)}, u32[]{:S(2)}) collective-permute-start(f32[2,2,8,64]{3,2,1,0:T(8,128)S(1)} %get-tuple-element.52), channel_id=1, source_target_pairs={{0,4},{1,5},{2,6},{3,7},{4,0},{5,1},{6,2},{7,3},{8,12},{9,13},{10,... | collective-permute-start | bytes 24584 | tf_op jit(solution)/shard_map/ppermute | solution.py:461
  90.9 7.9 %collective-permute-start.10 = (f32[8,64]{1,0:T(8,128)S(1)}, f32[8,64]{1,0:T(8,128)S(1)}, u32[]{:S(2)}, u32[]{:S(2)}) collective-permute-start(f32[8,64]{1,0:T(8,128)S(1)} %get-tuple-element.56), channel_id=1, source_target_pairs={{0,2},{1,3},{2,0},{3,1},{4,6},{5,7},{6,4},{7,5},{8,10},{9,11},{10,... | collective-permute-start | bytes 6152 | tf_op jit(solution)/shard_map/ppermute | solution.py:461
  97.3 1.6 %collective-permute-start.11 = (f32[8,64]{1,0:T(8,128)S(1)}, f32[8,64]{1,0:T(8,128)S(1)}, u32[]{:S(2)}, u32[]{:S(2)}) collective-permute-start(f32[8,64]{1,0:T(8,128)S(1)} %get-tuple-element.55), channel_id=1, source_target_pairs={{0,1},{1,0},{2,3},{3,2},{4,5},{5,4},{6,7},{7,6},{8,9},{9,8},{10,11... | collective-permute-start | bytes 6152 | tf_op jit(solution)/shard_map/ppermute | solution.py:461
  97.3 3.0 %collective-permute-start.9 = (f32[8,64]{1,0:T(8,128)S(1)}, f32[8,64]{1,0:T(8,128)S(1)}, u32[]{:S(2)}, u32[]{:S(2)}) collective-permute-start(f32[8,64]{1,0:T(8,128)S(1)} %get-tuple-element.54), channel_id=1, source_target_pairs={{0,3},{1,2},{2,1},{3,0},{4,7},{5,6},{6,5},{7,4},{8,11},{9,10},{10,... | collective-permute-start | bytes 6152 | tf_op jit(solution)/shard_map/ppermute | solution.py:461

commit v5 on v4

--- a/solution.py
+++ b/solution.py
@@ -1,5 +1,4 @@
 import functools
-import math
 
 import jax
 import jax.numpy as jnp
@@ -13,9 +12,11 @@
 GROUP = 8
 ROW_STEP = 16
 AHEAD = 2
+SHARES = 4
 VMEM_LIMIT = 60 * 1024 * 1024
 NEAR_LIMIT = 12 * 1024 * 1024
 ANY = pl.BlockSpec(memory_space=pl.ANY)
+HBM = pl.BlockSpec(memory_space=pltpu.HBM)
 SMEM = pl.BlockSpec(memory_space=pltpu.SMEM)
 
 
@@ -77,30 +78,43 @@
     )(odd, occ, vir, occ_flag, vir_flag)
 
 
-def cut_kernel(width, b_ref, flag_ref, x_ref, l_ref):
+def cut_kernel(blocks, begin, rows, width, b_hbm, flag_ref, out_hbm, zeros, sems):
     w = width
-    l_ref[...] = kept(flag_ref[0, 0], b_ref[:, :, :w])
-    x_ref[:, :, :w] = kept(flag_ref[0, 1], b_ref[:, :, w : 2 * w])
-    x_ref[:, :, w:] = kept(flag_ref[0, 2], b_ref[:, :, 2 * w :])
-
-
-def cut(tensor, flag, begin, rows):
-    aux, w, band = tensor.shape
-    size = math.gcd(begin, rows)
-    step = aux if size <= ROW_STEP else AUX_STEP
-    base = begin // size
-
-    def spec(lanes, first):
-        return pl.BlockSpec((step, size, lanes), lambda i, j: (i, first + j, 0))
-
+    group = out_hbm.shape[0] // SHARES
+    zeros[...] = jnp.zeros_like(zeros)
+
+    def copy(n, j, dropped):
+        aux = pl.ds(j * group, group)
+        source = b_hbm.at[aux, pl.ds(begin, rows), pl.ds(blocks[n] * w, w)]
+        target = out_hbm.at[aux, :, pl.ds(n * w, w)]
+        return pltpu.make_async_copy(zeros if dropped else source, target, sems.at[n, j])
+
+    for n, k in enumerate(blocks):
+        for j in range(SHARES):
+
+            @pl.when(flag_ref[0, k] != 0)
+            def keep(n=n, j=j):
+                copy(n, j, False).start()
+
+            @pl.when(flag_ref[0, k] == 0)
+            def drop(n=n, j=j):
+                copy(n, j, True).start()
+
+    for n in range(len(blocks)):
+        for j in range(SHARES):
+            copy(n, j, False).wait()
+
+
+def cut(tensor, flag, blocks, begin, rows):
+    aux, w, _ = tensor.shape
     return pl.pallas_call(
-        functools.partial(cut_kernel, w),
-        grid=(aux // step, rows // size),
-        in_specs=[spec(band, base), SMEM],
-        out_specs=[spec(2 * w, 0), spec(w, 0)],
-        out_shape=[
-            jax.ShapeDtypeStruct((aux, rows, 2 * w), tensor.dtype),
-            jax.ShapeDtypeStruct((aux, rows, w), tensor.dtype),
+        functools.partial(cut_kernel, blocks, begin, rows, w),
+        in_specs=[HBM, SMEM],
+        out_specs=HBM,
+        out_shape=jax.ShapeDtypeStruct((aux, rows, len(blocks) * w), tensor.dtype),
+        scratch_shapes=[
+            pltpu.VMEM((aux // SHARES, rows, w), tensor.dtype),
+            pltpu.SemaphoreType.DMA((len(blocks), SHARES)),
         ],
         compiler_params=pltpu.CompilerParams(vmem_limit_bytes=VMEM_LIMIT),
         name="cut",
@@ -354,10 +368,15 @@
     return pltpu.with_memory_space_constraint(value, pltpu.VMEM)
 
 
+def in_hbm(value):
+    return pltpu.with_memory_space_constraint(value, pltpu.HBM)
+
+
 def near_kernel(begin, steps, earlier, wide, thin, x_hbm, l_hbm, *rest):
     before, rest = rest[:earlier], rest[earlier:]
     out_ref, x, l, total, held, sems, held_sems = rest
     slots, aux, w = wide.shape[0], wide.shape[1], l.shape[3]
+    direct = earlier > 0
     times = slots // 2
 
     def copies(s):
@@ -373,23 +392,28 @@
         fetch.append(
             pltpu.make_async_copy(ref, held.at[n, pl.ds(0, size)], held_sems.at[n])
         )
-    for s in range(min(AHEAD, steps)):
+    for s in range(0 if direct else min(AHEAD, steps)):
         for copy in copies(s):
             copy.start()
     for copy in fetch:
         copy.start()
     total[...] = jnp.zeros_like(total)
     for s in range(steps):
-        if s + AHEAD < steps:
-            for copy in copies(s + AHEAD):
-                copy.start()
-        for copy in copies(s):
-            copy.wait()
+        if direct:
+            rows = slice(s * ROW_STEP, (s + 1) * ROW_STEP)
+            x_s, l_s = x_hbm[:, rows], l_hbm[:, rows]
+        else:
+            if s + AHEAD < steps:
+                for copy in copies(s + AHEAD):
+                    copy.start()
+            for copy in copies(s):
+                copy.wait()
+            x_s, l_s = x[s], l[s]
         far = begin + s * ROW_STEP
         wide_s = wide[:, :, far * 2 * w : (far + ROW_STEP) * 2 * w]
         thin_s = thin[:, :, far * w : (far + ROW_STEP) * w]
-        total[...] += dot_nt(wide_s.reshape(slots * aux, ROW_STEP * 2 * w), flat(x[s])) + dot_nt(
-            thin_s.reshape(slots * aux, ROW_STEP * w), flat(l[s])
+        total[...] += dot_nt(wide_s.reshape(slots * aux, ROW_STEP * 2 * w), flat(x_s)) + dot_nt(
+            thin_s.reshape(slots * aux, ROW_STEP * w), flat(l_s)
         )
     if not earlier:
         out_ref[...] = total[...]
@@ -413,7 +437,7 @@
     vmem = pl.BlockSpec(memory_space=pltpu.VMEM)
     return pl.pallas_call(
         functools.partial(near_kernel, begin, steps, len(before)),
-        in_specs=[vmem, vmem] + [ANY] * (2 + len(before)),
+        in_specs=[vmem, vmem] + [vmem if before else HBM] * 2 + [ANY] * len(before),
         out_specs=vmem,
         out_shape=jax.ShapeDtypeStruct(shape, jnp.float32),
         scratch_shapes=[
@@ -431,7 +455,7 @@
             transcendentals=0,
         ),
         name="near_sum",
-    )(in_vmem(wide), in_vmem(thin), x, l, *before)
+    )(in_vmem(wide), in_vmem(thin), *map(in_vmem if before else in_hbm, (x, l)), *before)
 
 
 def scattered_sum(value, axis):
@@ -479,9 +503,11 @@
     even_pair = lax.ppermute(even_pair, "orb", swaps[0])
     arrived = []
     for begin, rows in CUTS:
-        x, l = cut(source, tensor_mask, begin, rows)
-        source, x, l, even_pair, odd_pair = lax.optimization_barrier(
-            (source, x, l, even_pair, odd_pair)
+        x = cut(source, tensor_mask, (1, 2), begin, rows)
+        source, x = lax.optimization_barrier((source, x))
+        l = cut(source, tensor_mask, (0,), begin, rows)
+        source, x, l, odd_pair, even_pair = lax.optimization_barrier(
+            (source, x, l, odd_pair, even_pair)
         )
         arrived.append((lax.ppermute(x, "orb", forward), lax.ppermute(l, "orb", backward)))
 

time: 101 us -> 284 us (2.81)
  Pallas kernels: 61.2 us -> 186 us
  starting transfers between devices: 28.6 us -> 88.2 us
    pallas_call x2 -> x4, Pallas kernels: 9.19 us -> 134 us  [cut(): pl.pallas_call(functools.partial(cut_kernel, blocks, begin, rows, w), in_...]
    ppermute x2, starting transfers between devices: 10.8 us -> 70.4 us  [body(): lax.ppermute(x, 'orb', forward)]
    ppermute x6, starting transfers between devices: 14.1 us -> 10.2 us  [scattered_sum(): total = total + lax.ppermute(pick(flips), axis, pairs)]
    ppermute x1, starting transfers between devices: 0.45 us -> 4.38 us  [body(): even_pair = lax.ppermute(even_pair, 'orb', swaps[0])]
  transfers between devices with their start and end apart: 12 -> 12, of which waited for: 4 -> 3; matrix products, arithmetic and copies ran while one was open for 0% -> 0% of each run, Pallas kernels for 55% -> 64%
where the time goes in v5:
time: 284 us
  Pallas kernels  186 us (65%)
  starting transfers between devices  88.2 us (31%)
  waiting for transfers between devices  5.48 us (2%)
  local copies, waits for them, and re-layouts  3.43 us (1%)
    pallas_call x4, Pallas kernels, cut(): pl.pallas_call(functools.partial(cut_kernel, blocks, begin, rows, w), in_...  134 us
    ppermute x2, starting transfers between devices, body(): lax.ppermute(x, 'orb', forward)  70.4 us
    pallas_call x1, Pallas kernels, own_terms(): pl.pallas_call(functools.partial(own_kernel, times, w), grid=(aux // AUX_...  34.2 us
    ppermute x6, starting transfers between devices, scattered_sum(): total = total + lax.ppermute(pick(flips), axis, pairs)  10.2 us
    pallas_call x2, Pallas kernels, near_sum(): pl.pallas_call(functools.partial(near_kernel, begin, steps, len(before)),...  9.43 us
    pallas_call x1, Pallas kernels, hold(): pl.pallas_call(functools.partial(hold_kernel, parts), in_specs=[ANY, ANY]...  5.93 us
  transfers between devices with their start and end apart: 12, of which 3 were waited for; matrix products, arithmetic and copies ran while one was open for 0% of the time, Pallas kernels for 64%

profile of v5, /device:TPU:0, one launch (start us, length us, event | category | flops | bytes accessed | tf_op | source)
XLA Modules:
  0.0 283.7 jit_solution(9307734488994483283)
XLA Ops:
  0.0 1.9 edges.1
  1.9 0.7 collective-permute-start
  2.6 4.4 %collective-permute-start.1 = (bf16[2,128,384]{2,1,0:T(8,128)(2,1)}, bf16[2,128,384]{2,1,0:T(8,128)(2,1)S(1)}, u32[]{:S(2)}, u32[]{:S(2)}) collective-permute-start(bf16[2,128,384]{2,1,0:T(8,128)(2,1)} %get-tuple-element.34), channel_id=1, source_target_pairs={{0,1},{1,0},{2,3},{3,2},{4,5},{5,4},{6,7},{7,6},{8,9},{9,8},{10,11... | collective-permute-start | bytes 589832 | tf_op jit(solution)/shard_map/ppermute | solution.py:503
  7.0 81.3 %cut.4 = bf16[64,80,256]{2,1,0:T(8,128)(2,1)} custom-call(bf16[64,128,384]{2,1,0:T(8,128)(2,1)} %b_ref.1, s32[1,3]{1,0:T(1,128)} %flag_ref.9), custom_call_target="tpu_custom_call" | custom-call | tf_op jit(solution)/shard_map/cut/pallas_call | solution.py:110
  88.3 1.8 cut.5
  90.1 0.0 collective-permute-done.odd_pair
  90.1 43.3 %collective-permute-start.4 = (bf16[64,80,256]{2,1,0:T(8,128)(2,1)}, bf16[64,80,256]{2,1,0:T(8,128)(2,1)}, u32[]{:S(2)}, u32[]{:S(2)}) collective-permute-start(bf16[64,80,256]{2,1,0:T(8,128)(2,1)} %cut.4), channel_id=1, source_target_pairs={{0,1},{1,2},{2,3},{3,4},{4,5},{5,6},{6,7},{7,8},{8,9},{9,10},{10,1... | collective-permute-start | bytes 7864328 | tf_op jit(solution)/shard_map/ppermute | solution.py:512
  133.4 1.3 collective-permute-start.5
  134.7 49.5 %cut.6 = bf16[64,48,256]{2,1,0:T(8,128)(2,1)} custom-call(bf16[64,128,384]{2,1,0:T(8,128)(2,1)} %b_ref.1, s32[1,3]{1,0:T(1,128)} %flag_ref.9), custom_call_target="tpu_custom_call" | custom-call | tf_op jit(solution)/shard_map/cut/pallas_call | solution.py:110
  184.2 1.7 cut.7
  185.9 27.1 %collective-permute-start.2 = (bf16[64,48,256]{2,1,0:T(8,128)(2,1)}, bf16[64,48,256]{2,1,0:T(8,128)(2,1)S(1)}, u32[]{:S(2)}, u32[]{:S(2)}) collective-permute-start(bf16[64,48,256]{2,1,0:T(8,128)(2,1)} %cut.6), channel_id=1, source_target_pairs={{0,1},{1,2},{2,3},{3,4},{4,5},{5,6},{6,7},{7,8},{8,9},{9,10},{10,1... | collective-permute-start | bytes 4718600 | tf_op jit(solution)/shard_map/ppermute | solution.py:512
  213.0 1.3 collective-permute-start.3
  214.3 34.2 %own_terms.1 = (f32[128,64]{1,0:T(8,128)}, bf16[4,64,32768]{2,1,0:T(8,128)(2,1)}, bf16[4,64,16384]{2,1,0:T(8,128)(2,1)}) custom-call(s32[1]{0:T(128)} %bitcast.odd_ref, bf16[64,128,384]{2,1,0:T(8,128)(2,1)} %b_ref.1, s32[1,3]{1,0:T(1,128)} %flag_ref.9, bf16[2,128,384]{2,1,0:T(8,128)(2,1)} %occ_ref.3, bf16[2,128,384]{2,1,0:T(8,128)(2,1)} %vir_ref.3, ...), custom_call_target="tpu_custom_call" | custom-call | flops 246960624 | bytes 1000000 | tf_op jit(solution)/shard_map/own_terms/pallas_call | solution.py:300
  248.6 3.4 %copy-done = bf16[4,64,16384]{2,1,0:T(8,128)(2,1)S(1)} copy-done((bf16[4,64,16384]{2,1,0:T(8,128)(2,1)S(1)}, bf16[4,64,16384]{2,1,0:T(8,128)(2,1)}, u32[]{:S(2)}) %copy-start) | copy-done | bytes 8388632
  251.9 5.9 %hold.1 = (bf16[4,64,32768]{2,1,0:T(8,128)(2,1)S(1)}, bf16[4,64,16384]{2,1,0:T(8,128)(2,1)S(1)}) custom-call(bf16[4,64,32768]{2,1,0:T(8,128)(2,1)} %get-tuple-element.42.wide_hbm, bf16[4,64,16384]{2,1,0:T(8,128)(2,1)S(1)} %copy-done), custom_call_target="tpu_custom_call" | custom-call | tf_op jit(solution)/shard_map/hold/pallas_call | solution.py:356
  257.9 0.0 collective-permute-done.5.l_hbm
  257.9 0.0 collective-permute-done.4.x_hbm
  257.9 6.3 %near_sum.2.rest_1_ = f32[256,64]{1,0:T(8,128)S(1)} custom-call(bf16[4,64,32768]{2,1,0:T(8,128)(2,1)S(1)} %get-tuple-element.44.wide, bf16[4,64,16384]{2,1,0:T(8,128)(2,1)S(1)} %get-tuple-element.45.thin, bf16[64,80,256]{2,1,0:T(8,128)(2,1)} %collective-permute-done.4.x_hbm, bf16[64,80,128]{2,1,0:T(8,128)(2,1)} %collective-permute-done.5.l_hbm), custom_call_target="tpu_custom_call" | custom-call | flops 10066329600 | bytes 196608000 | tf_op jit(solution)/shard_map/near_sum/pallas_call | solution.py:438
  264.2 0.0 collective-permute-done.3.l_hbm
  264.2 0.0 collective-permute-done.2.x_hbm
  264.3 3.1 %near_sum.3 = f32[128,64]{1,0:T(8,128)S(1)} custom-call(bf16[4,64,32768]{2,1,0:T(8,128)(2,1)S(1)} %get-tuple-element.44.wide, bf16[4,64,16384]{2,1,0:T(8,128)(2,1)S(1)} %get-tuple-element.45.thin, bf16[64,48,256]{2,1,0:T(8,128)(2,1)S(1)} %collective-permute-done.2.x_hbm, bf16[64,48,128]{2,1,0:T(8,128)(2,1)S(1)} %collective-permute-done.3.l_hbm, ...), custom_call_target="tpu_custom_call" | custom-call | flops 6039797760 | bytes 117964800 | tf_op jit(solution)/shard_map/near_sum/pallas_call | solution.py:438
  267.4 7.3 %collective-permute-start.6 = (f32[2,2,8,64]{3,2,1,0:T(8,128)S(1)}, f32[2,2,8,64]{3,2,1,0:T(8,128)S(1)}, u32[]{:S(2)}, u32[]{:S(2)}) collective-permute-start(f32[2,2,8,64]{3,2,1,0:T(8,128)S(1)} %get-tuple-element.51), channel_id=1, source_target_pairs={{0,12},{1,13},{2,14},{3,15},{4,8},{5,9},{6,10},{7,11},{8,4},{9,5},... | collective-permute-start | bytes 24584 | tf_op jit(solution)/shard_map/ppermute | solution.py:485
  274.8 0.0 collective-permute-start.7
  274.8 0.6 collective-permute-start.8
  275.4 1.1 collective-permute-done.6
  276.5 2.9 %collective-permute-done.7 = f32[2,2,8,64]{3,2,1,0:T(8,128)S(1)} collective-permute-done((f32[2,2,8,64]{3,2,1,0:T(8,128)S(1)}, f32[2,2,8,64]{3,2,1,0:T(8,128)S(1)}, u32[]{:S(2)}, u32[]{:S(2)}) %collective-permute-start.7) | collective-permute-done | bytes 8224 | tf_op jit(solution)/shard_map/ppermute | solution.py:485
  279.4 0.0 collective-permute-done.8
  279.4 0.1 collective-permute-start.10
  279.5 0.1 collective-permute-start.11
  279.6 2.0 collective-permute-start.9
  281.7 1.5 collective-permute-done.10
  283.1 0.6 fusion.3
  (13 shorter events, 0.1 us)
Async XLA Ops:
  1.9 88.2 %collective-permute-start = (bf16[2,128,384]{2,1,0:T(8,128)(2,1)}, bf16[2,128,384]{2,1,0:T(8,128)(2,1)S(1)}, u32[]{:S(2)}, u32[]{:S(2)}) collective-permute-start(bf16[2,128,384]{2,1,0:T(8,128)(2,1)} %get-tuple-element.33), channel_id=1, source_target_pairs={{1,2},{2,1},{3,4},{4,3},{5,6},{6,5},{7,8},{8,7},{9,10},{10,9},{11,... | collective-permute-start | bytes 589832 | tf_op jit(solution)/shard_map/ppermute | solution.py:502
  2.6 87.5 %collective-permute-start.1 = (bf16[2,128,384]{2,1,0:T(8,128)(2,1)}, bf16[2,128,384]{2,1,0:T(8,128)(2,1)S(1)}, u32[]{:S(2)}, u32[]{:S(2)}) collective-permute-start(bf16[2,128,384]{2,1,0:T(8,128)(2,1)} %get-tuple-element.34), channel_id=1, source_target_pairs={{0,1},{1,0},{2,3},{3,2},{4,5},{5,4},{6,7},{7,6},{8,9},{9,8},{10,11... | collective-permute-start | bytes 589832 | tf_op jit(solution)/shard_map/ppermute | solution.py:503
  90.1 94.1 %copy-start.2 = (bf16[2,128,384]{2,1,0:T(8,128)(2,1)}, bf16[2,128,384]{2,1,0:T(8,128)(2,1)S(1)}, u32[]{:S(2)}) copy-start(bf16[2,128,384]{2,1,0:T(8,128)(2,1)S(1)} %collective-permute-done.odd_pair) | copy-start | bytes 589828
  90.1 94.1 %copy-start.3 = (bf16[2,128,384]{2,1,0:T(8,128)(2,1)}, bf16[2,128,384]{2,1,0:T(8,128)(2,1)S(1)}, u32[]{:S(2)}) copy-start(bf16[2,128,384]{2,1,0:T(8,128)(2,1)S(1)} %collective-permute-done.1.even_pair) | copy-start | bytes 589828
  90.1 167.8 %collective-permute-start.4 = (bf16[64,80,256]{2,1,0:T(8,128)(2,1)}, bf16[64,80,256]{2,1,0:T(8,128)(2,1)}, u32[]{:S(2)}, u32[]{:S(2)}) collective-permute-start(bf16[64,80,256]{2,1,0:T(8,128)(2,1)} %cut.4), channel_id=1, source_target_pairs={{0,1},{1,2},{2,3},{3,4},{4,5},{5,6},{6,7},{7,8},{8,9},{9,10},{10,1... | collective-permute-start | bytes 7864328 | tf_op jit(solution)/shard_map/ppermute | solution.py:512
  133.4 124.5 %collective-permute-start.5 = (bf16[64,80,128]{2,1,0:T(8,128)(2,1)}, bf16[64,80,128]{2,1,0:T(8,128)(2,1)}, u32[]{:S(2)}, u32[]{:S(2)}) collective-permute-start(bf16[64,80,128]{2,1,0:T(8,128)(2,1)} %cut.5), channel_id=1, source_target_pairs={{1,0},{2,1},{3,2},{4,3},{5,4},{6,5},{7,6},{8,7},{9,8},{10,9},{11,1... | collective-permute-start | bytes 3932168 | tf_op jit(solution)/shard_map/ppermute | solution.py:512
  185.9 78.4 %collective-permute-start.2 = (bf16[64,48,256]{2,1,0:T(8,128)(2,1)}, bf16[64,48,256]{2,1,0:T(8,128)(2,1)S(1)}, u32[]{:S(2)}, u32[]{:S(2)}) collective-permute-start(bf16[64,48,256]{2,1,0:T(8,128)(2,1)} %cut.6), channel_id=1, source_target_pairs={{0,1},{1,2},{2,3},{3,4},{4,5},{5,6},{6,7},{7,8},{8,9},{9,10},{10,1... | collective-permute-start | bytes 4718600 | tf_op jit(solution)/shard_map/ppermute | solution.py:512
  213.0 51.2 %collective-permute-start.3 = (bf16[64,48,128]{2,1,0:T(8,128)(2,1)}, bf16[64,48,128]{2,1,0:T(8,128)(2,1)S(1)}, u32[]{:S(2)}, u32[]{:S(2)}) collective-permute-start(bf16[64,48,128]{2,1,0:T(8,128)(2,1)} %cut.7), channel_id=1, source_target_pairs={{1,0},{2,1},{3,2},{4,3},{5,4},{6,5},{7,6},{8,7},{9,8},{10,9},{11,1... | collective-permute-start | bytes 2359304 | tf_op jit(solution)/shard_map/ppermute | solution.py:512
  248.6 3.4 %copy-start = (bf16[4,64,16384]{2,1,0:T(8,128)(2,1)S(1)}, bf16[4,64,16384]{2,1,0:T(8,128)(2,1)}, u32[]{:S(2)}) copy-start(bf16[4,64,16384]{2,1,0:T(8,128)(2,1)} %get-tuple-element.43.thin_hbm) | copy-start | bytes 25165828
  257.9 6.4 %copy-start.1 = (f32[128,64]{1,0:T(8,128)S(1)}, f32[128,64]{1,0:T(8,128)}, u32[]{:S(2)}) copy-start(f32[128,64]{1,0:T(8,128)} %get-tuple-element.48.rest_0_) | copy-start | bytes 98308
  267.4 9.1 %collective-permute-start.6 = (f32[2,2,8,64]{3,2,1,0:T(8,128)S(1)}, f32[2,2,8,64]{3,2,1,0:T(8,128)S(1)}, u32[]{:S(2)}, u32[]{:S(2)}) collective-permute-start(f32[2,2,8,64]{3,2,1,0:T(8,128)S(1)} %get-tuple-element.51), channel_id=1, source_target_pairs={{0,12},{1,13},{2,14},{3,15},{4,8},{5,9},{6,10},{7,11},{8,4},{9,5},... | collective-permute-start | bytes 24584 | tf_op jit(solution)/shard_map/ppermute | solution.py:485
  274.8 4.6 %collective-permute-start.7 = (f32[2,2,8,64]{3,2,1,0:T(8,128)S(1)}, f32[2,2,8,64]{3,2,1,0:T(8,128)S(1)}, u32[]{:S(2)}, u32[]{:S(2)}) collective-permute-start(f32[2,2,8,64]{3,2,1,0:T(8,128)S(1)} %get-tuple-element.53), channel_id=1, source_target_pairs={{0,8},{1,9},{2,10},{3,11},{4,12},{5,13},{6,14},{7,15},{8,0},{9,1},... | collective-permute-start | bytes 24584 | tf_op jit(solution)/shard_map/ppermute | solution.py:485
  274.8 4.6 %collective-permute-start.8 = (f32[2,2,8,64]{3,2,1,0:T(8,128)S(1)}, f32[2,2,8,64]{3,2,1,0:T(8,128)S(1)}, u32[]{:S(2)}, u32[]{:S(2)}) collective-permute-start(f32[2,2,8,64]{3,2,1,0:T(8,128)S(1)} %get-tuple-element.52), channel_id=1, source_target_pairs={{0,4},{1,5},{2,6},{3,7},{4,0},{5,1},{6,2},{7,3},{8,12},{9,13},{10,... | collective-permute-start | bytes 24584 | tf_op jit(solution)/shard_map/ppermute | solution.py:485
  279.4 3.7 %collective-permute-start.10 = (f32[8,64]{1,0:T(8,128)S(1)}, f32[8,64]{1,0:T(8,128)S(1)}, u32[]{:S(2)}, u32[]{:S(2)}) collective-permute-start(f32[8,64]{1,0:T(8,128)S(1)} %get-tuple-element.56), channel_id=1, source_target_pairs={{0,2},{1,3},{2,0},{3,1},{4,6},{5,7},{6,4},{7,5},{8,10},{9,11},{10,... | collective-permute-start | bytes 6152 | tf_op jit(solution)/shard_map/ppermute | solution.py:485
  279.5 3.6 %collective-permute-start.11 = (f32[8,64]{1,0:T(8,128)S(1)}, f32[8,64]{1,0:T(8,128)S(1)}, u32[]{:S(2)}, u32[]{:S(2)}) collective-permute-start(f32[8,64]{1,0:T(8,128)S(1)} %get-tuple-element.55), channel_id=1, source_target_pairs={{0,1},{1,0},{2,3},{3,2},{4,5},{5,4},{6,7},{7,6},{8,9},{9,8},{10,11... | collective-permute-start | bytes 6152 | tf_op jit(solution)/shard_map/ppermute | solution.py:485
  279.6 3.5 %collective-permute-start.9 = (f32[8,64]{1,0:T(8,128)S(1)}, f32[8,64]{1,0:T(8,128)S(1)}, u32[]{:S(2)}, u32[]{:S(2)}) collective-permute-start(f32[8,64]{1,0:T(8,128)S(1)} %get-tuple-element.54), channel_id=1, source_target_pairs={{0,3},{1,2},{2,1},{3,0},{4,7},{5,6},{6,5},{7,4},{8,11},{9,10},{10,... | collective-permute-start | bytes 6152 | tf_op jit(solution)/shard_map/ppermute | solution.py:485

commit v6 on v4

--- a/solution.py
+++ b/solution.py
@@ -16,6 +16,7 @@
 VMEM_LIMIT = 60 * 1024 * 1024
 NEAR_LIMIT = 12 * 1024 * 1024
 ANY = pl.BlockSpec(memory_space=pl.ANY)
+HBM = pl.BlockSpec(memory_space=pltpu.HBM)
 SMEM = pl.BlockSpec(memory_space=pltpu.SMEM)
 
 
@@ -354,10 +355,15 @@
     return pltpu.with_memory_space_constraint(value, pltpu.VMEM)
 
 
+def in_hbm(value):
+    return pltpu.with_memory_space_constraint(value, pltpu.HBM)
+
+
 def near_kernel(begin, steps, earlier, wide, thin, x_hbm, l_hbm, *rest):
     before, rest = rest[:earlier], rest[earlier:]
     out_ref, x, l, total, held, sems, held_sems = rest
     slots, aux, w = wide.shape[0], wide.shape[1], l.shape[3]
+    direct = earlier > 0
     times = slots // 2
 
     def copies(s):
@@ -373,23 +379,28 @@
         fetch.append(
             pltpu.make_async_copy(ref, held.at[n, pl.ds(0, size)], held_sems.at[n])
         )
-    for s in range(min(AHEAD, steps)):
+    for s in range(0 if direct else min(AHEAD, steps)):
         for copy in copies(s):
             copy.start()
     for copy in fetch:
         copy.start()
     total[...] = jnp.zeros_like(total)
     for s in range(steps):
-        if s + AHEAD < steps:
-            for copy in copies(s + AHEAD):
-                copy.start()
-        for copy in copies(s):
-            copy.wait()
+        if direct:
+            rows = slice(s * ROW_STEP, (s + 1) * ROW_STEP)
+            x_s, l_s = x_hbm[:, rows], l_hbm[:, rows]
+        else:
+            if s + AHEAD < steps:
+                for copy in copies(s + AHEAD):
+                    copy.start()
+            for copy in copies(s):
+                copy.wait()
+            x_s, l_s = x[s], l[s]
         far = begin + s * ROW_STEP
         wide_s = wide[:, :, far * 2 * w : (far + ROW_STEP) * 2 * w]
         thin_s = thin[:, :, far * w : (far + ROW_STEP) * w]
-        total[...] += dot_nt(wide_s.reshape(slots * aux, ROW_STEP * 2 * w), flat(x[s])) + dot_nt(
-            thin_s.reshape(slots * aux, ROW_STEP * w), flat(l[s])
+        total[...] += dot_nt(wide_s.reshape(slots * aux, ROW_STEP * 2 * w), flat(x_s)) + dot_nt(
+            thin_s.reshape(slots * aux, ROW_STEP * w), flat(l_s)
         )
     if not earlier:
         out_ref[...] = total[...]
@@ -413,7 +424,7 @@
     vmem = pl.BlockSpec(memory_space=pltpu.VMEM)
     return pl.pallas_call(
         functools.partial(near_kernel, begin, steps, len(before)),
-        in_specs=[vmem, vmem] + [ANY] * (2 + len(before)),
+        in_specs=[vmem, vmem] + [vmem if before else HBM] * 2 + [ANY] * len(before),
         out_specs=vmem,
         out_shape=jax.ShapeDtypeStruct(shape, jnp.float32),
         scratch_shapes=[
@@ -431,7 +442,7 @@
             transcendentals=0,
         ),
         name="near_sum",
-    )(in_vmem(wide), in_vmem(thin), x, l, *before)
+    )(in_vmem(wide), in_vmem(thin), *map(in_vmem if before else in_hbm, (x, l)), *before)
 
 
 def scattered_sum(value, axis):
@@ -480,8 +491,8 @@
     arrived = []
     for begin, rows in CUTS:
         x, l = cut(source, tensor_mask, begin, rows)
-        source, x, l, even_pair, odd_pair = lax.optimization_barrier(
-            (source, x, l, even_pair, odd_pair)
+        source, x, l, odd_pair, even_pair = lax.optimization_barrier(
+            (source, x, l, odd_pair, even_pair)
         )
         arrived.append((lax.ppermute(x, "orb", forward), lax.ppermute(l, "orb", backward)))
 

time: 101 us -> 101 us (level)
    ppermute x1, starting transfers between devices: 0.45 us -> 4.38 us  [body(): even_pair = lax.ppermute(even_pair, 'orb', swaps[0])]
    ppermute x2, starting transfers between devices: 10.8 us -> 6.92 us  [body(): lax.ppermute(x, 'orb', forward)]
where the time goes in v6:
time: 101 us; the launch traced here: 100 us
  Pallas kernels  60.7 us (60%)
  starting transfers between devices  28.6 us (28%)
  waiting for transfers between devices  6.85 us (7%)
  local copies, waits for them, and re-layouts  3.43 us (3%)
    pallas_call x1, Pallas kernels, own_terms(): pl.pallas_call(functools.partial(own_kernel, times, w), grid=(aux // AUX_...  34.2 us
    ppermute x6, starting transfers between devices, scattered_sum(): total = total + lax.ppermute(pick(flips), axis, pairs)  14.1 us
    pallas_call x2, Pallas kernels, near_sum(): pl.pallas_call(functools.partial(near_kernel, begin, steps, len(before)),...  9.43 us
    pallas_call x2, Pallas kernels, cut(): pl.pallas_call(functools.partial(cut_kernel, w), grid=(aux // step, rows...  9.17 us
    ppermute x2, starting transfers between devices, body(): lax.ppermute(x, 'orb', forward)  6.92 us
    ppermute x6, waiting for transfers between devices, scattered_sum(): total = total + lax.ppermute(pick(flips), axis, pairs)  6.84 us
    pallas_call x1, Pallas kernels, hold(): pl.pallas_call(functools.partial(hold_kernel, parts), in_specs=[ANY, ANY]...  5.93 us
    ppermute x1, starting transfers between devices, body(): even_pair = lax.ppermute(even_pair, 'orb', swaps[0])  4.38 us
  transfers between devices with their start and end apart: 12, of which 4 were waited for; matrix products, arithmetic and copies ran while one was open for 0% of the time, Pallas kernels for 55%

profile of v6, /device:TPU:0, one launch (start us, length us, event | category | flops | bytes accessed | tf_op | source)
XLA Modules:
  0.0 100.4 jit_solution(7834043966011683836)
XLA Ops:
  0.0 1.9 %edges.1 = (bf16[2,128,384]{2,1,0:T(8,128)(2,1)}, bf16[2,128,384]{2,1,0:T(8,128)(2,1)}) custom-call(s32[1]{0:T(128)} %bitcast.odd_ref, bf16[2,128,384]{2,1,0:T(8,128)(2,1)} %occ_ref.3, bf16[2,128,384]{2,1,0:T(8,128)(2,1)} %vir_ref.3, s32[2,1,3]{2,1,0:T(1,128)} %occ_flag.3, s32[2,1,3]{2,1,0:T(1,128)} %vir_flag.3), custom_call_target="tpu_custom_call" | custom-call | tf_op jit(solution)/shard_map/edges/pallas_call | solution.py:71
  1.9 0.7 collective-permute-start
  2.6 4.4 %collective-permute-start.1 = (bf16[2,128,384]{2,1,0:T(8,128)(2,1)}, bf16[2,128,384]{2,1,0:T(8,128)(2,1)S(1)}, u32[]{:S(2)}, u32[]{:S(2)}) collective-permute-start(bf16[2,128,384]{2,1,0:T(8,128)(2,1)} %get-tuple-element.34), channel_id=1, source_target_pairs={{0,1},{1,0},{2,3},{3,2},{4,5},{5,4},{6,7},{7,6},{8,9},{9,8},{10,11... | collective-permute-start | bytes 589832 | tf_op jit(solution)/shard_map/ppermute | solution.py:490
  6.9 4.9 %cut.2 = (bf16[64,80,256]{2,1,0:T(8,128)(2,1)}, bf16[64,80,128]{2,1,0:T(8,128)(2,1)}) custom-call(bf16[64,128,384]{2,1,0:T(8,128)(2,1)} %b_ref.3, s32[1,3]{1,0:T(1,128)} %flag_ref.5), custom_call_target="tpu_custom_call" | custom-call | tf_op jit(solution)/shard_map/cut/pallas_call | solution.py:97
  11.9 0.0 collective-permute-done.odd_pair
  11.9 0.0 collective-permute-done.1.even_pair
  11.9 3.6 %collective-permute-start.4 = (bf16[64,80,256]{2,1,0:T(8,128)(2,1)}, bf16[64,80,256]{2,1,0:T(8,128)(2,1)}, u32[]{:S(2)}, u32[]{:S(2)}) collective-permute-start(bf16[64,80,256]{2,1,0:T(8,128)(2,1)} %get-tuple-element.49), channel_id=1, source_target_pairs={{0,1},{1,2},{2,3},{3,4},{4,5},{5,6},{6,7},{7,8},{8,9},{9,10},{10,1... | collective-permute-start | bytes 7864328 | tf_op jit(solution)/shard_map/ppermute | solution.py:497
  15.5 1.3 %collective-permute-start.5 = (bf16[64,80,128]{2,1,0:T(8,128)(2,1)}, bf16[64,80,128]{2,1,0:T(8,128)(2,1)}, u32[]{:S(2)}, u32[]{:S(2)}) collective-permute-start(bf16[64,80,128]{2,1,0:T(8,128)(2,1)} %get-tuple-element.50), channel_id=1, source_target_pairs={{1,0},{2,1},{3,2},{4,3},{5,4},{6,5},{7,6},{8,7},{9,8},{10,9},{11,1... | collective-permute-start | bytes 3932168 | tf_op jit(solution)/shard_map/ppermute | solution.py:497
  16.8 4.2 %cut.3 = (bf16[64,48,256]{2,1,0:T(8,128)(2,1)}, bf16[64,48,128]{2,1,0:T(8,128)(2,1)}) custom-call(bf16[64,128,384]{2,1,0:T(8,128)(2,1)} %b_ref.3, s32[1,3]{1,0:T(1,128)} %flag_ref.5), custom_call_target="tpu_custom_call" | custom-call | tf_op jit(solution)/shard_map/cut/pallas_call | solution.py:97
  21.0 3.4 %collective-permute-start.2 = (bf16[64,48,256]{2,1,0:T(8,128)(2,1)}, bf16[64,48,256]{2,1,0:T(8,128)(2,1)S(1)}, u32[]{:S(2)}, u32[]{:S(2)}) collective-permute-start(bf16[64,48,256]{2,1,0:T(8,128)(2,1)} %get-tuple-element.46), channel_id=1, source_target_pairs={{0,1},{1,2},{2,3},{3,4},{4,5},{5,6},{6,7},{7,8},{8,9},{9,10},{10,1... | collective-permute-start | bytes 4718600 | tf_op jit(solution)/shard_map/ppermute | solution.py:497
  24.4 1.3 %collective-permute-start.3 = (bf16[64,48,128]{2,1,0:T(8,128)(2,1)}, bf16[64,48,128]{2,1,0:T(8,128)(2,1)S(1)}, u32[]{:S(2)}, u32[]{:S(2)}) collective-permute-start(bf16[64,48,128]{2,1,0:T(8,128)(2,1)} %get-tuple-element.47), channel_id=1, source_target_pairs={{1,0},{2,1},{3,2},{4,3},{5,4},{6,5},{7,6},{8,7},{9,8},{10,9},{11,1... | collective-permute-start | bytes 2359304 | tf_op jit(solution)/shard_map/ppermute | solution.py:497
  25.7 34.2 %own_terms.1 = (f32[128,64]{1,0:T(8,128)}, bf16[4,64,32768]{2,1,0:T(8,128)(2,1)}, bf16[4,64,16384]{2,1,0:T(8,128)(2,1)}) custom-call(s32[1]{0:T(128)} %bitcast.odd_ref, bf16[64,128,384]{2,1,0:T(8,128)(2,1)} %b_ref.3, s32[1,3]{1,0:T(1,128)} %flag_ref.5, bf16[2,128,384]{2,1,0:T(8,128)(2,1)} %occ_ref.3, bf16[2,128,384]{2,1,0:T(8,128)(2,1)} %vir_ref.3, ...), custom_call_target="tpu_custom_call" | custom-call | flops 246960624 | bytes 1000000 | tf_op jit(solution)/shard_map/own_terms/pallas_call | solution.py:287
  59.9 3.4 %copy-done = bf16[4,64,16384]{2,1,0:T(8,128)(2,1)S(1)} copy-done((bf16[4,64,16384]{2,1,0:T(8,128)(2,1)S(1)}, bf16[4,64,16384]{2,1,0:T(8,128)(2,1)}, u32[]{:S(2)}) %copy-start) | copy-done | bytes 8388632
  63.3 5.9 %hold.1 = (bf16[4,64,32768]{2,1,0:T(8,128)(2,1)S(1)}, bf16[4,64,16384]{2,1,0:T(8,128)(2,1)S(1)}) custom-call(bf16[4,64,32768]{2,1,0:T(8,128)(2,1)} %get-tuple-element.42.wide_hbm, bf16[4,64,16384]{2,1,0:T(8,128)(2,1)S(1)} %copy-done), custom_call_target="tpu_custom_call" | custom-call | tf_op jit(solution)/shard_map/hold/pallas_call | solution.py:343
  69.3 0.0 collective-permute-done.5.l_hbm
  69.3 0.0 collective-permute-done.4.x_hbm
  69.3 6.3 %near_sum.2.rest_1_ = f32[256,64]{1,0:T(8,128)S(1)} custom-call(bf16[4,64,32768]{2,1,0:T(8,128)(2,1)S(1)} %get-tuple-element.44.wide, bf16[4,64,16384]{2,1,0:T(8,128)(2,1)S(1)} %get-tuple-element.45.thin, bf16[64,80,256]{2,1,0:T(8,128)(2,1)} %collective-permute-done.4.x_hbm, bf16[64,80,128]{2,1,0:T(8,128)(2,1)} %collective-permute-done.5.l_hbm), custom_call_target="tpu_custom_call" | custom-call | flops 10066329600 | bytes 196608000 | tf_op jit(solution)/shard_map/near_sum/pallas_call | solution.py:425
  75.6 0.0 collective-permute-done.3.l_hbm
  75.6 0.0 collective-permute-done.2.x_hbm
  75.6 3.1 %near_sum.3 = f32[128,64]{1,0:T(8,128)S(1)} custom-call(bf16[4,64,32768]{2,1,0:T(8,128)(2,1)S(1)} %get-tuple-element.44.wide, bf16[4,64,16384]{2,1,0:T(8,128)(2,1)S(1)} %get-tuple-element.45.thin, bf16[64,48,256]{2,1,0:T(8,128)(2,1)S(1)} %collective-permute-done.2.x_hbm, bf16[64,48,128]{2,1,0:T(8,128)(2,1)S(1)} %collective-permute-done.3.l_hbm, ...), custom_call_target="tpu_custom_call" | custom-call | flops 6039797760 | bytes 117964800 | tf_op jit(solution)/shard_map/near_sum/pallas_call | solution.py:425
  78.8 7.1 %collective-permute-start.6 = (f32[2,2,8,64]{3,2,1,0:T(8,128)S(1)}, f32[2,2,8,64]{3,2,1,0:T(8,128)S(1)}, u32[]{:S(2)}, u32[]{:S(2)}) collective-permute-start(f32[2,2,8,64]{3,2,1,0:T(8,128)S(1)} %get-tuple-element.51), channel_id=1, source_target_pairs={{0,12},{1,13},{2,14},{3,15},{4,8},{5,9},{6,10},{7,11},{8,4},{9,5},... | collective-permute-start | bytes 24584 | tf_op jit(solution)/shard_map/ppermute | solution.py:472
  85.9 0.0 collective-permute-start.7
  85.9 0.6 collective-permute-start.8
  86.5 1.1 %collective-permute-done.6 = f32[2,2,8,64]{3,2,1,0:T(8,128)S(1)} collective-permute-done((f32[2,2,8,64]{3,2,1,0:T(8,128)S(1)}, f32[2,2,8,64]{3,2,1,0:T(8,128)S(1)}, u32[]{:S(2)}, u32[]{:S(2)}) %collective-permute-start.6) | collective-permute-done | bytes 8224 | tf_op jit(solution)/shard_map/ppermute | solution.py:472
  87.6 2.9 %collective-permute-done.7 = f32[2,2,8,64]{3,2,1,0:T(8,128)S(1)} collective-permute-done((f32[2,2,8,64]{3,2,1,0:T(8,128)S(1)}, f32[2,2,8,64]{3,2,1,0:T(8,128)S(1)}, u32[]{:S(2)}, u32[]{:S(2)}) %collective-permute-start.7) | collective-permute-done | bytes 8224 | tf_op jit(solution)/shard_map/ppermute | solution.py:472
  90.5 0.0 collective-permute-done.8
  90.6 6.2 %collective-permute-start.10 = (f32[8,64]{1,0:T(8,128)S(1)}, f32[8,64]{1,0:T(8,128)S(1)}, u32[]{:S(2)}, u32[]{:S(2)}) collective-permute-start(f32[8,64]{1,0:T(8,128)S(1)} %get-tuple-element.56), channel_id=1, source_target_pairs={{0,2},{1,3},{2,0},{3,1},{4,6},{5,7},{6,4},{7,5},{8,10},{9,11},{10,... | collective-permute-start | bytes 6152 | tf_op jit(solution)/shard_map/ppermute | solution.py:472
  96.7 0.2 collective-permute-start.9
  96.9 1.4 %collective-permute-done.10 = f32[8,64]{1,0:T(8,128)S(1)} collective-permute-done((f32[8,64]{1,0:T(8,128)S(1)}, f32[8,64]{1,0:T(8,128)S(1)}, u32[]{:S(2)}, u32[]{:S(2)}) %collective-permute-start.10) | collective-permute-done | bytes 2080 | tf_op jit(solution)/shard_map/ppermute | solution.py:472
  98.3 0.0 collective-permute-done.11
  98.3 1.4 %collective-permute-done.9 = f32[8,64]{1,0:T(8,128)S(1)} collective-permute-done((f32[8,64]{1,0:T(8,128)S(1)}, f32[8,64]{1,0:T(8,128)S(1)}, u32[]{:S(2)}, u32[]{:S(2)}) %collective-permute-start.9) | collective-permute-done | bytes 2080 | tf_op jit(solution)/shard_map/ppermute | solution.py:472
  99.8 0.6 fusion.3
  (11 shorter events, 0.1 us)
Async XLA Ops:
  1.9 10.0 %collective-permute-start = (bf16[2,128,384]{2,1,0:T(8,128)(2,1)}, bf16[2,128,384]{2,1,0:T(8,128)(2,1)S(1)}, u32[]{:S(2)}, u32[]{:S(2)}) collective-permute-start(bf16[2,128,384]{2,1,0:T(8,128)(2,1)} %get-tuple-element.33), channel_id=1, source_target_pairs={{1,2},{2,1},{3,4},{4,3},{5,6},{6,5},{7,8},{8,7},{9,10},{10,9},{11,... | collective-permute-start | bytes 589832 | tf_op jit(solution)/shard_map/ppermute | solution.py:489
  2.6 9.3 %collective-permute-start.1 = (bf16[2,128,384]{2,1,0:T(8,128)(2,1)}, bf16[2,128,384]{2,1,0:T(8,128)(2,1)S(1)}, u32[]{:S(2)}, u32[]{:S(2)}) collective-permute-start(bf16[2,128,384]{2,1,0:T(8,128)(2,1)} %get-tuple-element.34), channel_id=1, source_target_pairs={{0,1},{1,0},{2,3},{3,2},{4,5},{5,4},{6,7},{7,6},{8,9},{9,8},{10,11... | collective-permute-start | bytes 589832 | tf_op jit(solution)/shard_map/ppermute | solution.py:490
  11.9 9.1 %copy-start.2 = (bf16[2,128,384]{2,1,0:T(8,128)(2,1)}, bf16[2,128,384]{2,1,0:T(8,128)(2,1)S(1)}, u32[]{:S(2)}) copy-start(bf16[2,128,384]{2,1,0:T(8,128)(2,1)S(1)} %collective-permute-done.odd_pair) | copy-start | bytes 589828
  11.9 9.1 %copy-start.3 = (bf16[2,128,384]{2,1,0:T(8,128)(2,1)}, bf16[2,128,384]{2,1,0:T(8,128)(2,1)S(1)}, u32[]{:S(2)}) copy-start(bf16[2,128,384]{2,1,0:T(8,128)(2,1)S(1)} %collective-permute-done.1.even_pair) | copy-start | bytes 589828
  11.9 57.4 %collective-permute-start.4 = (bf16[64,80,256]{2,1,0:T(8,128)(2,1)}, bf16[64,80,256]{2,1,0:T(8,128)(2,1)}, u32[]{:S(2)}, u32[]{:S(2)}) collective-permute-start(bf16[64,80,256]{2,1,0:T(8,128)(2,1)} %get-tuple-element.49), channel_id=1, source_target_pairs={{0,1},{1,2},{2,3},{3,4},{4,5},{5,6},{6,7},{7,8},{8,9},{9,10},{10,1... | collective-permute-start | bytes 7864328 | tf_op jit(solution)/shard_map/ppermute | solution.py:497
  15.5 53.8 %collective-permute-start.5 = (bf16[64,80,128]{2,1,0:T(8,128)(2,1)}, bf16[64,80,128]{2,1,0:T(8,128)(2,1)}, u32[]{:S(2)}, u32[]{:S(2)}) collective-permute-start(bf16[64,80,128]{2,1,0:T(8,128)(2,1)} %get-tuple-element.50), channel_id=1, source_target_pairs={{1,0},{2,1},{3,2},{4,3},{5,4},{6,5},{7,6},{8,7},{9,8},{10,9},{11,1... | collective-permute-start | bytes 3932168 | tf_op jit(solution)/shard_map/ppermute | solution.py:497
  21.0 54.6 %collective-permute-start.2 = (bf16[64,48,256]{2,1,0:T(8,128)(2,1)}, bf16[64,48,256]{2,1,0:T(8,128)(2,1)S(1)}, u32[]{:S(2)}, u32[]{:S(2)}) collective-permute-start(bf16[64,48,256]{2,1,0:T(8,128)(2,1)} %get-tuple-element.46), channel_id=1, source_target_pairs={{0,1},{1,2},{2,3},{3,4},{4,5},{5,6},{6,7},{7,8},{8,9},{9,10},{10,1... | collective-permute-start | bytes 4718600 | tf_op jit(solution)/shard_map/ppermute | solution.py:497
  24.4 51.2 %collective-permute-start.3 = (bf16[64,48,128]{2,1,0:T(8,128)(2,1)}, bf16[64,48,128]{2,1,0:T(8,128)(2,1)S(1)}, u32[]{:S(2)}, u32[]{:S(2)}) collective-permute-start(bf16[64,48,128]{2,1,0:T(8,128)(2,1)} %get-tuple-element.47), channel_id=1, source_target_pairs={{1,0},{2,1},{3,2},{4,3},{5,4},{6,5},{7,6},{8,7},{9,8},{10,9},{11,1... | collective-permute-start | bytes 2359304 | tf_op jit(solution)/shard_map/ppermute | solution.py:497
  59.9 3.4 %copy-start = (bf16[4,64,16384]{2,1,0:T(8,128)(2,1)S(1)}, bf16[4,64,16384]{2,1,0:T(8,128)(2,1)}, u32[]{:S(2)}) copy-start(bf16[4,64,16384]{2,1,0:T(8,128)(2,1)} %get-tuple-element.43.thin_hbm) | copy-start | bytes 25165828
  69.3 6.4 %copy-start.1 = (f32[128,64]{1,0:T(8,128)S(1)}, f32[128,64]{1,0:T(8,128)}, u32[]{:S(2)}) copy-start(f32[128,64]{1,0:T(8,128)} %get-tuple-element.48.rest_0_) | copy-start | bytes 98308
  78.8 8.8 %collective-permute-start.6 = (f32[2,2,8,64]{3,2,1,0:T(8,128)S(1)}, f32[2,2,8,64]{3,2,1,0:T(8,128)S(1)}, u32[]{:S(2)}, u32[]{:S(2)}) collective-permute-start(f32[2,2,8,64]{3,2,1,0:T(8,128)S(1)} %get-tuple-element.51), channel_id=1, source_target_pairs={{0,12},{1,13},{2,14},{3,15},{4,8},{5,9},{6,10},{7,11},{8,4},{9,5},... | collective-permute-start | bytes 24584 | tf_op jit(solution)/shard_map/ppermute | solution.py:472
  85.9 4.6 %collective-permute-start.7 = (f32[2,2,8,64]{3,2,1,0:T(8,128)S(1)}, f32[2,2,8,64]{3,2,1,0:T(8,128)S(1)}, u32[]{:S(2)}, u32[]{:S(2)}) collective-permute-start(f32[2,2,8,64]{3,2,1,0:T(8,128)S(1)} %get-tuple-element.53), channel_id=1, source_target_pairs={{0,8},{1,9},{2,10},{3,11},{4,12},{5,13},{6,14},{7,15},{8,0},{9,1},... | collective-permute-start | bytes 24584 | tf_op jit(solution)/shard_map/ppermute | solution.py:472
  85.9 4.6 %collective-permute-start.8 = (f32[2,2,8,64]{3,2,1,0:T(8,128)S(1)}, f32[2,2,8,64]{3,2,1,0:T(8,128)S(1)}, u32[]{:S(2)}, u32[]{:S(2)}) collective-permute-start(f32[2,2,8,64]{3,2,1,0:T(8,128)S(1)} %get-tuple-element.52), channel_id=1, source_target_pairs={{0,4},{1,5},{2,6},{3,7},{4,0},{5,1},{6,2},{7,3},{8,12},{9,13},{10,... | collective-permute-start | bytes 24584 | tf_op jit(solution)/shard_map/ppermute | solution.py:472
  90.6 7.7 %collective-permute-start.10 = (f32[8,64]{1,0:T(8,128)S(1)}, f32[8,64]{1,0:T(8,128)S(1)}, u32[]{:S(2)}, u32[]{:S(2)}) collective-permute-start(f32[8,64]{1,0:T(8,128)S(1)} %get-tuple-element.56), channel_id=1, source_target_pairs={{0,2},{1,3},{2,0},{3,1},{4,6},{5,7},{6,4},{7,5},{8,10},{9,11},{10,... | collective-permute-start | bytes 6152 | tf_op jit(solution)/shard_map/ppermute | solution.py:472
  96.7 1.6 %collective-permute-start.11 = (f32[8,64]{1,0:T(8,128)S(1)}, f32[8,64]{1,0:T(8,128)S(1)}, u32[]{:S(2)}, u32[]{:S(2)}) collective-permute-start(f32[8,64]{1,0:T(8,128)S(1)} %get-tuple-element.55), channel_id=1, source_target_pairs={{0,1},{1,0},{2,3},{3,2},{4,5},{5,4},{6,7},{7,6},{8,9},{9,8},{10,11... | collective-permute-start | bytes 6152 | tf_op jit(solution)/shard_map/ppermute | solution.py:472
  96.7 3.0 %collective-permute-start.9 = (f32[8,64]{1,0:T(8,128)S(1)}, f32[8,64]{1,0:T(8,128)S(1)}, u32[]{:S(2)}, u32[]{:S(2)}) collective-permute-start(f32[8,64]{1,0:T(8,128)S(1)} %get-tuple-element.54), channel_id=1, source_target_pairs={{0,3},{1,2},{2,1},{3,0},{4,7},{5,6},{6,5},{7,4},{8,11},{9,10},{10,... | collective-permute-start | bytes 6152 | tf_op jit(solution)/shard_map/ppermute | solution.py:472

commit v7 on v6

--- a/solution.py
+++ b/solution.py
@@ -466,7 +466,10 @@
             return block.reshape((2,) * (len(left) - len(chosen)) + (share, value.shape[1]))
 
         total = pick(0)
-        for code in reversed(range(1, 1 << len(chosen))):
+        codes = list(reversed(range(1, 1 << len(chosen))))
+        if len(left) < bits:
+            codes = codes[-1:] + codes[:-1]
+        for code in codes:
             flips = sum(((code >> j) & 1) << bit for j, bit in enumerate(chosen))
             pairs = [(i, i ^ flips) for i in range(count)]
             total = total + lax.ppermute(pick(flips), axis, pairs)

time: 101 us -> 99.9 us (0.989)
  waiting for transfers between devices: 6.85 us -> 5.64 us
    ppermute x6, waiting for transfers between devices: 6.84 us -> 5.62 us  [scattered_sum(): total = total + lax.ppermute(pick(flips), axis, pairs)]
  transfers between devices with their start and end apart: 12 -> 12, of which waited for: 4 -> 3; matrix products, arithmetic and copies ran while one was open for 0% -> 0% of each run, Pallas kernels for 55% -> 56%
where the time goes in v7:
time: 99.9 us; the launch traced here: 99.1 us
  Pallas kernels  60.7 us (61%)
  starting transfers between devices  28.6 us (29%)
  waiting for transfers between devices  5.64 us (6%)
  local copies, waits for them, and re-layouts  3.43 us (3%)
    pallas_call x1, Pallas kernels, own_terms(): pl.pallas_call(functools.partial(own_kernel, times, w), grid=(aux // AUX_...  34.2 us
    ppermute x6, starting transfers between devices, scattered_sum(): total = total + lax.ppermute(pick(flips), axis, pairs)  14.1 us
    pallas_call x2, Pallas kernels, near_sum(): pl.pallas_call(functools.partial(near_kernel, begin, steps, len(before)),...  9.43 us
    pallas_call x2, Pallas kernels, cut(): pl.pallas_call(functools.partial(cut_kernel, w), grid=(aux // step, rows...  9.17 us
    ppermute x2, starting transfers between devices, body(): lax.ppermute(x, 'orb', forward)  6.92 us
    pallas_call x1, Pallas kernels, hold(): pl.pallas_call(functools.partial(hold_kernel, parts), in_specs=[ANY, ANY]...  5.93 us
    ppermute x6, waiting for transfers between devices, scattered_sum(): total = total + lax.ppermute(pick(flips), axis, pairs)  5.62 us
    ppermute x1, starting transfers between devices, body(): even_pair = lax.ppermute(even_pair, 'orb', swaps[0])  4.38 us
  transfers between devices with their start and end apart: 12, of which 3 were waited for; matrix products, arithmetic and copies ran while one was open for 0% of the time, Pallas kernels for 56%

profile of v7, /device:TPU:0, one launch (start us, length us, event | category | flops | bytes accessed | tf_op | source)
XLA Modules:
  0.0 99.1 jit_solution(7393903009737955902)
XLA Ops:
  0.0 1.9 %edges.1 = (bf16[2,128,384]{2,1,0:T(8,128)(2,1)}, bf16[2,128,384]{2,1,0:T(8,128)(2,1)}) custom-call(s32[1]{0:T(128)} %bitcast.odd_ref, bf16[2,128,384]{2,1,0:T(8,128)(2,1)} %occ_ref.3, bf16[2,128,384]{2,1,0:T(8,128)(2,1)} %vir_ref.3, s32[2,1,3]{2,1,0:T(1,128)} %occ_flag.3, s32[2,1,3]{2,1,0:T(1,128)} %vir_flag.3), custom_call_target="tpu_custom_call" | custom-call | tf_op jit(solution)/shard_map/edges/pallas_call | solution.py:71
  1.9 0.7 collective-permute-start
  2.6 4.4 %collective-permute-start.1 = (bf16[2,128,384]{2,1,0:T(8,128)(2,1)}, bf16[2,128,384]{2,1,0:T(8,128)(2,1)S(1)}, u32[]{:S(2)}, u32[]{:S(2)}) collective-permute-start(bf16[2,128,384]{2,1,0:T(8,128)(2,1)} %get-tuple-element.34), channel_id=1, source_target_pairs={{0,1},{1,0},{2,3},{3,2},{4,5},{5,4},{6,7},{7,6},{8,9},{9,8},{10,11... | collective-permute-start | bytes 589832 | tf_op jit(solution)/shard_map/ppermute | solution.py:493
  6.9 4.9 %cut.2 = (bf16[64,80,256]{2,1,0:T(8,128)(2,1)}, bf16[64,80,128]{2,1,0:T(8,128)(2,1)}) custom-call(bf16[64,128,384]{2,1,0:T(8,128)(2,1)} %b_ref.3, s32[1,3]{1,0:T(1,128)} %flag_ref.5), custom_call_target="tpu_custom_call" | custom-call | tf_op jit(solution)/shard_map/cut/pallas_call | solution.py:97
  11.9 0.0 collective-permute-done.odd_pair
  11.9 0.0 collective-permute-done.1.even_pair
  11.9 3.6 %collective-permute-start.4 = (bf16[64,80,256]{2,1,0:T(8,128)(2,1)}, bf16[64,80,256]{2,1,0:T(8,128)(2,1)}, u32[]{:S(2)}, u32[]{:S(2)}) collective-permute-start(bf16[64,80,256]{2,1,0:T(8,128)(2,1)} %get-tuple-element.49), channel_id=1, source_target_pairs={{0,1},{1,2},{2,3},{3,4},{4,5},{5,6},{6,7},{7,8},{8,9},{9,10},{10,1... | collective-permute-start | bytes 7864328 | tf_op jit(solution)/shard_map/ppermute | solution.py:500
  15.5 1.3 %collective-permute-start.5 = (bf16[64,80,128]{2,1,0:T(8,128)(2,1)}, bf16[64,80,128]{2,1,0:T(8,128)(2,1)}, u32[]{:S(2)}, u32[]{:S(2)}) collective-permute-start(bf16[64,80,128]{2,1,0:T(8,128)(2,1)} %get-tuple-element.50), channel_id=1, source_target_pairs={{1,0},{2,1},{3,2},{4,3},{5,4},{6,5},{7,6},{8,7},{9,8},{10,9},{11,1... | collective-permute-start | bytes 3932168 | tf_op jit(solution)/shard_map/ppermute | solution.py:500
  16.8 4.2 %cut.3 = (bf16[64,48,256]{2,1,0:T(8,128)(2,1)}, bf16[64,48,128]{2,1,0:T(8,128)(2,1)}) custom-call(bf16[64,128,384]{2,1,0:T(8,128)(2,1)} %b_ref.3, s32[1,3]{1,0:T(1,128)} %flag_ref.5), custom_call_target="tpu_custom_call" | custom-call | tf_op jit(solution)/shard_map/cut/pallas_call | solution.py:97
  21.0 3.4 %collective-permute-start.2 = (bf16[64,48,256]{2,1,0:T(8,128)(2,1)}, bf16[64,48,256]{2,1,0:T(8,128)(2,1)S(1)}, u32[]{:S(2)}, u32[]{:S(2)}) collective-permute-start(bf16[64,48,256]{2,1,0:T(8,128)(2,1)} %get-tuple-element.46), channel_id=1, source_target_pairs={{0,1},{1,2},{2,3},{3,4},{4,5},{5,6},{6,7},{7,8},{8,9},{9,10},{10,1... | collective-permute-start | bytes 4718600 | tf_op jit(solution)/shard_map/ppermute | solution.py:500
  24.4 1.3 %collective-permute-start.3 = (bf16[64,48,128]{2,1,0:T(8,128)(2,1)}, bf16[64,48,128]{2,1,0:T(8,128)(2,1)S(1)}, u32[]{:S(2)}, u32[]{:S(2)}) collective-permute-start(bf16[64,48,128]{2,1,0:T(8,128)(2,1)} %get-tuple-element.47), channel_id=1, source_target_pairs={{1,0},{2,1},{3,2},{4,3},{5,4},{6,5},{7,6},{8,7},{9,8},{10,9},{11,1... | collective-permute-start | bytes 2359304 | tf_op jit(solution)/shard_map/ppermute | solution.py:500
  25.7 34.2 %own_terms.1 = (f32[128,64]{1,0:T(8,128)}, bf16[4,64,32768]{2,1,0:T(8,128)(2,1)}, bf16[4,64,16384]{2,1,0:T(8,128)(2,1)}) custom-call(s32[1]{0:T(128)} %bitcast.odd_ref, bf16[64,128,384]{2,1,0:T(8,128)(2,1)} %b_ref.3, s32[1,3]{1,0:T(1,128)} %flag_ref.5, bf16[2,128,384]{2,1,0:T(8,128)(2,1)} %occ_ref.3, bf16[2,128,384]{2,1,0:T(8,128)(2,1)} %vir_ref.3, ...), custom_call_target="tpu_custom_call" | custom-call | flops 246960624 | bytes 1000000 | tf_op jit(solution)/shard_map/own_terms/pallas_call | solution.py:287
  59.9 3.4 %copy-done = bf16[4,64,16384]{2,1,0:T(8,128)(2,1)S(1)} copy-done((bf16[4,64,16384]{2,1,0:T(8,128)(2,1)S(1)}, bf16[4,64,16384]{2,1,0:T(8,128)(2,1)}, u32[]{:S(2)}) %copy-start) | copy-done | bytes 8388632
  63.3 5.9 %hold.1 = (bf16[4,64,32768]{2,1,0:T(8,128)(2,1)S(1)}, bf16[4,64,16384]{2,1,0:T(8,128)(2,1)S(1)}) custom-call(bf16[4,64,32768]{2,1,0:T(8,128)(2,1)} %get-tuple-element.42.wide_hbm, bf16[4,64,16384]{2,1,0:T(8,128)(2,1)S(1)} %copy-done), custom_call_target="tpu_custom_call" | custom-call | tf_op jit(solution)/shard_map/hold/pallas_call | solution.py:343
  69.3 0.0 collective-permute-done.5.l_hbm
  69.3 0.0 collective-permute-done.4.x_hbm
  69.3 6.3 %near_sum.2.rest_1_ = f32[256,64]{1,0:T(8,128)S(1)} custom-call(bf16[4,64,32768]{2,1,0:T(8,128)(2,1)S(1)} %get-tuple-element.44.wide, bf16[4,64,16384]{2,1,0:T(8,128)(2,1)S(1)} %get-tuple-element.45.thin, bf16[64,80,256]{2,1,0:T(8,128)(2,1)} %collective-permute-done.4.x_hbm, bf16[64,80,128]{2,1,0:T(8,128)(2,1)} %collective-permute-done.5.l_hbm), custom_call_target="tpu_custom_call" | custom-call | flops 10066329600 | bytes 196608000 | tf_op jit(solution)/shard_map/near_sum/pallas_call | solution.py:425
  75.6 0.0 collective-permute-done.3.l_hbm
  75.6 0.0 collective-permute-done.2.x_hbm
  75.6 3.1 %near_sum.3 = f32[128,64]{1,0:T(8,128)S(1)} custom-call(bf16[4,64,32768]{2,1,0:T(8,128)(2,1)S(1)} %get-tuple-element.44.wide, bf16[4,64,16384]{2,1,0:T(8,128)(2,1)S(1)} %get-tuple-element.45.thin, bf16[64,48,256]{2,1,0:T(8,128)(2,1)S(1)} %collective-permute-done.2.x_hbm, bf16[64,48,128]{2,1,0:T(8,128)(2,1)S(1)} %collective-permute-done.3.l_hbm, ...), custom_call_target="tpu_custom_call" | custom-call | flops 6039797760 | bytes 117964800 | tf_op jit(solution)/shard_map/near_sum/pallas_call | solution.py:425
  78.8 7.1 %collective-permute-start.6 = (f32[2,2,8,64]{3,2,1,0:T(8,128)S(1)}, f32[2,2,8,64]{3,2,1,0:T(8,128)S(1)}, u32[]{:S(2)}, u32[]{:S(2)}) collective-permute-start(f32[2,2,8,64]{3,2,1,0:T(8,128)S(1)} %get-tuple-element.51), channel_id=1, source_target_pairs={{0,12},{1,13},{2,14},{3,15},{4,8},{5,9},{6,10},{7,11},{8,4},{9,5},... | collective-permute-start | bytes 24584 | tf_op jit(solution)/shard_map/ppermute | solution.py:475
  85.9 0.0 collective-permute-start.7
  85.9 0.6 collective-permute-start.8
  86.5 1.1 %collective-permute-done.6 = f32[2,2,8,64]{3,2,1,0:T(8,128)S(1)} collective-permute-done((f32[2,2,8,64]{3,2,1,0:T(8,128)S(1)}, f32[2,2,8,64]{3,2,1,0:T(8,128)S(1)}, u32[]{:S(2)}, u32[]{:S(2)}) %collective-permute-start.6) | collective-permute-done | bytes 8224 | tf_op jit(solution)/shard_map/ppermute | solution.py:475
  87.6 2.9 %collective-permute-done.7 = f32[2,2,8,64]{3,2,1,0:T(8,128)S(1)} collective-permute-done((f32[2,2,8,64]{3,2,1,0:T(8,128)S(1)}, f32[2,2,8,64]{3,2,1,0:T(8,128)S(1)}, u32[]{:S(2)}, u32[]{:S(2)}) %collective-permute-start.7) | collective-permute-done | bytes 8224 | tf_op jit(solution)/shard_map/ppermute | solution.py:475
  90.6 0.1 collective-permute-start.10
  90.7 6.2 %collective-permute-start.11 = (f32[8,64]{1,0:T(8,128)S(1)}, f32[8,64]{1,0:T(8,128)S(1)}, u32[]{:S(2)}, u32[]{:S(2)}) collective-permute-start(f32[8,64]{1,0:T(8,128)S(1)} %get-tuple-element.55), channel_id=1, source_target_pairs={{0,2},{1,3},{2,0},{3,1},{4,6},{5,7},{6,4},{7,5},{8,10},{9,11},{10,... | collective-permute-start | bytes 6152 | tf_op jit(solution)/shard_map/ppermute | solution.py:475
  96.9 0.0 collective-permute-start.9
  96.9 0.0 collective-permute-done.10
  96.9 1.6 %collective-permute-done.11 = f32[8,64]{1,0:T(8,128)S(1)} collective-permute-done((f32[8,64]{1,0:T(8,128)S(1)}, f32[8,64]{1,0:T(8,128)S(1)}, u32[]{:S(2)}, u32[]{:S(2)}) %collective-permute-start.11) | collective-permute-done | bytes 2080 | tf_op jit(solution)/shard_map/ppermute | solution.py:475
  98.5 0.0 collective-permute-done.9
  98.5 0.6 fusion.3
  (11 shorter events, 0.1 us)
Async XLA Ops:
  1.9 10.0 %collective-permute-start = (bf16[2,128,384]{2,1,0:T(8,128)(2,1)}, bf16[2,128,384]{2,1,0:T(8,128)(2,1)S(1)}, u32[]{:S(2)}, u32[]{:S(2)}) collective-permute-start(bf16[2,128,384]{2,1,0:T(8,128)(2,1)} %get-tuple-element.33), channel_id=1, source_target_pairs={{1,2},{2,1},{3,4},{4,3},{5,6},{6,5},{7,8},{8,7},{9,10},{10,9},{11,... | collective-permute-start | bytes 589832 | tf_op jit(solution)/shard_map/ppermute | solution.py:492
  2.6 9.3 %collective-permute-start.1 = (bf16[2,128,384]{2,1,0:T(8,128)(2,1)}, bf16[2,128,384]{2,1,0:T(8,128)(2,1)S(1)}, u32[]{:S(2)}, u32[]{:S(2)}) collective-permute-start(bf16[2,128,384]{2,1,0:T(8,128)(2,1)} %get-tuple-element.34), channel_id=1, source_target_pairs={{0,1},{1,0},{2,3},{3,2},{4,5},{5,4},{6,7},{7,6},{8,9},{9,8},{10,11... | collective-permute-start | bytes 589832 | tf_op jit(solution)/shard_map/ppermute | solution.py:493
  11.9 9.1 %copy-start.2 = (bf16[2,128,384]{2,1,0:T(8,128)(2,1)}, bf16[2,128,384]{2,1,0:T(8,128)(2,1)S(1)}, u32[]{:S(2)}) copy-start(bf16[2,128,384]{2,1,0:T(8,128)(2,1)S(1)} %collective-permute-done.odd_pair) | copy-start | bytes 589828
  11.9 9.1 %copy-start.3 = (bf16[2,128,384]{2,1,0:T(8,128)(2,1)}, bf16[2,128,384]{2,1,0:T(8,128)(2,1)S(1)}, u32[]{:S(2)}) copy-start(bf16[2,128,384]{2,1,0:T(8,128)(2,1)S(1)} %collective-permute-done.1.even_pair) | copy-start | bytes 589828
  11.9 57.4 %collective-permute-start.4 = (bf16[64,80,256]{2,1,0:T(8,128)(2,1)}, bf16[64,80,256]{2,1,0:T(8,128)(2,1)}, u32[]{:S(2)}, u32[]{:S(2)}) collective-permute-start(bf16[64,80,256]{2,1,0:T(8,128)(2,1)} %get-tuple-element.49), channel_id=1, source_target_pairs={{0,1},{1,2},{2,3},{3,4},{4,5},{5,6},{6,7},{7,8},{8,9},{9,10},{10,1... | collective-permute-start | bytes 7864328 | tf_op jit(solution)/shard_map/ppermute | solution.py:500
  15.5 53.8 %collective-permute-start.5 = (bf16[64,80,128]{2,1,0:T(8,128)(2,1)}, bf16[64,80,128]{2,1,0:T(8,128)(2,1)}, u32[]{:S(2)}, u32[]{:S(2)}) collective-permute-start(bf16[64,80,128]{2,1,0:T(8,128)(2,1)} %get-tuple-element.50), channel_id=1, source_target_pairs={{1,0},{2,1},{3,2},{4,3},{5,4},{6,5},{7,6},{8,7},{9,8},{10,9},{11,1... | collective-permute-start | bytes 3932168 | tf_op jit(solution)/shard_map/ppermute | solution.py:500
  21.0 54.6 %collective-permute-start.2 = (bf16[64,48,256]{2,1,0:T(8,128)(2,1)}, bf16[64,48,256]{2,1,0:T(8,128)(2,1)S(1)}, u32[]{:S(2)}, u32[]{:S(2)}) collective-permute-start(bf16[64,48,256]{2,1,0:T(8,128)(2,1)} %get-tuple-element.46), channel_id=1, source_target_pairs={{0,1},{1,2},{2,3},{3,4},{4,5},{5,6},{6,7},{7,8},{8,9},{9,10},{10,1... | collective-permute-start | bytes 4718600 | tf_op jit(solution)/shard_map/ppermute | solution.py:500
  24.4 51.2 %collective-permute-start.3 = (bf16[64,48,128]{2,1,0:T(8,128)(2,1)}, bf16[64,48,128]{2,1,0:T(8,128)(2,1)S(1)}, u32[]{:S(2)}, u32[]{:S(2)}) collective-permute-start(bf16[64,48,128]{2,1,0:T(8,128)(2,1)} %get-tuple-element.47), channel_id=1, source_target_pairs={{1,0},{2,1},{3,2},{4,3},{5,4},{6,5},{7,6},{8,7},{9,8},{10,9},{11,1... | collective-permute-start | bytes 2359304 | tf_op jit(solution)/shard_map/ppermute | solution.py:500
  59.9 3.4 %copy-start = (bf16[4,64,16384]{2,1,0:T(8,128)(2,1)S(1)}, bf16[4,64,16384]{2,1,0:T(8,128)(2,1)}, u32[]{:S(2)}) copy-start(bf16[4,64,16384]{2,1,0:T(8,128)(2,1)} %get-tuple-element.43.thin_hbm) | copy-start | bytes 25165828
  69.3 6.4 %copy-start.1 = (f32[128,64]{1,0:T(8,128)S(1)}, f32[128,64]{1,0:T(8,128)}, u32[]{:S(2)}) copy-start(f32[128,64]{1,0:T(8,128)} %get-tuple-element.48.rest_0_) | copy-start | bytes 98308
  78.8 8.8 %collective-permute-start.6 = (f32[2,2,8,64]{3,2,1,0:T(8,128)S(1)}, f32[2,2,8,64]{3,2,1,0:T(8,128)S(1)}, u32[]{:S(2)}, u32[]{:S(2)}) collective-permute-start(f32[2,2,8,64]{3,2,1,0:T(8,128)S(1)} %get-tuple-element.51), channel_id=1, source_target_pairs={{0,12},{1,13},{2,14},{3,15},{4,8},{5,9},{6,10},{7,11},{8,4},{9,5},... | collective-permute-start | bytes 24584 | tf_op jit(solution)/shard_map/ppermute | solution.py:475
  85.9 4.6 %collective-permute-start.7 = (f32[2,2,8,64]{3,2,1,0:T(8,128)S(1)}, f32[2,2,8,64]{3,2,1,0:T(8,128)S(1)}, u32[]{:S(2)}, u32[]{:S(2)}) collective-permute-start(f32[2,2,8,64]{3,2,1,0:T(8,128)S(1)} %get-tuple-element.53), channel_id=1, source_target_pairs={{0,8},{1,9},{2,10},{3,11},{4,12},{5,13},{6,14},{7,15},{8,0},{9,1},... | collective-permute-start | bytes 24584 | tf_op jit(solution)/shard_map/ppermute | solution.py:475
  85.9 4.6 %collective-permute-start.8 = (f32[2,2,8,64]{3,2,1,0:T(8,128)S(1)}, f32[2,2,8,64]{3,2,1,0:T(8,128)S(1)}, u32[]{:S(2)}, u32[]{:S(2)}) collective-permute-start(f32[2,2,8,64]{3,2,1,0:T(8,128)S(1)} %get-tuple-element.52), channel_id=1, source_target_pairs={{0,4},{1,5},{2,6},{3,7},{4,0},{5,1},{6,2},{7,3},{8,12},{9,13},{10,... | collective-permute-start | bytes 24584 | tf_op jit(solution)/shard_map/ppermute | solution.py:475
  90.6 6.3 %collective-permute-start.10 = (f32[8,64]{1,0:T(8,128)S(1)}, f32[8,64]{1,0:T(8,128)S(1)}, u32[]{:S(2)}, u32[]{:S(2)}) collective-permute-start(f32[8,64]{1,0:T(8,128)S(1)} %get-tuple-element.56), channel_id=1, source_target_pairs={{0,3},{1,2},{2,1},{3,0},{4,7},{5,6},{6,5},{7,4},{8,11},{9,10},{10,... | collective-permute-start | bytes 6152 | tf_op jit(solution)/shard_map/ppermute | solution.py:475
  90.7 7.9 %collective-permute-start.11 = (f32[8,64]{1,0:T(8,128)S(1)}, f32[8,64]{1,0:T(8,128)S(1)}, u32[]{:S(2)}, u32[]{:S(2)}) collective-permute-start(f32[8,64]{1,0:T(8,128)S(1)} %get-tuple-element.55), channel_id=1, source_target_pairs={{0,2},{1,3},{2,0},{3,1},{4,6},{5,7},{6,4},{7,5},{8,10},{9,11},{10,... | collective-permute-start | bytes 6152 | tf_op jit(solution)/shard_map/ppermute | solution.py:475
  96.9 1.6 %collective-permute-start.9 = (f32[8,64]{1,0:T(8,128)S(1)}, f32[8,64]{1,0:T(8,128)S(1)}, u32[]{:S(2)}, u32[]{:S(2)}) collective-permute-start(f32[8,64]{1,0:T(8,128)S(1)} %get-tuple-element.54), channel_id=1, source_target_pairs={{0,1},{1,0},{2,3},{3,2},{4,5},{5,4},{6,7},{7,6},{8,9},{9,8},{10,11... | collective-permute-start | bytes 6152 | tf_op jit(solution)/shard_map/ppermute | solution.py:475
